TPU v7x, 768 devices: a whole 4x8x12 slice. The times are simulated.
768 devices in a mesh: gx: 24 (over z_lo, x), gy: 32 (over z_hi, y, core).
Axes of the slice: x: 4, y: 8, z: 12 (z_hi: 2, z_lo: 6; z = z_hi * 6 + z_lo), core: 2. Of those that a mesh axis runs over, the one named last changes fastest.
Arguments:
- positions: float32 [3, 6291456], P(None, ('gx', 'gy')), may hold values from -6 to 6
- velocities: float32 [3, 6291456], P(None, ('gx', 'gy')), may hold values from -4 to 4
- masses: float32 [6291456], P(('gx', 'gy')), may hold values from 0.005 to 0.05
- long_kick: float32 [3, 6291456], P(None, ('gx', 'gy')), may hold values from -3 to 3
- leaf_lists: int32 [8, 49152], P(None, ('gx', 'gy')), may hold values from 0 to 135, as said below
- ghost_ids: int32 [6144], P(('gx', 'gy')), may hold values from 0 to 63, as said below
- leaf_counts: int32 [768], P(('gx', 'gy')), may hold values from 1 to 64, as said below
Outputs:
- new_positions: float32 [3, 6291456], P(None, ('gx', 'gy'))
- new_velocities: float32 [3, 6291456], P(None, ('gx', 'gy'))
Inputs may be any that keep to these rules, and one draw needn't show every extreme that they name: leaf_counts of a domain is at least 1; the counts of domains (i, j) and (i, j + 16) for j below 16 sum to at most 80, and some pair reaches it with one count equal to 64. `leaf_lists`: every entry below 64 is below the count of its domain; entries from 64 on name pool ghost leaves. `ghost_ids`: each id is below the count of its domain; ids may repeat.
All inputs are finite; a program needn't handle non-finite values.
Results may differ from a plain program's by a relative error of at most 0.00011.
Values sent between devices are 32-bit elements; how exact they have to be, the bound alone decides.
No kernel may reach another device: no remote copies, remote signals or barrier semaphores. Data moves between devices by JAX's collectives and lax.ppermute only.
A program may use at most 32 MiB of HBM per device.

v0:
```python
import jax
import jax.numpy as jnp
from jax import lax
from jax.sharding import PartitionSpec as P

SUBCYCLES = 4
BAL = 40


soften_sq = 0.04
cutoff_sq = 9.0
time_step = 0.5


def with_halo(cells, sides, width):
    for axis, dim in sides:
        count = lax.axis_size(axis)
        head = lax.slice_in_dim(cells, 0, width, axis=dim)
        tail = lax.slice_in_dim(cells, cells.shape[dim] - width, cells.shape[dim], axis=dim)
        cells = jnp.concatenate(
            [
                lax.ppermute(tail, axis, [(i, (i + 1) % count) for i in range(count)]),
                cells,
                lax.ppermute(head, axis, [((i + 1) % count, i) for i in range(count)]),
            ],
            axis=dim,
        )
    return cells


def swapped(block, axis, distance):
    count = lax.axis_size(axis)
    route = []
    for low in range(count):
        high = low | 1 << distance
        if high != low and high < count:
            route += [(low, high), (high, low)]
    return lax.ppermute(block, axis, route)


def pair_accel(targets, sources):
    offsets = sources[:3, :, None, :] - targets[:, :, :, None]
    distance = jnp.sum(offsets * offsets, axis=0)
    tapers = jnp.square(jnp.maximum(1.0 - distance / cutoff_sq, 0.0))
    inverse = lax.rsqrt(distance + soften_sq)
    weight = sources[3][:, None, :] * tapers * inverse * inverse * inverse
    return jnp.sum(offsets * weight[None], axis=3)


def accumulate(targets, operands):

    def add_tile(index, summed):
        sources = lax.dynamic_index_in_dim(operands, index, 1, keepdims=False)
        return summed + pair_accel(targets, sources)

    return lax.fori_loop(0, operands.shape[1], add_tile, jnp.zeros(targets.shape, targets.dtype))


def body(positions, velocities, masses, long_kick, leaf_lists, ghost_ids, leaf_counts):
    leaves = leaf_lists.shape[1]
    leaf_size = positions.shape[1] // leaves
    spare_slots = leaves - BAL
    live_count = leaf_counts[0]
    places = positions.reshape(3, leaves, leaf_size)
    speeds = velocities.reshape(3, leaves, leaf_size)
    kicks = long_kick.reshape(3, leaves, leaf_size)
    mass_rows = masses.reshape(1, leaves, leaf_size)
    live = (jnp.arange(leaves) < live_count)[None, :, None]
    for subcycle in range(SUBCYCLES):
        own_rows = jnp.concatenate([places, mass_rows], axis=0)
        chosen = jnp.take(own_rows, ghost_ids, axis=1).reshape(4, 1, 1, -1)
        beside_all = with_halo(chosen, (("gx", 1), ("gy", 2)), 1)
        pool = jnp.concatenate([own_rows, beside_all.reshape(4, -1, leaf_size)], axis=1)
        operands = jnp.take(pool, leaf_lists, axis=1)
        top_bit = lax.axis_size("gy").bit_length() - 2
        payload = jnp.concatenate([operands[:, :, BAL:], own_rows[:, None, BAL:]], axis=1)
        arrived = swapped(payload, "gy", top_bit)
        slot_operands = jnp.concatenate([operands[:, :, :BAL], arrived[:, :-1]], axis=2)
        slot_targets = jnp.concatenate([places[:, :BAL], arrived[:3, -1]], axis=1)
        slots = jnp.arange(BAL)
        picked = jnp.where(
            slots < live_count, slots, jnp.minimum(BAL + slots - live_count, leaves - 1)
        )
        slot_accel = accumulate(
            jnp.take(slot_targets, picked, axis=1), jnp.take(slot_operands, picked, axis=2)
        )
        lent_slots = jnp.minimum(live_count + jnp.arange(spare_slots), BAL - 1)
        returned = jnp.take(slot_accel, lent_slots, axis=1)
        came_back = swapped(returned, "gy", top_bit)
        accel = jnp.concatenate([slot_accel, came_back], axis=1)
        speeds = jnp.where(live, speeds + time_step * (accel + kicks), speeds)
        places = jnp.where(live, places + time_step * speeds, places)
    return (places.reshape(3, -1), speeds.reshape(3, -1))


def solution(mesh):
    return jax.shard_map(
        body,
        mesh=mesh,
        in_specs=(
            P(None, ("gx", "gy")),
            P(None, ("gx", "gy")),
            P(("gx", "gy")),
            P(None, ("gx", "gy")),
            P(None, ("gx", "gy")),
            P(("gx", "gy")),
            P(("gx", "gy")),
        ),
        out_specs=(P(None, ("gx", "gy")), P(None, ("gx", "gy"))),
        check_vma=False,
    )
```

profile of v0, /device:TPU:0, one launch (start us, length us, event | category | flops | bytes accessed | tf_op | source)
XLA Modules:
  0.0 648.5 jit_solution(8576193461383889045)
XLA Ops:
  5.5 10.8 %collective-permute-start.1 = (f32[4,1,1,1024]{3,0,2,1:T(4,128)S(1)}, f32[4,1,1,1024]{3,0,2,1:T(4,128)S(1)}, u32[]{:S(2)}, u32[]{:S(2)}) collective-permute-start(f32[4,1,1,1024]{3,0,2,1:T(4,128)S(1)} %select_bitcast_fusion.19), channel_id=1, source_target_pairs={{32,0},{64,32},{96,64},{128,96},{160,128},{192,160},{224,192},{256... | collective-permute-start | bytes 49160 | tf_op jit(solution)/shard_map/ppermute | solution.py:24
  21.3 12.1 %collective-permute-start.3 = (f32[4,3,1,1024]{3,0,2,1:T(4,128)S(1)}, f32[4,3,1,1024]{3,0,2,1:T(4,128)S(1)}, u32[]{:S(2)}, u32[]{:S(2)}) collective-permute-start(f32[4,3,1,1024]{3,0,2,1:T(4,128)S(1)} %pad_maximum_fusion.24), channel_id=1, source_target_pairs={{1,0},{2,1},{3,2},{4,3},{5,4},{6,5},{7,6},{8,7},{9,8},{10,9},{11,1... | collective-permute-start | bytes 147464 | tf_op jit(solution)/shard_map/ppermute | solution.py:24
  45.4 19.4 %collective-permute-done.4 = f32[4,9,24,128]{3,0,2,1:T(4,128)S(1)} collective-permute-done((f32[4,9,24,128]{3,0,2,1:T(4,128)S(1)}, f32[4,9,24,128]{3,0,2,1:T(4,128)S(1)}, u32[]{:S(2)}, u32[]{:S(2)}) %collective-permute-start.4) | collective-permute-done | bytes 442400 | tf_op jit(solution)/shard_map/ppermute | solution.py:38
  67.3 81.2 %while.56 = (s32[]{:T(128)}, f32[3,40,128]{2,1,0:T(8,128)S(1)}, f32[4,8,40,128]{3,1,0,2:T(8,128)S(1)}, f32[3,40,128]{2,1,0:T(8,128)S(1)}, s32[]{:T(128)}, /*index=5*/s32[]{:T(128)}, s32[]{}) while((s32[]{:T(128)}, f32[3,40,128]{2,1,0:T(8,128)S(1)}, f32[4,8,40,128]{3,1,0,2:T(8,128)S(1)}, f32[3,40,128]{2,1,0:T(8,128)S(1)}, ...), condition=%wide.region_3.8_spmd.clone, body=%wide.region_0.7_spmd.clone.sunk | while | flops 17054724 | bytes 16527527 | solution.py:56
  149.2 8.9 %collective-permute-start.5 = (f32[3,24,128]{2,0,1:T(4,128)S(1)}, f32[3,24,128]{2,0,1:T(4,128)S(1)}, u32[]{:S(2)}, u32[]{:S(2)}) collective-permute-start(f32[3,24,128]{2,0,1:T(4,128)S(1)} %select_bitcast_fusion.15), channel_id=1, source_target_pairs={{0,16},{16,0},{1,17},{17,1},{2,18},{18,2},{3,19},{19,3},{4,20},{20... | collective-permute-start | bytes 110600 | tf_op jit(solution)/shard_map/ppermute | solution.py:38
  164.3 12.7 %collective-permute-start.7 = (f32[4,1,1,1024]{3,0,2,1:T(4,128)S(1)}, f32[4,1,1,1024]{3,0,2,1:T(4,128)S(1)}, u32[]{:S(2)}, u32[]{:S(2)}) collective-permute-start(f32[4,1,1,1024]{3,0,2,1:T(4,128)S(1)} %select_bitcast_fusion.18), channel_id=1, source_target_pairs={{32,0},{64,32},{96,64},{128,96},{160,128},{192,160},{224,192},{256... | collective-permute-start | bytes 49160 | tf_op jit(solution)/shard_map/ppermute | solution.py:24
  180.4 12.1 %collective-permute-start.9 = (f32[4,3,1,1024]{3,0,2,1:T(4,128)S(1)}, f32[4,3,1,1024]{3,0,2,1:T(4,128)S(1)}, u32[]{:S(2)}, u32[]{:S(2)}) collective-permute-start(f32[4,3,1,1024]{3,0,2,1:T(4,128)S(1)} %pad_maximum_fusion.25), channel_id=1, source_target_pairs={{1,0},{2,1},{3,2},{4,3},{5,4},{6,5},{7,6},{8,7},{9,8},{10,9},{11,1... | collective-permute-start | bytes 147464 | tf_op jit(solution)/shard_map/ppermute | solution.py:24
  192.5 13.8 %collective-permute-done.9 = f32[4,3,1,1024]{3,0,2,1:T(4,128)S(1)} collective-permute-done((f32[4,3,1,1024]{3,0,2,1:T(4,128)S(1)}, f32[4,3,1,1024]{3,0,2,1:T(4,128)S(1)}, u32[]{:S(2)}, u32[]{:S(2)}) %collective-permute-start.9) | collective-permute-done | bytes 49184 | tf_op jit(solution)/shard_map/ppermute | solution.py:24
  212.1 13.9 %collective-permute-done.10 = f32[4,9,24,128]{3,0,2,1:T(4,128)S(1)} collective-permute-done((f32[4,9,24,128]{3,0,2,1:T(4,128)S(1)}, f32[4,9,24,128]{3,0,2,1:T(4,128)S(1)}, u32[]{:S(2)}, u32[]{:S(2)}) %collective-permute-start.10) | collective-permute-done | bytes 442400 | tf_op jit(solution)/shard_map/ppermute | solution.py:38
  229.3 83.0 %while.57 = (s32[]{:T(128)}, f32[3,40,128]{2,1,0:T(8,128)S(1)}, f32[4,8,40,128]{3,1,0,2:T(8,128)}, f32[3,40,128]{2,1,0:T(8,128)S(1)}, s32[]{:T(128)}, /*index=5*/s32[]{:T(128)}, s32[]{}) while((s32[]{:T(128)}, f32[3,40,128]{2,1,0:T(8,128)S(1)}, f32[4,8,40,128]{3,1,0,2:T(8,128)}, f32[3,40,128]{2,1,0:T(8,128)S(1)}, s32[]{:T(128)}, ...), condition=%wide.region_7.13_spmd.clone, body=%wide.region_4.12_spmd.clone.sunk | while | flops 17054724 | bytes 11284591 | solution.py:56
  234.8 4.8 fusion.42
  255.6 4.8 fusion.42
  276.3 4.8 fusion.42
  297.1 4.8 fusion.42
  307.5 4.8 fusion.42
  317.0 8.3 %collective-permute-done.11 = f32[3,24,128]{2,0,1:T(4,128)S(1)} collective-permute-done((f32[3,24,128]{2,0,1:T(4,128)S(1)}, f32[3,24,128]{2,0,1:T(4,128)S(1)}, u32[]{:S(2)}, u32[]{:S(2)}) %collective-permute-start.11) | collective-permute-done | bytes 36896 | tf_op jit(solution)/shard_map/ppermute | solution.py:38
  328.8 10.8 %collective-permute-start.13 = (f32[4,1,1,1024]{3,0,2,1:T(4,128)S(1)}, f32[4,1,1,1024]{3,0,2,1:T(4,128)S(1)}, u32[]{:S(2)}, u32[]{:S(2)}) collective-permute-start(f32[4,1,1,1024]{3,0,2,1:T(4,128)S(1)} %select_bitcast_fusion.17), channel_id=1, source_target_pairs={{32,0},{64,32},{96,64},{128,96},{160,128},{192,160},{224,192},{256... | collective-permute-start | bytes 49160 | tf_op jit(solution)/shard_map/ppermute | solution.py:24
  343.0 12.1 %collective-permute-start.15 = (f32[4,3,1,1024]{3,0,2,1:T(4,128)S(1)}, f32[4,3,1,1024]{3,0,2,1:T(4,128)S(1)}, u32[]{:S(2)}, u32[]{:S(2)}) collective-permute-start(f32[4,3,1,1024]{3,0,2,1:T(4,128)S(1)} %pad_maximum_fusion.26), channel_id=1, source_target_pairs={{1,0},{2,1},{3,2},{4,3},{5,4},{6,5},{7,6},{8,7},{9,8},{10,9},{11,1... | collective-permute-start | bytes 147464 | tf_op jit(solution)/shard_map/ppermute | solution.py:24
  355.2 8.8 %collective-permute-done.15 = f32[4,3,1,1024]{3,0,2,1:T(4,128)S(1)} collective-permute-done((f32[4,3,1,1024]{3,0,2,1:T(4,128)S(1)}, f32[4,3,1,1024]{3,0,2,1:T(4,128)S(1)}, u32[]{:S(2)}, u32[]{:S(2)}) %collective-permute-start.15) | collective-permute-done | bytes 49184 | tf_op jit(solution)/shard_map/ppermute | solution.py:24
  367.1 8.7 %collective-permute-start.16 = (f32[4,9,24,128]{3,0,2,1:T(4,128)S(1)}, f32[4,9,24,128]{3,0,2,1:T(4,128)S(1)}, u32[]{:S(2)}, u32[]{:S(2)}) collective-permute-start(f32[4,9,24,128]{3,0,2,1:T(4,128)S(1)} %pad_maximum_fusion.10), channel_id=1, source_target_pairs={{0,16},{16,0},{1,17},{17,1},{2,18},{18,2},{3,19},{19,3},{4,20},{20... | collective-permute-start | bytes 1327112 | tf_op jit(solution)/shard_map/ppermute | solution.py:38
  375.9 10.2 %collective-permute-done.16 = f32[4,9,24,128]{3,0,2,1:T(4,128)S(1)} collective-permute-done((f32[4,9,24,128]{3,0,2,1:T(4,128)S(1)}, f32[4,9,24,128]{3,0,2,1:T(4,128)S(1)}, u32[]{:S(2)}, u32[]{:S(2)}) %collective-permute-start.16) | collective-permute-done | bytes 442400 | tf_op jit(solution)/shard_map/ppermute | solution.py:38
  389.5 83.1 %while.58 = (s32[]{:T(128)}, f32[3,40,128]{2,1,0:T(8,128)S(1)}, f32[4,8,40,128]{3,1,0,2:T(8,128)}, f32[3,40,128]{2,1,0:T(8,128)S(1)}, s32[]{:T(128)}, /*index=5*/s32[]{:T(128)}, s32[]{}) while((s32[]{:T(128)}, f32[3,40,128]{2,1,0:T(8,128)S(1)}, f32[4,8,40,128]{3,1,0,2:T(8,128)}, f32[3,40,128]{2,1,0:T(8,128)S(1)}, s32[]{:T(128)}, ...), condition=%wide.region_11.17_spmd.clone, body=%wide.region_8.16_spmd.clone.sunk | while | flops 17054724 | bytes 11284591 | solution.py:56
  405.4 4.8 fusion.44
  473.3 8.3 %collective-permute-start.17 = (f32[3,24,128]{2,0,1:T(4,128)S(1)}, f32[3,24,128]{2,0,1:T(4,128)S(1)}, u32[]{:S(2)}, u32[]{:S(2)}) collective-permute-start(f32[3,24,128]{2,0,1:T(4,128)S(1)} %select_bitcast_fusion.13), channel_id=1, source_target_pairs={{0,16},{16,0},{1,17},{17,1},{2,18},{18,2},{3,19},{19,3},{4,20},{20... | collective-permute-start | bytes 110600 | tf_op jit(solution)/shard_map/ppermute | solution.py:38
  488.5 10.8 %collective-permute-start.19 = (f32[4,1,1,1024]{3,0,2,1:T(4,128)S(1)}, f32[4,1,1,1024]{3,0,2,1:T(4,128)S(1)}, u32[]{:S(2)}, u32[]{:S(2)}) collective-permute-start(f32[4,1,1,1024]{3,0,2,1:T(4,128)S(1)} %select_bitcast_fusion.16), channel_id=1, source_target_pairs={{32,0},{64,32},{96,64},{128,96},{160,128},{192,160},{224,192},{256... | collective-permute-start | bytes 49160 | tf_op jit(solution)/shard_map/ppermute | solution.py:24
  502.7 12.3 %collective-permute-start.21 = (f32[4,3,1,1024]{3,0,2,1:T(4,128)S(1)}, f32[4,3,1,1024]{3,0,2,1:T(4,128)S(1)}, u32[]{:S(2)}, u32[]{:S(2)}) collective-permute-start(f32[4,3,1,1024]{3,0,2,1:T(4,128)S(1)} %pad_maximum_fusion.27), channel_id=1, source_target_pairs={{1,0},{2,1},{3,2},{4,3},{5,4},{6,5},{7,6},{8,7},{9,8},{10,9},{11,1... | collective-permute-start | bytes 147464 | tf_op jit(solution)/shard_map/ppermute | solution.py:24
  515.0 9.9 %collective-permute-done.21 = f32[4,3,1,1024]{3,0,2,1:T(4,128)S(1)} collective-permute-done((f32[4,3,1,1024]{3,0,2,1:T(4,128)S(1)}, f32[4,3,1,1024]{3,0,2,1:T(4,128)S(1)}, u32[]{:S(2)}, u32[]{:S(2)}) %collective-permute-start.21) | collective-permute-done | bytes 49184 | tf_op jit(solution)/shard_map/ppermute | solution.py:24
  528.1 6.2 collective-permute-start.22
  534.4 12.7 %collective-permute-done.22 = f32[4,9,24,128]{3,0,2,1:T(4,128)S(1)} collective-permute-done((f32[4,9,24,128]{3,0,2,1:T(4,128)S(1)}, f32[4,9,24,128]{3,0,2,1:T(4,128)S(1)}, u32[]{:S(2)}, u32[]{:S(2)}) %collective-permute-start.22) | collective-permute-done | bytes 442400 | tf_op jit(solution)/shard_map/ppermute | solution.py:38
  550.5 83.1 %while.59 = (s32[]{:T(128)}, f32[3,40,128]{2,1,0:T(8,128)S(1)}, f32[4,8,40,128]{3,1,0,2:T(8,128)}, f32[3,40,128]{2,1,0:T(8,128)S(1)}, s32[]{:T(128)}, /*index=5*/s32[]{:T(128)}, s32[]{}) while((s32[]{:T(128)}, f32[3,40,128]{2,1,0:T(8,128)S(1)}, f32[4,8,40,128]{3,1,0,2:T(8,128)}, f32[3,40,128]{2,1,0:T(8,128)S(1)}, s32[]{:T(128)}, ...), condition=%wide.region_15.21_spmd.clone, body=%wide.region_12.20_spmd.clone.sunk | while | flops 17054724 | bytes 11284591 | solution.py:56
  634.3 5.9 collective-permute-start.23
  640.2 6.3 collective-permute-done.23
  (423 shorter events, 380.2 us)
Async XLA Ops:
  3.6 15.7 %collective-permute-start = (f32[4,1,1,1024]{3,0,2,1:T(4,128)S(1)}, f32[4,1,1,1024]{3,0,2,1:T(4,128)S(1)}, u32[]{:S(2)}, u32[]{:S(2)}) collective-permute-start(f32[4,1,1,1024]{3,0,2,1:T(4,128)S(1)} %select_bitcast_fusion.19), channel_id=1, source_target_pairs={{0,32},{32,64},{64,96},{96,128},{128,160},{160,192},{192,224},{224... | collective-permute-start | bytes 49160 | tf_op jit(solution)/shard_map/ppermute | solution.py:22
  5.5 13.8 %collective-permute-start.1 = (f32[4,1,1,1024]{3,0,2,1:T(4,128)S(1)}, f32[4,1,1,1024]{3,0,2,1:T(4,128)S(1)}, u32[]{:S(2)}, u32[]{:S(2)}) collective-permute-start(f32[4,1,1,1024]{3,0,2,1:T(4,128)S(1)} %select_bitcast_fusion.19), channel_id=1, source_target_pairs={{32,0},{64,32},{96,64},{128,96},{160,128},{192,160},{224,192},{256... | collective-permute-start | bytes 49160 | tf_op jit(solution)/shard_map/ppermute | solution.py:24
  19.3 14.9 %collective-permute-start.2 = (f32[4,3,1,1024]{3,0,2,1:T(4,128)S(1)}, f32[4,3,1,1024]{3,0,2,1:T(4,128)S(1)}, u32[]{:S(2)}, u32[]{:S(2)}) collective-permute-start(f32[4,3,1,1024]{3,0,2,1:T(4,128)S(1)} %pad_maximum_fusion.24), channel_id=1, source_target_pairs={{0,1},{1,2},{2,3},{3,4},{4,5},{5,6},{6,7},{7,8},{8,9},{9,10},{10,1... | collective-permute-start | bytes 147464 | tf_op jit(solution)/shard_map/ppermute | solution.py:22
  21.3 17.5 %collective-permute-start.3 = (f32[4,3,1,1024]{3,0,2,1:T(4,128)S(1)}, f32[4,3,1,1024]{3,0,2,1:T(4,128)S(1)}, u32[]{:S(2)}, u32[]{:S(2)}) collective-permute-start(f32[4,3,1,1024]{3,0,2,1:T(4,128)S(1)} %pad_maximum_fusion.24), channel_id=1, source_target_pairs={{1,0},{2,1},{3,2},{4,3},{5,4},{6,5},{7,6},{8,7},{9,8},{10,9},{11,1... | collective-permute-start | bytes 147464 | tf_op jit(solution)/shard_map/ppermute | solution.py:24
  42.9 21.9 %collective-permute-start.4 = (f32[4,9,24,128]{3,0,2,1:T(4,128)S(1)}, f32[4,9,24,128]{3,0,2,1:T(4,128)S(1)}, u32[]{:S(2)}, u32[]{:S(2)}) collective-permute-start(f32[4,9,24,128]{3,0,2,1:T(4,128)S(1)} %pad_maximum_fusion.8), channel_id=1, source_target_pairs={{0,16},{16,0},{1,17},{17,1},{2,18},{18,2},{3,19},{19,3},{4,20},{20... | collective-permute-start | bytes 1327112 | tf_op jit(solution)/shard_map/ppermute | solution.py:38
  67.2 94.3 %copy-start = (f32[3,8192]{1,0:T(4,128)S(1)}, f32[3,8192]{1,0:T(4,128)}, u32[]{:S(2)}) copy-start(f32[3,8192]{1,0:T(4,128)} %param.25) | copy-start | bytes 294916
  67.3 94.3 %copy-start.2 = (f32[3,8192]{1,0:T(4,128)S(1)}, f32[3,8192]{1,0:T(4,128)}, u32[]{:S(2)}) copy-start(f32[3,8192]{1,0:T(4,128)} %param.28) | copy-start | bytes 294916
  67.3 94.3 %copy-start.3 = (f32[3,8192]{1,0:T(4,128)S(1)}, f32[3,8192]{1,0:T(4,128)}, u32[]{:S(2)}) copy-start(f32[3,8192]{1,0:T(4,128)} %param.26) | copy-start | bytes 294916
  67.3 94.4 %copy-start.1 = (f32[8192]{0:T(1024)S(1)}, f32[8192]{0:T(1024)}, u32[]{:S(2)}) copy-start(f32[8192]{0:T(1024)} %param.27) | copy-start | bytes 98308
  149.2 12.3 %collective-permute-start.5 = (f32[3,24,128]{2,0,1:T(4,128)S(1)}, f32[3,24,128]{2,0,1:T(4,128)S(1)}, u32[]{:S(2)}, u32[]{:S(2)}) collective-permute-start(f32[3,24,128]{2,0,1:T(4,128)S(1)} %select_bitcast_fusion.15), channel_id=1, source_target_pairs={{0,16},{16,0},{1,17},{17,1},{2,18},{18,2},{3,19},{19,3},{4,20},{20... | collective-permute-start | bytes 110600 | tf_op jit(solution)/shard_map/ppermute | solution.py:38
  162.4 14.6 %collective-permute-start.6 = (f32[4,1,1,1024]{3,0,2,1:T(4,128)S(1)}, f32[4,1,1,1024]{3,0,2,1:T(4,128)S(1)}, u32[]{:S(2)}, u32[]{:S(2)}) collective-permute-start(f32[4,1,1,1024]{3,0,2,1:T(4,128)S(1)} %select_bitcast_fusion.18), channel_id=1, source_target_pairs={{0,32},{32,64},{64,96},{96,128},{128,160},{160,192},{192,224},{224... | collective-permute-start | bytes 49160 | tf_op jit(solution)/shard_map/ppermute | solution.py:22
  164.3 14.1 %collective-permute-start.7 = (f32[4,1,1,1024]{3,0,2,1:T(4,128)S(1)}, f32[4,1,1,1024]{3,0,2,1:T(4,128)S(1)}, u32[]{:S(2)}, u32[]{:S(2)}) collective-permute-start(f32[4,1,1,1024]{3,0,2,1:T(4,128)S(1)} %select_bitcast_fusion.18), channel_id=1, source_target_pairs={{32,0},{64,32},{96,64},{128,96},{160,128},{192,160},{224,192},{256... | collective-permute-start | bytes 49160 | tf_op jit(solution)/shard_map/ppermute | solution.py:24
  178.5 14.0 %collective-permute-start.8 = (f32[4,3,1,1024]{3,0,2,1:T(4,128)S(1)}, f32[4,3,1,1024]{3,0,2,1:T(4,128)S(1)}, u32[]{:S(2)}, u32[]{:S(2)}) collective-permute-start(f32[4,3,1,1024]{3,0,2,1:T(4,128)S(1)} %pad_maximum_fusion.25), channel_id=1, source_target_pairs={{0,1},{1,2},{2,3},{3,4},{4,5},{5,6},{6,7},{7,8},{8,9},{9,10},{10,1... | collective-permute-start | bytes 147464 | tf_op jit(solution)/shard_map/ppermute | solution.py:22
  180.4 25.9 %collective-permute-start.9 = (f32[4,3,1,1024]{3,0,2,1:T(4,128)S(1)}, f32[4,3,1,1024]{3,0,2,1:T(4,128)S(1)}, u32[]{:S(2)}, u32[]{:S(2)}) collective-permute-start(f32[4,3,1,1024]{3,0,2,1:T(4,128)S(1)} %pad_maximum_fusion.25), channel_id=1, source_target_pairs={{1,0},{2,1},{3,2},{4,3},{5,4},{6,5},{7,6},{8,7},{9,8},{10,9},{11,1... | collective-permute-start | bytes 147464 | tf_op jit(solution)/shard_map/ppermute | solution.py:24
  209.4 16.5 %collective-permute-start.10 = (f32[4,9,24,128]{3,0,2,1:T(4,128)S(1)}, f32[4,9,24,128]{3,0,2,1:T(4,128)S(1)}, u32[]{:S(2)}, u32[]{:S(2)}) collective-permute-start(f32[4,9,24,128]{3,0,2,1:T(4,128)S(1)} %pad_maximum_fusion.9), channel_id=1, source_target_pairs={{0,16},{16,0},{1,17},{17,1},{2,18},{18,2},{3,19},{19,3},{4,20},{20... | collective-permute-start | bytes 1327112 | tf_op jit(solution)/shard_map/ppermute | solution.py:38
  313.0 12.3 %collective-permute-start.11 = (f32[3,24,128]{2,0,1:T(4,128)S(1)}, f32[3,24,128]{2,0,1:T(4,128)S(1)}, u32[]{:S(2)}, u32[]{:S(2)}) collective-permute-start(f32[3,24,128]{2,0,1:T(4,128)S(1)} %select_bitcast_fusion.14), channel_id=1, source_target_pairs={{0,16},{16,0},{1,17},{17,1},{2,18},{18,2},{3,19},{19,3},{4,20},{20... | collective-permute-start | bytes 110600 | tf_op jit(solution)/shard_map/ppermute | solution.py:38
  325.4 38.7 %copy-start.6 = (f32[3,64,128]{2,0,1:T(4,128)}, f32[3,64,128]{2,0,1:T(4,128)S(1)}, u32[]{:S(2)}) copy-start(f32[3,64,128]{2,0,1:T(4,128)S(1)} %constant_dynamic-update-slice_fusion.2) | copy-start | bytes 294916
  326.9 12.8 %collective-permute-start.12 = (f32[4,1,1,1024]{3,0,2,1:T(4,128)S(1)}, f32[4,1,1,1024]{3,0,2,1:T(4,128)S(1)}, u32[]{:S(2)}, u32[]{:S(2)}) collective-permute-start(f32[4,1,1,1024]{3,0,2,1:T(4,128)S(1)} %select_bitcast_fusion.17), channel_id=1, source_target_pairs={{0,32},{32,64},{64,96},{96,128},{128,160},{160,192},{192,224},{224... | collective-permute-start | bytes 49160 | tf_op jit(solution)/shard_map/ppermute | solution.py:22
  328.8 12.3 %collective-permute-start.13 = (f32[4,1,1,1024]{3,0,2,1:T(4,128)S(1)}, f32[4,1,1,1024]{3,0,2,1:T(4,128)S(1)}, u32[]{:S(2)}, u32[]{:S(2)}) collective-permute-start(f32[4,1,1,1024]{3,0,2,1:T(4,128)S(1)} %select_bitcast_fusion.17), channel_id=1, source_target_pairs={{32,0},{64,32},{96,64},{128,96},{160,128},{192,160},{224,192},{256... | collective-permute-start | bytes 49160 | tf_op jit(solution)/shard_map/ppermute | solution.py:24
  341.1 14.0 %collective-permute-start.14 = (f32[4,3,1,1024]{3,0,2,1:T(4,128)S(1)}, f32[4,3,1,1024]{3,0,2,1:T(4,128)S(1)}, u32[]{:S(2)}, u32[]{:S(2)}) collective-permute-start(f32[4,3,1,1024]{3,0,2,1:T(4,128)S(1)} %pad_maximum_fusion.26), channel_id=1, source_target_pairs={{0,1},{1,2},{2,3},{3,4},{4,5},{5,6},{6,7},{7,8},{8,9},{9,10},{10,1... | collective-permute-start | bytes 147464 | tf_op jit(solution)/shard_map/ppermute | solution.py:22
  343.0 20.9 %collective-permute-start.15 = (f32[4,3,1,1024]{3,0,2,1:T(4,128)S(1)}, f32[4,3,1,1024]{3,0,2,1:T(4,128)S(1)}, u32[]{:S(2)}, u32[]{:S(2)}) collective-permute-start(f32[4,3,1,1024]{3,0,2,1:T(4,128)S(1)} %pad_maximum_fusion.26), channel_id=1, source_target_pairs={{1,0},{2,1},{3,2},{4,3},{5,4},{6,5},{7,6},{8,7},{9,8},{10,9},{11,1... | collective-permute-start | bytes 147464 | tf_op jit(solution)/shard_map/ppermute | solution.py:24
  367.1 19.0 %collective-permute-start.16 = (f32[4,9,24,128]{3,0,2,1:T(4,128)S(1)}, f32[4,9,24,128]{3,0,2,1:T(4,128)S(1)}, u32[]{:S(2)}, u32[]{:S(2)}) collective-permute-start(f32[4,9,24,128]{3,0,2,1:T(4,128)S(1)} %pad_maximum_fusion.10), channel_id=1, source_target_pairs={{0,16},{16,0},{1,17},{17,1},{2,18},{18,2},{3,19},{19,3},{4,20},{20... | collective-permute-start | bytes 1327112 | tf_op jit(solution)/shard_map/ppermute | solution.py:38
  389.5 96.1 %copy-start.9 = (f32[3,64,128]{2,0,1:T(4,128)S(1)}, f32[3,64,128]{2,0,1:T(4,128)}, u32[]{:S(2)}) copy-start(f32[3,64,128]{2,0,1:T(4,128)} %get-tuple-element.482) | copy-start | bytes 294916
  473.3 12.3 %collective-permute-start.17 = (f32[3,24,128]{2,0,1:T(4,128)S(1)}, f32[3,24,128]{2,0,1:T(4,128)S(1)}, u32[]{:S(2)}, u32[]{:S(2)}) collective-permute-start(f32[3,24,128]{2,0,1:T(4,128)S(1)} %select_bitcast_fusion.13), channel_id=1, source_target_pairs={{0,16},{16,0},{1,17},{17,1},{2,18},{18,2},{3,19},{19,3},{4,20},{20... | collective-permute-start | bytes 110600 | tf_op jit(solution)/shard_map/ppermute | solution.py:38
  485.6 39.4 %copy-start.8 = (f32[3,64,128]{2,0,1:T(4,128)}, f32[3,64,128]{2,0,1:T(4,128)S(1)}, u32[]{:S(2)}) copy-start(f32[3,64,128]{2,0,1:T(4,128)S(1)} %constant_dynamic-update-slice_fusion.4) | copy-start | bytes 294916
  486.6 12.8 %collective-permute-start.18 = (f32[4,1,1,1024]{3,0,2,1:T(4,128)S(1)}, f32[4,1,1,1024]{3,0,2,1:T(4,128)S(1)}, u32[]{:S(2)}, u32[]{:S(2)}) collective-permute-start(f32[4,1,1,1024]{3,0,2,1:T(4,128)S(1)} %select_bitcast_fusion.16), channel_id=1, source_target_pairs={{0,32},{32,64},{64,96},{96,128},{128,160},{160,192},{192,224},{224... | collective-permute-start | bytes 49160 | tf_op jit(solution)/shard_map/ppermute | solution.py:22
  488.5 12.3 %collective-permute-start.19 = (f32[4,1,1,1024]{3,0,2,1:T(4,128)S(1)}, f32[4,1,1,1024]{3,0,2,1:T(4,128)S(1)}, u32[]{:S(2)}, u32[]{:S(2)}) collective-permute-start(f32[4,1,1,1024]{3,0,2,1:T(4,128)S(1)} %select_bitcast_fusion.16), channel_id=1, source_target_pairs={{32,0},{64,32},{96,64},{128,96},{160,128},{192,160},{224,192},{256... | collective-permute-start | bytes 49160 | tf_op jit(solution)/shard_map/ppermute | solution.py:24
  500.8 14.3 %collective-permute-start.20 = (f32[4,3,1,1024]{3,0,2,1:T(4,128)S(1)}, f32[4,3,1,1024]{3,0,2,1:T(4,128)S(1)}, u32[]{:S(2)}, u32[]{:S(2)}) collective-permute-start(f32[4,3,1,1024]{3,0,2,1:T(4,128)S(1)} %pad_maximum_fusion.27), channel_id=1, source_target_pairs={{0,1},{1,2},{2,3},{3,4},{4,5},{5,6},{6,7},{7,8},{8,9},{9,10},{10,1... | collective-permute-start | bytes 147464 | tf_op jit(solution)/shard_map/ppermute | solution.py:22
  502.7 22.3 %collective-permute-start.21 = (f32[4,3,1,1024]{3,0,2,1:T(4,128)S(1)}, f32[4,3,1,1024]{3,0,2,1:T(4,128)S(1)}, u32[]{:S(2)}, u32[]{:S(2)}) collective-permute-start(f32[4,3,1,1024]{3,0,2,1:T(4,128)S(1)} %pad_maximum_fusion.27), channel_id=1, source_target_pairs={{1,0},{2,1},{3,2},{4,3},{5,4},{6,5},{7,6},{8,7},{9,8},{10,9},{11,1... | collective-permute-start | bytes 147464 | tf_op jit(solution)/shard_map/ppermute | solution.py:24
  528.1 19.0 %collective-permute-start.22 = (f32[4,9,24,128]{3,0,2,1:T(4,128)S(1)}, f32[4,9,24,128]{3,0,2,1:T(4,128)S(1)}, u32[]{:S(2)}, u32[]{:S(2)}) collective-permute-start(f32[4,9,24,128]{3,0,2,1:T(4,128)S(1)} %pad_maximum_fusion.11), channel_id=1, source_target_pairs={{0,16},{16,0},{1,17},{17,1},{2,18},{18,2},{3,19},{19,3},{4,20},{20... | collective-permute-start | bytes 1327112 | tf_op jit(solution)/shard_map/ppermute | solution.py:38
  550.5 96.1 %copy-start.7 = (f32[3,64,128]{2,0,1:T(4,128)S(1)}, f32[3,64,128]{2,0,1:T(4,128)}, u32[]{:S(2)}) copy-start(f32[3,64,128]{2,0,1:T(4,128)} %copy-done.6) | copy-start | bytes 294916
  634.3 12.3 %collective-permute-start.23 = (f32[3,24,128]{2,0,1:T(4,128)S(1)}, f32[3,24,128]{2,0,1:T(4,128)S(1)}, u32[]{:S(2)}, u32[]{:S(2)}) collective-permute-start(f32[3,24,128]{2,0,1:T(4,128)S(1)} %select_bitcast_fusion.12), channel_id=1, source_target_pairs={{0,16},{16,0},{1,17},{17,1},{2,18},{18,2},{3,19},{19,3},{4,20},{20... | collective-permute-start | bytes 110600 | tf_op jit(solution)/shard_map/ppermute | solution.py:38
  (16 other events, 45.6 us)
where the time goes:
time: 661 us; the launch traced here: 648 us
  other arithmetic  283 us (43%)
  starting transfers between devices  156 us (24%)
  waiting for transfers between devices  120 us (18%)
  local copies, waits for them, and re-layouts  85.2 us (13%)
    reduce_sum x32, other arithmetic, pair_accel(): return jnp.sum(offsets * weight[None], axis=3)  153 us
    ppermute x8, starting transfers between devices, with_halo(): lax.ppermute(head, axis, [((i + 1) % count, i) for i in range(count)])  93.7 us
    reduce_sum x32, other arithmetic, pair_accel(): distance = jnp.sum(offsets * offsets, axis=0)  82.9 us
    ppermute x8, waiting for transfers between devices, swapped(): return lax.ppermute(block, axis, route)  78.2 us
    ppermute x8, starting transfers between devices, swapped(): return lax.ppermute(block, axis, route)  47 us
    ppermute x8, waiting for transfers between devices, with_halo(): lax.ppermute(head, axis, [((i + 1) % count, i) for i in range(count)])  41.3 us
    slice x32, local copies, waits for them, and re-layouts, pair_accel(): weight = sources[3][:, None, :] * tapers * inverse * inverse * inverse  30.1 us
    mul x32, other arithmetic, pair_accel(): weight = sources[3][:, None, :] * tapers * inverse * inverse * inverse  28.4 us
  transfers between devices with their start and end apart: 24, of which 15 were waited for; matrix products, arithmetic and copies ran while one was open for 1% of the time, Pallas kernels for 0%

commit v1 on v0

v1 whole, which is shorter than its diff:
```python
import jax
import jax.numpy as jnp
from jax import lax
from jax.experimental import pallas as pl
from jax.experimental.pallas import tpu as pltpu
from jax.sharding import PartitionSpec as P

SUBCYCLES = 4
LEAF = 128
LEAVES = 64
GHOSTS = 8
NEIGHBOURS = 8
POOL = LEAVES + 9 * GHOSTS
FEATURES = 32
SUMS = 16
GROUP = 4
UNROLL = 8

soften_sq = 0.04
cutoff_sq = 9.0
time_step = 0.5

f32, bf16 = jnp.float32, jnp.bfloat16


def three_parts(value):
    first = value.astype(bf16).astype(f32)
    rest = value - first
    second = rest.astype(bf16).astype(f32)
    return first, second, (rest - second).astype(bf16).astype(f32)


def norm_parts(record, more=0.0):
    square = record * record
    return three_parts(square[0:1] + square[1:2] + square[2:3] + more)


def with_row(parts, row):
    last = lax.broadcasted_iota(jnp.int32, parts.shape, 0) == 3
    return jnp.where(last, jnp.broadcast_to(row, parts.shape), parts)


def source_features(record):
    a, b, c = three_parts(record)
    n1, n2, n3 = norm_parts(record)
    one = jnp.ones_like(n1)
    zero = jnp.zeros((8, LEAF), f32)
    return jnp.concatenate(
        [
            with_row(a, n1),
            with_row(a, n2),
            with_row(b, n3),
            with_row(b, one),
            with_row(a, one),
            with_row(c, one),
            zero,
        ],
        axis=0,
    )


def target_features(record):
    a, b, c = three_parts(record * -2.0)
    n1, n2, n3 = norm_parts(record, soften_sq)
    one = jnp.ones_like(n1)
    zero = jnp.zeros((8, LEAF), f32)
    return jnp.concatenate(
        [
            with_row(a, one),
            with_row(b, one),
            with_row(a, one),
            with_row(b, n1),
            with_row(c, n2),
            with_row(a, n3),
            zero,
        ],
        axis=0,
    )


def moment_rows(record):
    mass = jnp.broadcast_to(record[3:4], record.shape)
    a, b, c = three_parts(with_row(record, jnp.ones((1, LEAF), f32)) * mass)
    return jnp.concatenate([a, b, c, jnp.zeros_like(a)], axis=0).astype(bf16)


def enter(sources, moments, slot, record):
    features = source_features(record)
    blank = jnp.zeros((LEAF - FEATURES, LEAF), f32)
    sources[slot] = jnp.concatenate([features, blank], axis=0).T.astype(bf16)
    moments[slot] = moment_rows(record)


def enter_all(sources, moments, rows, slot_of, many):
    def some(index, carry):
        for u in range(UNROLL):
            row = index * UNROLL + u
            enter(sources, moments, slot_of(row), rows[row])
        return carry

    lax.fori_loop(0, many // UNROLL, some, 0)


def pair_sums(lists, sources, moments, leaves, records):
    blank = jnp.zeros((FEATURES, LEAF), bf16)
    rest = jnp.zeros((LEAF - FEATURES, 2 * LEAF), bf16)
    first, second = (target_features(r).astype(bf16) for r in records)
    targets = jnp.concatenate(
        [
            jnp.concatenate([first, blank], axis=1),
            rest,
            jnp.concatenate([blank, second], axis=1),
            rest,
        ],
        axis=0,
    )
    total = jnp.zeros((2 * SUMS, 2 * LEAF), f32)
    for n in range(NEIGHBOURS):
        slots = [lists[n, leaf] for leaf in leaves]
        apart = jnp.dot(
            jnp.concatenate([sources[s] for s in slots], axis=1),
            targets,
            preferred_element_type=f32,
        )
        near = jnp.maximum(apart, soften_sq)
        taper = jnp.maximum(cutoff_sq + soften_sq - near, 0.0)
        inverse = lax.rsqrt(near)
        product = taper * inverse
        weight = product * product * inverse
        high = weight.astype(bf16)
        low = (weight - high.astype(f32)).astype(bf16)
        rows = jnp.concatenate([moments[s] for s in slots], axis=0)
        total += jnp.dot(
            jnp.concatenate([rows, rows], axis=1),
            jnp.concatenate([high, low], axis=0),
            preferred_element_type=f32,
        )
    return total[:SUMS, :LEAF], total[SUMS:, LEAF:]


def moved(total, record, speed, kick):
    sums = (total[0:4] + total[4:8] + total[8:12]) * (1.0 / (cutoff_sq * cutoff_sq))
    accel = sums - record * jnp.broadcast_to(sums[3:4], sums.shape)
    row = lax.broadcasted_iota(jnp.int32, record.shape, 0)
    speed = jnp.where(row < 3, speed + time_step * (accel + kick), 0.0)
    return record + time_step * speed, speed


def group_moved(lists, sources, moments, own, speeds, kicks, leaves):
    records = [own[leaf] for leaf in leaves]
    totals = []
    for k in range(0, GROUP, 2):
        totals += pair_sums(lists, sources, moments, leaves[k : k + 2], records[k : k + 2])
    return [
        moved(total, record, speeds[leaf], kicks[leaf])
        for total, record, leaf in zip(totals, records, leaves)
    ]


def move_groups(lists, count, sources, moments, own, speeds, kicks, new_own, new_speeds, begin, end):
    def group(index, carry):
        leaves = [index * GROUP + u for u in range(GROUP)]
        results = group_moved(lists, sources, moments, own, speeds, kicks, leaves)
        for leaf, (record, speed) in zip(leaves, results):
            live = leaf < count[0]
            new_own[leaf] = jnp.where(live, record, own[leaf])
            new_speeds[leaf] = jnp.where(live, speed, speeds[leaf])
        return carry

    lax.fori_loop(begin, end, group, 0)


def choose_kernel(ids, own, chosen):
    for g in range(GHOSTS):
        chosen[g] = own[ids[g]]


def open_kernel(own, sources, moments):
    enter_all(sources, moments, own, lambda leaf: leaf, LEAVES)


def enter_ghosts(parity, sides, sources, moments):
    for q, side in enumerate(sides):
        b = jnp.where(parity[1] == 1, 2 - q, q)
        for p in range(3):
            a = jnp.where(parity[0] == 1, 2 - p, p)
            for g in range(GHOSTS):
                enter(sources, moments, LEAVES + (a * 3 + b) * GHOSTS + g, side[p * GHOSTS + g])


def ghost_kernel(
    lists, ids, parity, own, speeds, kicks, far, middle, near, old_sources, old_moments,
    sources, moments, chosen,
):
    enter_ghosts(parity, (far, middle, near), sources, moments)

    def group(index, carry):
        places = [index * GROUP + u for u in range(GROUP)]
        leaves = [ids[g] for g in places]
        results = group_moved(lists, sources, moments, own, speeds, kicks, leaves)
        for g, (record, _) in zip(places, results):
            chosen[g] = record
        return carry

    lax.fori_loop(0, GHOSTS // GROUP, group, 0)


def groups_of(count):
    return lax.div(count[0] + (GROUP - 1), GROUP)


def early_kernel(
    lists, count, own, speeds, kicks, sources, moments, new_own, new_speeds
):
    move_groups(
        lists, count, sources, moments, own, speeds, kicks, new_own, new_speeds,
        0, lax.div(groups_of(count), 2),
    )


def late_kernel(
    lists, count, own, speeds, kicks, old_sources, old_moments,
    new_own, new_speeds, sources, moments,
):
    groups = groups_of(count)
    move_groups(
        lists, count, sources, moments, own, speeds, kicks, new_own, new_speeds,
        lax.div(groups, 2), groups,
    )
    enter_all(sources, moments, new_own, lambda leaf: leaf, LEAVES)


def last_kernel(
    lists, parity, count, own, speeds, kicks, far, middle, near, old_sources, old_moments,
    new_own, new_speeds, sources, moments,
):
    enter_ghosts(parity, (far, middle, near), sources, moments)
    move_groups(
        lists, count, sources, moments, own, speeds, kicks, new_own, new_speeds,
        0, groups_of(count),
    )


VMEM = pl.BlockSpec(memory_space=pltpu.VMEM)
SMEM = pl.BlockSpec(memory_space=pltpu.SMEM)
record_shape = jax.ShapeDtypeStruct((LEAVES, 4, LEAF), f32)
chosen_shape = jax.ShapeDtypeStruct((GHOSTS, 4, LEAF), f32)
sources_shape = jax.ShapeDtypeStruct((POOL, LEAF, LEAF), bf16)
moments_shape = jax.ShapeDtypeStruct((POOL, SUMS, LEAF), bf16)


def call(kernel, name, scalars, arrays, outs, aliases=None, leaves=0):
    pairs = leaves * NEIGHBOURS * LEAF * LEAF
    return pl.pallas_call(
        kernel,
        out_shape=outs,
        in_specs=[SMEM] * len(scalars) + [VMEM] * len(arrays),
        out_specs=jax.tree.map(lambda _: VMEM, outs),
        input_output_aliases={len(scalars) + i: o for i, o in (aliases or {}).items()},
        compiler_params=pltpu.CompilerParams(vmem_limit_bytes=16 * 2**20),
        cost_estimate=pl.CostEstimate(
            flops=300 * pairs, bytes_accessed=2**20, transcendentals=pairs
        ),
        name=name,
    )(*scalars, *arrays)


def swapped(block, axis, odd):
    size = lax.axis_size(axis)
    route = []
    for i in range(odd, size + odd, 2):
        route += [(i % size, (i + 1) % size), ((i + 1) % size, i % size)]
    return lax.ppermute(block, axis, route)


def body(positions, velocities, masses, long_kick, leaf_lists, ghost_ids, leaf_counts):
    def records(parts):
        return jnp.swapaxes(parts.reshape(-1, LEAVES, LEAF), 0, 1)

    blank = jnp.zeros((1, LEAVES * LEAF), f32)
    own = records(jnp.concatenate([positions, masses[None]], axis=0))
    speeds = records(jnp.concatenate([velocities, blank], axis=0))
    kicks = records(jnp.concatenate([long_kick, blank], axis=0))
    parity = jnp.stack([lax.axis_index("gx"), lax.axis_index("gy")]).astype(jnp.int32) % 2
    lists, ids, count = leaf_lists, ghost_ids, leaf_counts

    chosen = call(choose_kernel, "choose", (ids,), (own,), chosen_shape)
    sources, moments = call(open_kernel, "open", (), (own,), (sources_shape, moments_shape))
    for subcycle in range(SUBCYCLES):
        far = swapped(chosen, "gx", 1)
        near = swapped(chosen, "gx", 0)
        if subcycle:
            own, speeds = call(
                early_kernel, "early", (lists, count), (own, speeds, kicks, sources, moments),
                (record_shape, record_shape), {0: 0, 1: 1}, LEAVES // 2,
            )
        middle = jnp.concatenate([far, chosen, near], axis=0)
        far = swapped(middle, "gy", 1)
        near = swapped(middle, "gy", 0)
        if subcycle:
            own, speeds, sources, moments = call(
                late_kernel, "late", (lists, count), (own, speeds, kicks, sources, moments),
                (record_shape, record_shape, sources_shape, moments_shape),
                {0: 0, 1: 1, 3: 2, 4: 3}, LEAVES // 2,
            )
        if subcycle < SUBCYCLES - 1:
            sources, moments, chosen = call(
                ghost_kernel, "ghost", (lists, ids, parity),
                (own, speeds, kicks, far, middle, near, sources, moments),
                (sources_shape, moments_shape, chosen_shape), {6: 0, 7: 1}, GHOSTS,
            )
        else:
            own, speeds, _, _ = call(
                last_kernel, "last", (lists, parity, count),
                (own, speeds, kicks, far, middle, near, sources, moments),
                (record_shape, record_shape, sources_shape, moments_shape),
                {0: 0, 1: 1, 6: 2, 7: 3}, LEAVES,
            )

    def whole(parts):
        return jnp.swapaxes(parts[:, :3], 0, 1).reshape(3, -1)

    return whole(own), whole(speeds)


def solution(mesh):
    split = P(("gx", "gy"))
    columns = P(None, ("gx", "gy"))
    return jax.shard_map(
        body,
        mesh=mesh,
        in_specs=(columns, columns, split, columns, columns, split, split),
        out_specs=(columns, columns),
        check_vma=False,
    )
```

time: 661 us -> 186 us (0.28); the launches traced: 648 us -> 185 us
  other arithmetic: 283 us -> 1.08 us
  Pallas kernels: 0 us -> 118 us
  waiting for transfers between devices: 120 us -> 6.27 us
  starting transfers between devices: 156 us -> 53.6 us
  local copies, waits for them, and re-layouts: 85.2 us -> 4.4 us
    reduce_sum x64 -> x0, other arithmetic: 236 us -> none  [the longest x32 153 us: pair_accel(): return jnp.sum(offsets * weight[None], axis=3)]
    pallas_call x0 -> x12, Pallas kernels: none -> 118 us  [call(): pl.pallas_call(kernel, out_shape=outs, in_specs=[SMEM] * len(scalars) + [...]
    ppermute x16 -> x0, starting transfers between devices: 109 us -> none  [the longest x8 93.7 us: with_halo(): lax.ppermute(head, axis, [((i + 1) % count, i) for i in range(count)])]
    ppermute x8 -> x16, waiting for transfers between devices: 78.2 us -> 6.27 us  [swapped(): return lax.ppermute(block, axis, route)]
    slice x80 -> x0, local copies, waits for them, and re-layouts: 58 us -> none  [the longest x32 30.1 us: pair_accel(): weight = sources[3][:, None, :] * tapers * inverse * inverse * inverse]
    ppermute x16 -> x0, waiting for transfers between devices: 41.4 us -> none  [the longest x8 41.3 us: with_halo(): lax.ppermute(head, axis, [((i + 1) % count, i) for i in range(count)])]
    mul x32 -> x0, other arithmetic: 28.4 us -> none  [pair_accel(): weight = sources[3][:, None, :] * tapers * inverse * inverse * inverse]
    gather x20 -> x0, local copies, waits for them, and re-layouts: 18 us -> none  [the longest x4 8.3 us: body(): operands = jnp.take(pool, leaf_lists, axis=1)]
  transfers between devices with their start and end apart: 24 -> 16, of which waited for: 15 -> 2; matrix products, arithmetic and copies ran while one was open for 1% -> 1% of each run, Pallas kernels for 0% -> 43%
where the time goes in v1:
time: 186 us; the launch traced here: 185 us
  Pallas kernels  118 us (63%)
  starting transfers between devices  53.6 us (29%)
  waiting for transfers between devices  6.27 us (3%)
  local copies, waits for them, and re-layouts  4.4 us (2%)
    pallas_call x12, Pallas kernels, call(): pl.pallas_call(kernel, out_shape=outs, in_specs=[SMEM] * len(scalars) + [...  118 us
    ppermute x16, starting transfers between devices, swapped(): return lax.ppermute(block, axis, route)  53.6 us
    ppermute x16, waiting for transfers between devices, swapped(): return lax.ppermute(block, axis, route)  6.27 us
  transfers between devices with their start and end apart: 16, of which 2 were waited for; matrix products, arithmetic and copies ran while one was open for 1% of the time, Pallas kernels for 43%

profile of v1, /device:TPU:0, one launch (start us, length us, event | category | flops | bytes accessed | tf_op | source)
XLA Modules:
  0.0 185.3 jit_solution(11154203190592537677)
XLA Ops:
  0.6 1.0 maximum_bitcast_fusion.own
  2.8 1.9 %collective-permute-start.1 = (f32[8,4,128]{2,1,0:T(4,128)S(1)}, f32[8,4,128]{2,1,0:T(4,128)S(1)}, u32[]{:S(2)}, u32[]{:S(2)}) collective-permute-start(f32[8,4,128]{2,1,0:T(4,128)S(1)} %choose.1), channel_id=1, source_target_pairs={{0,32},{32,0},{64,96},{96,64},{128,160},{160,128},{192,224},{224,1... | collective-permute-start | bytes 49160 | tf_op jit(solution)/shard_map/ppermute | solution.py:273
  4.8 6.7 %collective-permute-start = (f32[8,4,128]{2,1,0:T(4,128)S(1)}, f32[8,4,128]{2,1,0:T(4,128)S(1)}, u32[]{:S(2)}, u32[]{:S(2)}) collective-permute-start(f32[8,4,128]{2,1,0:T(4,128)S(1)} %choose.1), channel_id=1, source_target_pairs={{32,64},{64,32},{96,128},{128,96},{160,192},{192,160},{224,256},{2... | collective-permute-start | bytes 49160 | tf_op jit(solution)/shard_map/ppermute | solution.py:273
  11.5 1.0 pad_bitcast_fusion
  12.5 4.8 %collective-permute-done = f32[8,4,128]{2,1,0:T(4,128)S(1)} collective-permute-done((f32[8,4,128]{2,1,0:T(4,128)S(1)}, f32[8,4,128]{2,1,0:T(4,128)S(1)}, u32[]{:S(2)}, u32[]{:S(2)}) %collective-permute-start) | collective-permute-done | bytes 16416 | tf_op jit(solution)/shard_map/ppermute | solution.py:273
  17.3 1.9 %collective-permute-start.3 = (f32[24,4,128]{2,1,0:T(4,128)S(1)}, f32[24,4,128]{2,1,0:T(4,128)S(1)}, u32[]{:S(2)}, u32[]{:S(2)}) collective-permute-start(f32[24,4,128]{2,1,0:T(4,128)S(1)} %pad_maximum_fusion.middle), channel_id=1, source_target_pairs={{0,1},{1,0},{2,3},{3,2},{4,5},{5,4},{6,7},{7,6},{8,9},{9,8},{10,11... | collective-permute-start | bytes 147464 | tf_op jit(solution)/shard_map/ppermute | solution.py:273
  19.3 10.6 %collective-permute-start.2 = (f32[24,4,128]{2,1,0:T(4,128)S(1)}, f32[24,4,128]{2,1,0:T(4,128)S(1)}, u32[]{:S(2)}, u32[]{:S(2)}) collective-permute-start(f32[24,4,128]{2,1,0:T(4,128)S(1)} %pad_maximum_fusion.middle), channel_id=1, source_target_pairs={{1,2},{2,1},{3,4},{4,3},{5,6},{6,5},{7,8},{8,7},{9,10},{10,9},{11,... | collective-permute-start | bytes 147464 | tf_op jit(solution)/shard_map/ppermute | solution.py:273
  30.0 1.3 open.1
  31.9 1.5 collective-permute-done.2.far
  33.4 0.7 copy-done
  34.7 4.4 %ghost.3 = (bf16[136,128,128]{2,1,0:T(8,128)(2,1)S(1)}, bf16[136,16,128]{2,1,0:T(8,128)(2,1)S(1)}, f32[8,4,128]{2,1,0:T(4,128)S(1)}) custom-call(s32[8,64]{1,0:T(8,128)S(1)} %copy-done, s32[8]{0:T(128)S(1)} %copy-done.2, s32[2]{0:T(128)S(1)} %and_select_fusion.parity, ...), custom_call_target="tpu_custom_call", output_to_operand_aliasing={{0}: (9, {}), {1}: (10, {})} | custom-call | flops 314572800 | bytes 1048576 | tf_op jit(solution)/shard_map/ghost/pallas_call | solution.py:254
  39.1 1.9 %collective-permute-start.5 = (f32[8,4,128]{2,1,0:T(4,128)S(1)}, f32[8,4,128]{2,1,0:T(4,128)S(1)}, u32[]{:S(2)}, u32[]{:S(2)}) collective-permute-start(f32[8,4,128]{2,1,0:T(4,128)S(1)} %get-tuple-element.41), channel_id=1, source_target_pairs={{0,32},{32,0},{64,96},{96,64},{128,160},{160,128},{192,224},{224,1... | collective-permute-start | bytes 49160 | tf_op jit(solution)/shard_map/ppermute | solution.py:273
  41.0 7.1 %collective-permute-start.4 = (f32[8,4,128]{2,1,0:T(4,128)S(1)}, f32[8,4,128]{2,1,0:T(4,128)S(1)}, u32[]{:S(2)}, u32[]{:S(2)}) collective-permute-start(f32[8,4,128]{2,1,0:T(4,128)S(1)} %get-tuple-element.41), channel_id=1, source_target_pairs={{32,64},{64,32},{96,128},{128,96},{160,192},{192,160},{224,256},{2... | collective-permute-start | bytes 49160 | tf_op jit(solution)/shard_map/ppermute | solution.py:273
  48.1 12.4 %early.3 = (f32[64,4,128]{2,1,0:T(4,128)S(1)}, f32[64,4,128]{2,1,0:T(4,128)S(1)}) custom-call(s32[8,64]{1,0:T(8,128)S(1)} %copy-done, s32[1]{0:T(128)S(6)} %copy.71.count, f32[64,4,128]{2,1,0:T(4,128)S(1)} %maximum_bitcast_fusion.own, f32[64,4,128]{2,1,0:T(4,128)S(1)} %get-tuple-element.65.speeds, ...), custom_call_target="tpu_custom_call", output_to_operand_aliasing={{0}: (2, {}), {1}: (3, {})} | custom-call | flops 1258291200 | bytes 1048576 | tf_op jit(solution)/shard_map/early/pallas_call | solution.py:254
  60.6 1.9 %collective-permute-start.7 = (f32[24,4,128]{2,1,0:T(4,128)S(1)}, f32[24,4,128]{2,1,0:T(4,128)S(1)}, u32[]{:S(2)}, u32[]{:S(2)}) collective-permute-start(f32[24,4,128]{2,1,0:T(4,128)S(1)} %constant_dynamic-update-slice_fusion.middle), channel_id=1, source_target_pairs={{0,1},{1,0},{2,3},{3,2},{4,5},{5,4},{6,7},{7,6},{8,9},{9,8},{10,11... | collective-permute-start | bytes 147464 | tf_op jit(solution)/shard_map/ppermute | solution.py:273
  62.5 2.2 %collective-permute-start.6 = (f32[24,4,128]{2,1,0:T(4,128)S(1)}, f32[24,4,128]{2,1,0:T(4,128)S(1)}, u32[]{:S(2)}, u32[]{:S(2)}) collective-permute-start(f32[24,4,128]{2,1,0:T(4,128)S(1)} %constant_dynamic-update-slice_fusion.middle), channel_id=1, source_target_pairs={{1,2},{2,1},{3,4},{4,3},{5,6},{6,5},{7,8},{8,7},{9,10},{10,9},{11,... | collective-permute-start | bytes 147464 | tf_op jit(solution)/shard_map/ppermute | solution.py:273
  64.7 13.7 %late.3 = (f32[64,4,128]{2,1,0:T(4,128)S(1)}, f32[64,4,128]{2,1,0:T(4,128)S(1)}, bf16[136,128,128]{2,1,0:T(8,128)(2,1)S(1)}, bf16[136,16,128]{2,1,0:T(8,128)(2,1)S(1)}) custom-call(s32[8,64]{1,0:T(8,128)S(1)} %copy-done, s32[1]{0:T(128)S(6)} %copy.71.count, ...), custom_call_target="tpu_custom_call", output_to_operand_aliasing={{0}: (2, {}), {1}: (3, {}), {2}: (5, {}), {3}: (6, {})} | custom-call | flops 1258291200 | bytes 1048576 | tf_op jit(solution)/shard_map/late/pallas_call | solution.py:254
  78.4 4.4 %ghost.4 = (bf16[136,128,128]{2,1,0:T(8,128)(2,1)S(1)}, bf16[136,16,128]{2,1,0:T(8,128)(2,1)S(1)}, f32[8,4,128]{2,1,0:T(4,128)S(1)}) custom-call(s32[8,64]{1,0:T(8,128)S(1)} %copy-done, s32[8]{0:T(128)S(1)} %copy-done.2, s32[2]{0:T(128)S(1)} %and_select_fusion.parity, ...), custom_call_target="tpu_custom_call", output_to_operand_aliasing={{0}: (9, {}), {1}: (10, {})} | custom-call | flops 314572800 | bytes 1048576 | tf_op jit(solution)/shard_map/ghost/pallas_call | solution.py:254
  82.8 1.9 %collective-permute-start.9 = (f32[8,4,128]{2,1,0:T(4,128)S(1)}, f32[8,4,128]{2,1,0:T(4,128)S(1)}, u32[]{:S(2)}, u32[]{:S(2)}) collective-permute-start(f32[8,4,128]{2,1,0:T(4,128)S(1)} %get-tuple-element.50), channel_id=1, source_target_pairs={{0,32},{32,0},{64,96},{96,64},{128,160},{160,128},{192,224},{224,1... | collective-permute-start | bytes 49160 | tf_op jit(solution)/shard_map/ppermute | solution.py:273
  84.7 5.9 %collective-permute-start.8 = (f32[8,4,128]{2,1,0:T(4,128)S(1)}, f32[8,4,128]{2,1,0:T(4,128)S(1)}, u32[]{:S(2)}, u32[]{:S(2)}) collective-permute-start(f32[8,4,128]{2,1,0:T(4,128)S(1)} %get-tuple-element.50), channel_id=1, source_target_pairs={{32,64},{64,32},{96,128},{128,96},{160,192},{192,160},{224,256},{2... | collective-permute-start | bytes 49160 | tf_op jit(solution)/shard_map/ppermute | solution.py:273
  90.6 12.4 %early.4 = (f32[64,4,128]{2,1,0:T(4,128)S(1)}, f32[64,4,128]{2,1,0:T(4,128)S(1)}) custom-call(s32[8,64]{1,0:T(8,128)S(1)} %copy-done, s32[1]{0:T(128)S(6)} %copy.71.count, f32[64,4,128]{2,1,0:T(4,128)S(1)} %get-tuple-element.39.own, f32[64,4,128]{2,1,0:T(4,128)S(1)} %get-tuple-element.40.speeds, ...), custom_call_target="tpu_custom_call", output_to_operand_aliasing={{0}: (2, {}), {1}: (3, {})} | custom-call | flops 1258291200 | bytes 1048576 | tf_op jit(solution)/shard_map/early/pallas_call | solution.py:254
  103.0 1.9 %collective-permute-start.11 = (f32[24,4,128]{2,1,0:T(4,128)S(1)}, f32[24,4,128]{2,1,0:T(4,128)S(1)}, u32[]{:S(2)}, u32[]{:S(2)}) collective-permute-start(f32[24,4,128]{2,1,0:T(4,128)S(1)} %constant_dynamic-update-slice_fusion.3.middle), channel_id=1, source_target_pairs={{0,1},{1,0},{2,3},{3,2},{4,5},{5,4},{6,7},{7,6},{8,9},{9,8},{10,11... | collective-permute-start | bytes 147464 | tf_op jit(solution)/shard_map/ppermute | solution.py:273
  105.0 1.9 %collective-permute-start.10 = (f32[24,4,128]{2,1,0:T(4,128)S(1)}, f32[24,4,128]{2,1,0:T(4,128)S(1)}, u32[]{:S(2)}, u32[]{:S(2)}) collective-permute-start(f32[24,4,128]{2,1,0:T(4,128)S(1)} %constant_dynamic-update-slice_fusion.3.middle), channel_id=1, source_target_pairs={{1,2},{2,1},{3,4},{4,3},{5,6},{6,5},{7,8},{8,7},{9,10},{10,9},{11,... | collective-permute-start | bytes 147464 | tf_op jit(solution)/shard_map/ppermute | solution.py:273
  106.9 13.7 %late.4 = (f32[64,4,128]{2,1,0:T(4,128)S(1)}, f32[64,4,128]{2,1,0:T(4,128)S(1)}, bf16[136,128,128]{2,1,0:T(8,128)(2,1)S(1)}, bf16[136,16,128]{2,1,0:T(8,128)(2,1)S(1)}) custom-call(s32[8,64]{1,0:T(8,128)S(1)} %copy-done, s32[1]{0:T(128)S(6)} %copy.71.count, ...), custom_call_target="tpu_custom_call", output_to_operand_aliasing={{0}: (2, {}), {1}: (3, {}), {2}: (5, {}), {3}: (6, {})} | custom-call | flops 1258291200 | bytes 1048576 | tf_op jit(solution)/shard_map/late/pallas_call | solution.py:254
  120.6 4.4 %ghost.5 = (bf16[136,128,128]{2,1,0:T(8,128)(2,1)S(1)}, bf16[136,16,128]{2,1,0:T(8,128)(2,1)S(1)}, f32[8,4,128]{2,1,0:T(4,128)S(1)}) custom-call(s32[8,64]{1,0:T(8,128)S(1)} %copy-done, s32[8]{0:T(128)S(1)} %copy-done.2, s32[2]{0:T(128)S(1)} %and_select_fusion.parity, ...), custom_call_target="tpu_custom_call", output_to_operand_aliasing={{0}: (9, {}), {1}: (10, {})} | custom-call | flops 314572800 | bytes 1048576 | tf_op jit(solution)/shard_map/ghost/pallas_call | solution.py:254
  125.0 1.9 %collective-permute-start.13 = (f32[8,4,128]{2,1,0:T(4,128)S(1)}, f32[8,4,128]{2,1,0:T(4,128)S(1)}, u32[]{:S(2)}, u32[]{:S(2)}) collective-permute-start(f32[8,4,128]{2,1,0:T(4,128)S(1)} %get-tuple-element.59), channel_id=1, source_target_pairs={{0,32},{32,0},{64,96},{96,64},{128,160},{160,128},{192,224},{224,1... | collective-permute-start | bytes 49160 | tf_op jit(solution)/shard_map/ppermute | solution.py:273
  126.9 1.9 %collective-permute-start.12 = (f32[8,4,128]{2,1,0:T(4,128)S(1)}, f32[8,4,128]{2,1,0:T(4,128)S(1)}, u32[]{:S(2)}, u32[]{:S(2)}) collective-permute-start(f32[8,4,128]{2,1,0:T(4,128)S(1)} %get-tuple-element.59), channel_id=1, source_target_pairs={{32,64},{64,32},{96,128},{128,96},{160,192},{192,160},{224,256},{2... | collective-permute-start | bytes 49160 | tf_op jit(solution)/shard_map/ppermute | solution.py:273
  128.8 12.6 %early.5 = (f32[64,4,128]{2,1,0:T(4,128)S(1)}, f32[64,4,128]{2,1,0:T(4,128)S(1)}) custom-call(s32[8,64]{1,0:T(8,128)S(1)} %copy-done, s32[1]{0:T(128)S(6)} %copy.71.count, f32[64,4,128]{2,1,0:T(4,128)S(1)} %get-tuple-element.48.own, f32[64,4,128]{2,1,0:T(4,128)S(1)} %get-tuple-element.49.speeds, ...), custom_call_target="tpu_custom_call", output_to_operand_aliasing={{0}: (2, {}), {1}: (3, {})} | custom-call | flops 1258291200 | bytes 1048576 | tf_op jit(solution)/shard_map/early/pallas_call | solution.py:254
  141.5 1.9 %collective-permute-start.15 = (f32[24,4,128]{2,1,0:T(4,128)S(1)}, f32[24,4,128]{2,1,0:T(4,128)S(1)}, u32[]{:S(2)}, u32[]{:S(2)}) collective-permute-start(f32[24,4,128]{2,1,0:T(4,128)S(1)} %constant_dynamic-update-slice_fusion.6.middle), channel_id=1, source_target_pairs={{0,1},{1,0},{2,3},{3,2},{4,5},{5,4},{6,7},{7,6},{8,9},{9,8},{10,11... | collective-permute-start | bytes 147464 | tf_op jit(solution)/shard_map/ppermute | solution.py:273
  143.4 1.9 %collective-permute-start.14 = (f32[24,4,128]{2,1,0:T(4,128)S(1)}, f32[24,4,128]{2,1,0:T(4,128)S(1)}, u32[]{:S(2)}, u32[]{:S(2)}) collective-permute-start(f32[24,4,128]{2,1,0:T(4,128)S(1)} %constant_dynamic-update-slice_fusion.6.middle), channel_id=1, source_target_pairs={{1,2},{2,1},{3,4},{4,3},{5,6},{6,5},{7,8},{8,7},{9,10},{10,9},{11,... | collective-permute-start | bytes 147464 | tf_op jit(solution)/shard_map/ppermute | solution.py:273
  145.3 13.7 %late.5 = (f32[64,4,128]{2,1,0:T(4,128)S(1)}, f32[64,4,128]{2,1,0:T(4,128)S(1)}, bf16[136,128,128]{2,1,0:T(8,128)(2,1)S(1)}, bf16[136,16,128]{2,1,0:T(8,128)(2,1)S(1)}) custom-call(s32[8,64]{1,0:T(8,128)S(1)} %copy-done, s32[1]{0:T(128)S(6)} %copy.71.count, ...), custom_call_target="tpu_custom_call", output_to_operand_aliasing={{0}: (2, {}), {1}: (3, {}), {2}: (5, {}), {3}: (6, {})} | custom-call | flops 1258291200 | bytes 1048576 | tf_op jit(solution)/shard_map/late/pallas_call | solution.py:254
  159.0 24.9 %last.1 = (f32[64,4,128]{2,1,0:T(4,128)S(1)}, f32[64,4,128]{2,1,0:T(4,128)S(1)}, bf16[136,128,128]{2,1,0:T(8,128)(2,1)S(1)}, bf16[136,16,128]{2,1,0:T(8,128)(2,1)S(1)}) custom-call(s32[8,64]{1,0:T(8,128)S(1)} %copy-done, s32[2]{0:T(128)S(1)} %and_select_fusion.parity, ...), custom_call_target="tpu_custom_call", output_to_operand_aliasing={{0}: (3, {}), {1}: (4, {}), {2}: (9, {}), {3}: (10, {})} | custom-call | flops 2516582400 | bytes 1048576 | tf_op jit(solution)/shard_map/last/pallas_call | solution.py:254
  (33 shorter events, 3.4 us)
Async XLA Ops:
  1.6 0.7 copy-start.1
  2.8 9.7 %collective-permute-start.1 = (f32[8,4,128]{2,1,0:T(4,128)S(1)}, f32[8,4,128]{2,1,0:T(4,128)S(1)}, u32[]{:S(2)}, u32[]{:S(2)}) collective-permute-start(f32[8,4,128]{2,1,0:T(4,128)S(1)} %choose.1), channel_id=1, source_target_pairs={{0,32},{32,0},{64,96},{96,64},{128,160},{160,128},{192,224},{224,1... | collective-permute-start | bytes 49160 | tf_op jit(solution)/shard_map/ppermute | solution.py:273
  4.8 12.5 %collective-permute-start = (f32[8,4,128]{2,1,0:T(4,128)S(1)}, f32[8,4,128]{2,1,0:T(4,128)S(1)}, u32[]{:S(2)}, u32[]{:S(2)}) collective-permute-start(f32[8,4,128]{2,1,0:T(4,128)S(1)} %choose.1), channel_id=1, source_target_pairs={{32,64},{64,32},{96,128},{128,96},{160,192},{192,160},{224,256},{2... | collective-permute-start | bytes 49160 | tf_op jit(solution)/shard_map/ppermute | solution.py:273
  17.3 14.6 %collective-permute-start.3 = (f32[24,4,128]{2,1,0:T(4,128)S(1)}, f32[24,4,128]{2,1,0:T(4,128)S(1)}, u32[]{:S(2)}, u32[]{:S(2)}) collective-permute-start(f32[24,4,128]{2,1,0:T(4,128)S(1)} %pad_maximum_fusion.middle), channel_id=1, source_target_pairs={{0,1},{1,0},{2,3},{3,2},{4,5},{5,4},{6,7},{7,6},{8,9},{9,8},{10,11... | collective-permute-start | bytes 147464 | tf_op jit(solution)/shard_map/ppermute | solution.py:273
  19.3 14.1 %collective-permute-start.2 = (f32[24,4,128]{2,1,0:T(4,128)S(1)}, f32[24,4,128]{2,1,0:T(4,128)S(1)}, u32[]{:S(2)}, u32[]{:S(2)}) collective-permute-start(f32[24,4,128]{2,1,0:T(4,128)S(1)} %pad_maximum_fusion.middle), channel_id=1, source_target_pairs={{1,2},{2,1},{3,4},{4,3},{5,6},{6,5},{7,8},{8,7},{9,10},{10,9},{11,... | collective-permute-start | bytes 147464 | tf_op jit(solution)/shard_map/ppermute | solution.py:273
  33.4 0.7 copy-start
  34.1 0.7 copy-start.2
  39.1 21.5 %collective-permute-start.5 = (f32[8,4,128]{2,1,0:T(4,128)S(1)}, f32[8,4,128]{2,1,0:T(4,128)S(1)}, u32[]{:S(2)}, u32[]{:S(2)}) collective-permute-start(f32[8,4,128]{2,1,0:T(4,128)S(1)} %get-tuple-element.41), channel_id=1, source_target_pairs={{0,32},{32,0},{64,96},{96,64},{128,160},{160,128},{192,224},{224,1... | collective-permute-start | bytes 49160 | tf_op jit(solution)/shard_map/ppermute | solution.py:273
  41.0 19.5 %collective-permute-start.4 = (f32[8,4,128]{2,1,0:T(4,128)S(1)}, f32[8,4,128]{2,1,0:T(4,128)S(1)}, u32[]{:S(2)}, u32[]{:S(2)}) collective-permute-start(f32[8,4,128]{2,1,0:T(4,128)S(1)} %get-tuple-element.41), channel_id=1, source_target_pairs={{32,64},{64,32},{96,128},{128,96},{160,192},{192,160},{224,256},{2... | collective-permute-start | bytes 49160 | tf_op jit(solution)/shard_map/ppermute | solution.py:273
  60.6 17.8 %collective-permute-start.7 = (f32[24,4,128]{2,1,0:T(4,128)S(1)}, f32[24,4,128]{2,1,0:T(4,128)S(1)}, u32[]{:S(2)}, u32[]{:S(2)}) collective-permute-start(f32[24,4,128]{2,1,0:T(4,128)S(1)} %constant_dynamic-update-slice_fusion.middle), channel_id=1, source_target_pairs={{0,1},{1,0},{2,3},{3,2},{4,5},{5,4},{6,7},{7,6},{8,9},{9,8},{10,11... | collective-permute-start | bytes 147464 | tf_op jit(solution)/shard_map/ppermute | solution.py:273
  62.5 15.9 %collective-permute-start.6 = (f32[24,4,128]{2,1,0:T(4,128)S(1)}, f32[24,4,128]{2,1,0:T(4,128)S(1)}, u32[]{:S(2)}, u32[]{:S(2)}) collective-permute-start(f32[24,4,128]{2,1,0:T(4,128)S(1)} %constant_dynamic-update-slice_fusion.middle), channel_id=1, source_target_pairs={{1,2},{2,1},{3,4},{4,3},{5,6},{6,5},{7,8},{8,7},{9,10},{10,9},{11,... | collective-permute-start | bytes 147464 | tf_op jit(solution)/shard_map/ppermute | solution.py:273
  82.8 20.2 %collective-permute-start.9 = (f32[8,4,128]{2,1,0:T(4,128)S(1)}, f32[8,4,128]{2,1,0:T(4,128)S(1)}, u32[]{:S(2)}, u32[]{:S(2)}) collective-permute-start(f32[8,4,128]{2,1,0:T(4,128)S(1)} %get-tuple-element.50), channel_id=1, source_target_pairs={{0,32},{32,0},{64,96},{96,64},{128,160},{160,128},{192,224},{224,1... | collective-permute-start | bytes 49160 | tf_op jit(solution)/shard_map/ppermute | solution.py:273
  84.7 18.3 %collective-permute-start.8 = (f32[8,4,128]{2,1,0:T(4,128)S(1)}, f32[8,4,128]{2,1,0:T(4,128)S(1)}, u32[]{:S(2)}, u32[]{:S(2)}) collective-permute-start(f32[8,4,128]{2,1,0:T(4,128)S(1)} %get-tuple-element.50), channel_id=1, source_target_pairs={{32,64},{64,32},{96,128},{128,96},{160,192},{192,160},{224,256},{2... | collective-permute-start | bytes 49160 | tf_op jit(solution)/shard_map/ppermute | solution.py:273
  103.0 17.5 %collective-permute-start.11 = (f32[24,4,128]{2,1,0:T(4,128)S(1)}, f32[24,4,128]{2,1,0:T(4,128)S(1)}, u32[]{:S(2)}, u32[]{:S(2)}) collective-permute-start(f32[24,4,128]{2,1,0:T(4,128)S(1)} %constant_dynamic-update-slice_fusion.3.middle), channel_id=1, source_target_pairs={{0,1},{1,0},{2,3},{3,2},{4,5},{5,4},{6,7},{7,6},{8,9},{9,8},{10,11... | collective-permute-start | bytes 147464 | tf_op jit(solution)/shard_map/ppermute | solution.py:273
  105.0 15.6 %collective-permute-start.10 = (f32[24,4,128]{2,1,0:T(4,128)S(1)}, f32[24,4,128]{2,1,0:T(4,128)S(1)}, u32[]{:S(2)}, u32[]{:S(2)}) collective-permute-start(f32[24,4,128]{2,1,0:T(4,128)S(1)} %constant_dynamic-update-slice_fusion.3.middle), channel_id=1, source_target_pairs={{1,2},{2,1},{3,4},{4,3},{5,6},{6,5},{7,8},{8,7},{9,10},{10,9},{11,... | collective-permute-start | bytes 147464 | tf_op jit(solution)/shard_map/ppermute | solution.py:273
  125.0 16.5 %collective-permute-start.13 = (f32[8,4,128]{2,1,0:T(4,128)S(1)}, f32[8,4,128]{2,1,0:T(4,128)S(1)}, u32[]{:S(2)}, u32[]{:S(2)}) collective-permute-start(f32[8,4,128]{2,1,0:T(4,128)S(1)} %get-tuple-element.59), channel_id=1, source_target_pairs={{0,32},{32,0},{64,96},{96,64},{128,160},{160,128},{192,224},{224,1... | collective-permute-start | bytes 49160 | tf_op jit(solution)/shard_map/ppermute | solution.py:273
  126.9 14.5 %collective-permute-start.12 = (f32[8,4,128]{2,1,0:T(4,128)S(1)}, f32[8,4,128]{2,1,0:T(4,128)S(1)}, u32[]{:S(2)}, u32[]{:S(2)}) collective-permute-start(f32[8,4,128]{2,1,0:T(4,128)S(1)} %get-tuple-element.59), channel_id=1, source_target_pairs={{32,64},{64,32},{96,128},{128,96},{160,192},{192,160},{224,256},{2... | collective-permute-start | bytes 49160 | tf_op jit(solution)/shard_map/ppermute | solution.py:273
  141.5 17.5 %collective-permute-start.15 = (f32[24,4,128]{2,1,0:T(4,128)S(1)}, f32[24,4,128]{2,1,0:T(4,128)S(1)}, u32[]{:S(2)}, u32[]{:S(2)}) collective-permute-start(f32[24,4,128]{2,1,0:T(4,128)S(1)} %constant_dynamic-update-slice_fusion.6.middle), channel_id=1, source_target_pairs={{0,1},{1,0},{2,3},{3,2},{4,5},{5,4},{6,7},{7,6},{8,9},{9,8},{10,11... | collective-permute-start | bytes 147464 | tf_op jit(solution)/shard_map/ppermute | solution.py:273
  143.4 15.6 %collective-permute-start.14 = (f32[24,4,128]{2,1,0:T(4,128)S(1)}, f32[24,4,128]{2,1,0:T(4,128)S(1)}, u32[]{:S(2)}, u32[]{:S(2)}) collective-permute-start(f32[24,4,128]{2,1,0:T(4,128)S(1)} %constant_dynamic-update-slice_fusion.6.middle), channel_id=1, source_target_pairs={{1,2},{2,1},{3,4},{4,3},{5,6},{6,5},{7,8},{8,7},{9,10},{10,9},{11,... | collective-permute-start | bytes 147464 | tf_op jit(solution)/shard_map/ppermute | solution.py:273

commit v2 on v1

--- a/solution.py
+++ b/solution.py
@@ -13,7 +13,7 @@
 POOL = LEAVES + 9 * GHOSTS
 FEATURES = 32
 SUMS = 16
-GROUP = 4
+GROUP = 8
 UNROLL = 8
 
 soften_sq = 0.04
@@ -114,27 +114,28 @@
         ],
         axis=0,
     )
-    total = jnp.zeros((2 * SUMS, 2 * LEAF), f32)
-    for n in range(NEIGHBOURS):
-        slots = [lists[n, leaf] for leaf in leaves]
-        apart = jnp.dot(
-            jnp.concatenate([sources[s] for s in slots], axis=1),
-            targets,
-            preferred_element_type=f32,
-        )
-        near = jnp.maximum(apart, soften_sq)
+    slots = [[lists[n, leaf] for leaf in leaves] for n in range(NEIGHBOURS)]
+    apart = jnp.dot(
+        jnp.concatenate([jnp.concatenate([sources[s] for s in pair], axis=1) for pair in slots], axis=0),
+        targets,
+        preferred_element_type=f32,
+    )
+    weights, rows = [], []
+    for n, pair in enumerate(slots):
+        near = jnp.maximum(apart[n * LEAF : (n + 1) * LEAF], soften_sq)
         taper = jnp.maximum(cutoff_sq + soften_sq - near, 0.0)
         inverse = lax.rsqrt(near)
         product = taper * inverse
         weight = product * product * inverse
         high = weight.astype(bf16)
         low = (weight - high.astype(f32)).astype(bf16)
-        rows = jnp.concatenate([moments[s] for s in slots], axis=0)
-        total += jnp.dot(
-            jnp.concatenate([rows, rows], axis=1),
-            jnp.concatenate([high, low], axis=0),
-            preferred_element_type=f32,
-        )
+        weights += [high, low]
+        rows += [jnp.concatenate([moments[s] for s in pair], axis=0)] * 2
+    total = jnp.dot(
+        jnp.concatenate(rows, axis=1),
+        jnp.concatenate(weights, axis=0),
+        preferred_element_type=f32,
+    )
     return total[:SUMS, :LEAF], total[SUMS:, LEAF:]
 
 
@@ -170,13 +171,33 @@
     lax.fori_loop(begin, end, group, 0)
 
 
-def choose_kernel(ids, own, chosen):
+def lanes(leaf):
+    return pl.ds(pl.multiple_of(leaf * LEAF, LEAF), LEAF)
+
+
+def first_record(positions, masses, leaf):
+    return jnp.concatenate([positions[:, lanes(leaf)], masses[:, lanes(leaf)]], axis=0)
+
+
+def choose_kernel(ids, positions, masses, chosen):
     for g in range(GHOSTS):
-        chosen[g] = own[ids[g]]
-
-
-def open_kernel(own, sources, moments):
-    enter_all(sources, moments, own, lambda leaf: leaf, LEAVES)
+        chosen[g] = first_record(positions, masses, ids[g])
+
+
+def open_kernel(positions, velocities, masses, long_kick, own, speeds, kicks, sources, moments):
+    blank = jnp.zeros((1, LEAF), f32)
+
+    def some(index, carry):
+        for u in range(UNROLL):
+            leaf = index * UNROLL + u
+            record = first_record(positions, masses, leaf)
+            own[leaf] = record
+            speeds[leaf] = jnp.concatenate([velocities[:, lanes(leaf)], blank], axis=0)
+            kicks[leaf] = jnp.concatenate([long_kick[:, lanes(leaf)], blank], axis=0)
+            enter(sources, moments, leaf, record)
+        return carry
+
+    lax.fori_loop(0, LEAVES // UNROLL, some, 0)
 
 
 def enter_ghosts(parity, sides, sources, moments):
@@ -194,15 +215,11 @@
 ):
     enter_ghosts(parity, (far, middle, near), sources, moments)
 
-    def group(index, carry):
-        places = [index * GROUP + u for u in range(GROUP)]
-        leaves = [ids[g] for g in places]
-        results = group_moved(lists, sources, moments, own, speeds, kicks, leaves)
-        for g, (record, _) in zip(places, results):
-            chosen[g] = record
-        return carry
-
-    lax.fori_loop(0, GHOSTS // GROUP, group, 0)
+    results = group_moved(
+        lists, sources, moments, own, speeds, kicks, [ids[g] for g in range(GHOSTS)]
+    )
+    for g, (record, _) in enumerate(results):
+        chosen[g] = record
 
 
 def groups_of(count):
@@ -232,18 +249,33 @@
 
 def last_kernel(
     lists, parity, count, own, speeds, kicks, far, middle, near, old_sources, old_moments,
-    new_own, new_speeds, sources, moments,
+    places, paces, sources, moments,
 ):
     enter_ghosts(parity, (far, middle, near), sources, moments)
-    move_groups(
-        lists, count, sources, moments, own, speeds, kicks, new_own, new_speeds,
-        0, groups_of(count),
-    )
+
+    def group(index, carry):
+        leaves = [index * GROUP + u for u in range(GROUP)]
+        results = group_moved(lists, sources, moments, own, speeds, kicks, leaves)
+        for leaf, (record, speed) in zip(leaves, results):
+            live = leaf < count[0]
+            places[:, lanes(leaf)] = jnp.where(live, record, own[leaf])[:3]
+            paces[:, lanes(leaf)] = jnp.where(live, speed, speeds[leaf])[:3]
+        return carry
+
+    def keep(leaf, carry):
+        places[:, lanes(leaf)] = own[leaf][:3]
+        paces[:, lanes(leaf)] = speeds[leaf][:3]
+        return carry
+
+    groups = groups_of(count)
+    lax.fori_loop(0, groups, group, 0)
+    lax.fori_loop(groups * GROUP, LEAVES, keep, 0)
 
 
 VMEM = pl.BlockSpec(memory_space=pltpu.VMEM)
 SMEM = pl.BlockSpec(memory_space=pltpu.SMEM)
 record_shape = jax.ShapeDtypeStruct((LEAVES, 4, LEAF), f32)
+whole_shape = jax.ShapeDtypeStruct((3, LEAVES * LEAF), f32)
 chosen_shape = jax.ShapeDtypeStruct((GHOSTS, 4, LEAF), f32)
 sources_shape = jax.ShapeDtypeStruct((POOL, LEAF, LEAF), bf16)
 moments_shape = jax.ShapeDtypeStruct((POOL, SUMS, LEAF), bf16)
@@ -274,18 +306,15 @@
 
 
 def body(positions, velocities, masses, long_kick, leaf_lists, ghost_ids, leaf_counts):
-    def records(parts):
-        return jnp.swapaxes(parts.reshape(-1, LEAVES, LEAF), 0, 1)
-
-    blank = jnp.zeros((1, LEAVES * LEAF), f32)
-    own = records(jnp.concatenate([positions, masses[None]], axis=0))
-    speeds = records(jnp.concatenate([velocities, blank], axis=0))
-    kicks = records(jnp.concatenate([long_kick, blank], axis=0))
     parity = jnp.stack([lax.axis_index("gx"), lax.axis_index("gy")]).astype(jnp.int32) % 2
     lists, ids, count = leaf_lists, ghost_ids, leaf_counts
 
-    chosen = call(choose_kernel, "choose", (ids,), (own,), chosen_shape)
-    sources, moments = call(open_kernel, "open", (), (own,), (sources_shape, moments_shape))
+    masses = masses[None]
+    chosen = call(choose_kernel, "choose", (ids,), (positions, masses), chosen_shape)
+    own, speeds, kicks, sources, moments = call(
+        open_kernel, "open", (), (positions, velocities, masses, long_kick),
+        (record_shape,) * 3 + (sources_shape, moments_shape),
+    )
     for subcycle in range(SUBCYCLES):
         far = swapped(chosen, "gx", 1)
         near = swapped(chosen, "gx", 0)
@@ -310,17 +339,13 @@
                 (sources_shape, moments_shape, chosen_shape), {6: 0, 7: 1}, GHOSTS,
             )
         else:
-            own, speeds, _, _ = call(
+            places, paces, _, _ = call(
                 last_kernel, "last", (lists, parity, count),
                 (own, speeds, kicks, far, middle, near, sources, moments),
-                (record_shape, record_shape, sources_shape, moments_shape),
-                {0: 0, 1: 1, 6: 2, 7: 3}, LEAVES,
+                (whole_shape, whole_shape, sources_shape, moments_shape),
+                {6: 2, 7: 3}, LEAVES,
             )
-
-    def whole(parts):
-        return jnp.swapaxes(parts[:, :3], 0, 1).reshape(3, -1)
-
-    return whole(own), whole(speeds)
+    return places, paces
 
 
 def solution(mesh):

time: 186 us -> 165 us (0.89)
  the two profiles are of different devices: /device:TPU:0 before, /device:TPU:8 now
where the time goes in v2:
time: 165 us; the launch traced here: 164 us
  Pallas kernels  76.8 us (47%)
  starting transfers between devices  73 us (44%)
  local copies, waits for them, and re-layouts  7.18 us (4%)
  waiting for transfers between devices  5.46 us (3%)
  between operations  1.66 us (1%)
    pallas_call x12, Pallas kernels, call(): pl.pallas_call(kernel, out_shape=outs, in_specs=[SMEM] * len(scalars) + [...  76.8 us
    ppermute x16, starting transfers between devices, swapped(): return lax.ppermute(block, axis, route)  73 us
    unnamed x26, local copies, waits for them, and re-layouts  7.15 us
    ppermute x16, waiting for transfers between devices, swapped(): return lax.ppermute(block, axis, route)  5.46 us
  transfers between devices with their start and end apart: 16, of which 3 were waited for; matrix products, arithmetic and copies ran while one was open for 0% of the time, Pallas kernels for 31%

profile of v2, /device:TPU:8, one launch (start us, length us, event | category | flops | bytes accessed | tf_op | source)
XLA Modules:
  0.0 164.1 jit_solution(15823850600206137131)
XLA Ops:
  3.5 3.4 %collective-permute-start.1 = (f32[8,4,128]{2,1,0:T(4,128)S(1)}, f32[8,4,128]{2,1,0:T(4,128)S(1)}, u32[]{:S(2)}, u32[]{:S(2)}) collective-permute-start(f32[8,4,128]{2,1,0:T(4,128)S(1)} %choose.1), channel_id=1, source_target_pairs={{0,32},{32,0},{64,96},{96,64},{128,160},{160,128},{192,224},{224,1... | collective-permute-start | bytes 49160 | tf_op jit(solution)/shard_map/ppermute | solution.py:305
  6.9 14.3 %collective-permute-start = (f32[8,4,128]{2,1,0:T(4,128)S(1)}, f32[8,4,128]{2,1,0:T(4,128)S(1)}, u32[]{:S(2)}, u32[]{:S(2)}) collective-permute-start(f32[8,4,128]{2,1,0:T(4,128)S(1)} %choose.1), channel_id=1, source_target_pairs={{32,64},{64,32},{96,128},{128,96},{160,192},{192,160},{224,256},{2... | collective-permute-start | bytes 49160 | tf_op jit(solution)/shard_map/ppermute | solution.py:305
  21.2 1.7 %collective-permute-done = f32[8,4,128]{2,1,0:T(4,128)S(1)} collective-permute-done((f32[8,4,128]{2,1,0:T(4,128)S(1)}, f32[8,4,128]{2,1,0:T(4,128)S(1)}, u32[]{:S(2)}, u32[]{:S(2)}) %collective-permute-start) | collective-permute-done | bytes 16416 | tf_op jit(solution)/shard_map/ppermute | solution.py:305
  22.9 1.9 %collective-permute-start.3 = (f32[24,4,128]{2,1,0:T(4,128)S(1)}, f32[24,4,128]{2,1,0:T(4,128)S(1)}, u32[]{:S(2)}, u32[]{:S(2)}) collective-permute-start(f32[24,4,128]{2,1,0:T(4,128)S(1)} %pad_maximum_fusion.middle), channel_id=1, source_target_pairs={{0,1},{1,0},{2,3},{3,2},{4,5},{5,4},{6,7},{7,6},{8,9},{9,8},{10,11... | collective-permute-start | bytes 147464 | tf_op jit(solution)/shard_map/ppermute | solution.py:305
  24.8 6.6 %collective-permute-start.2 = (f32[24,4,128]{2,1,0:T(4,128)S(1)}, f32[24,4,128]{2,1,0:T(4,128)S(1)}, u32[]{:S(2)}, u32[]{:S(2)}) collective-permute-start(f32[24,4,128]{2,1,0:T(4,128)S(1)} %pad_maximum_fusion.middle), channel_id=1, source_target_pairs={{1,2},{2,1},{3,4},{4,3},{5,6},{6,5},{7,8},{8,7},{9,10},{10,9},{11,... | collective-permute-start | bytes 147464 | tf_op jit(solution)/shard_map/ppermute | solution.py:305
  33.1 0.9 copy-done.2
  34.0 0.9 copy-done.3
  35.6 1.3 open.1
  38.3 3.1 %ghost.3 = (bf16[136,128,128]{2,1,0:T(8,128)(2,1)S(1)}, bf16[136,16,128]{2,1,0:T(8,128)(2,1)S(1)}, f32[8,4,128]{2,1,0:T(4,128)S(1)}) custom-call(s32[8,64]{1,0:T(8,128)S(1)} %copy-done.6, s32[8]{0:T(128)S(1)} %copy-done.9, s32[2]{0:T(128)S(1)} %and_select_fusion.parity, ...), custom_call_target="tpu_custom_call", output_to_operand_aliasing={{0}: (9, {}), {1}: (10, {})} | custom-call | flops 314572800 | bytes 1048576 | tf_op jit(solution)/shard_map/ghost/pallas_call | solution.py:286
  41.4 1.9 %collective-permute-start.5 = (f32[8,4,128]{2,1,0:T(4,128)S(1)}, f32[8,4,128]{2,1,0:T(4,128)S(1)}, u32[]{:S(2)}, u32[]{:S(2)}) collective-permute-start(f32[8,4,128]{2,1,0:T(4,128)S(1)} %get-tuple-element.47), channel_id=1, source_target_pairs={{0,32},{32,0},{64,96},{96,64},{128,160},{160,128},{192,224},{224,1... | collective-permute-start | bytes 49160 | tf_op jit(solution)/shard_map/ppermute | solution.py:305
  43.4 6.7 %collective-permute-start.4 = (f32[8,4,128]{2,1,0:T(4,128)S(1)}, f32[8,4,128]{2,1,0:T(4,128)S(1)}, u32[]{:S(2)}, u32[]{:S(2)}) collective-permute-start(f32[8,4,128]{2,1,0:T(4,128)S(1)} %get-tuple-element.47), channel_id=1, source_target_pairs={{32,64},{64,32},{96,128},{128,96},{160,192},{192,160},{224,256},{2... | collective-permute-start | bytes 49160 | tf_op jit(solution)/shard_map/ppermute | solution.py:305
  50.1 7.6 %early.3 = (f32[64,4,128]{2,1,0:T(4,128)S(1)}, f32[64,4,128]{2,1,0:T(4,128)S(1)}) custom-call(s32[8,64]{1,0:T(8,128)S(1)} %copy-done.6, s32[1]{0:T(128)S(6)} %copy.67.count, f32[64,4,128]{2,1,0:T(4,128)S(1)} %get-tuple-element.36.own, f32[64,4,128]{2,1,0:T(4,128)S(1)} %get-tuple-element.37.speeds, ...), custom_call_target="tpu_custom_call", output_to_operand_aliasing={{0}: (2, {}), {1}: (3, {})} | custom-call | flops 1258291200 | bytes 1048576 | tf_op jit(solution)/shard_map/early/pallas_call | solution.py:286
  57.7 1.9 %collective-permute-start.7 = (f32[24,4,128]{2,1,0:T(4,128)S(1)}, f32[24,4,128]{2,1,0:T(4,128)S(1)}, u32[]{:S(2)}, u32[]{:S(2)}) collective-permute-start(f32[24,4,128]{2,1,0:T(4,128)S(1)} %constant_dynamic-update-slice_fusion.middle), channel_id=1, source_target_pairs={{0,1},{1,0},{2,3},{3,2},{4,5},{5,4},{6,7},{7,6},{8,9},{9,8},{10,11... | collective-permute-start | bytes 147464 | tf_op jit(solution)/shard_map/ppermute | solution.py:305
  59.7 12.4 %collective-permute-start.6 = (f32[24,4,128]{2,1,0:T(4,128)S(1)}, f32[24,4,128]{2,1,0:T(4,128)S(1)}, u32[]{:S(2)}, u32[]{:S(2)}) collective-permute-start(f32[24,4,128]{2,1,0:T(4,128)S(1)} %constant_dynamic-update-slice_fusion.middle), channel_id=1, source_target_pairs={{1,2},{2,1},{3,4},{4,3},{5,6},{6,5},{7,8},{8,7},{9,10},{10,9},{11,... | collective-permute-start | bytes 147464 | tf_op jit(solution)/shard_map/ppermute | solution.py:305
  72.1 8.9 %late.3 = (f32[64,4,128]{2,1,0:T(4,128)S(1)}, f32[64,4,128]{2,1,0:T(4,128)S(1)}, bf16[136,128,128]{2,1,0:T(8,128)(2,1)S(1)}, bf16[136,16,128]{2,1,0:T(8,128)(2,1)S(1)}) custom-call(s32[8,64]{1,0:T(8,128)S(1)} %copy-done.6, s32[1]{0:T(128)S(6)} %copy.67.count, ...), custom_call_target="tpu_custom_call", output_to_operand_aliasing={{0}: (2, {}), {1}: (3, {}), {2}: (5, {}), {3}: (6, {})} | custom-call | flops 1258291200 | bytes 1048576 | tf_op jit(solution)/shard_map/late/pallas_call | solution.py:286
  81.0 3.1 %ghost.4 = (bf16[136,128,128]{2,1,0:T(8,128)(2,1)S(1)}, bf16[136,16,128]{2,1,0:T(8,128)(2,1)S(1)}, f32[8,4,128]{2,1,0:T(4,128)S(1)}) custom-call(s32[8,64]{1,0:T(8,128)S(1)} %copy-done.6, s32[8]{0:T(128)S(1)} %copy-done.9, s32[2]{0:T(128)S(1)} %and_select_fusion.parity, ...), custom_call_target="tpu_custom_call", output_to_operand_aliasing={{0}: (9, {}), {1}: (10, {})} | custom-call | flops 314572800 | bytes 1048576 | tf_op jit(solution)/shard_map/ghost/pallas_call | solution.py:286
  84.1 1.9 %collective-permute-start.9 = (f32[8,4,128]{2,1,0:T(4,128)S(1)}, f32[8,4,128]{2,1,0:T(4,128)S(1)}, u32[]{:S(2)}, u32[]{:S(2)}) collective-permute-start(f32[8,4,128]{2,1,0:T(4,128)S(1)} %get-tuple-element.56), channel_id=1, source_target_pairs={{0,32},{32,0},{64,96},{96,64},{128,160},{160,128},{192,224},{224,1... | collective-permute-start | bytes 49160 | tf_op jit(solution)/shard_map/ppermute | solution.py:305
  86.1 3.2 %collective-permute-start.8 = (f32[8,4,128]{2,1,0:T(4,128)S(1)}, f32[8,4,128]{2,1,0:T(4,128)S(1)}, u32[]{:S(2)}, u32[]{:S(2)}) collective-permute-start(f32[8,4,128]{2,1,0:T(4,128)S(1)} %get-tuple-element.56), channel_id=1, source_target_pairs={{32,64},{64,32},{96,128},{128,96},{160,192},{192,160},{224,256},{2... | collective-permute-start | bytes 49160 | tf_op jit(solution)/shard_map/ppermute | solution.py:305
  89.3 7.6 %early.4 = (f32[64,4,128]{2,1,0:T(4,128)S(1)}, f32[64,4,128]{2,1,0:T(4,128)S(1)}) custom-call(s32[8,64]{1,0:T(8,128)S(1)} %copy-done.6, s32[1]{0:T(128)S(6)} %copy.67.count, f32[64,4,128]{2,1,0:T(4,128)S(1)} %get-tuple-element.45.own, f32[64,4,128]{2,1,0:T(4,128)S(1)} %get-tuple-element.46.speeds, ...), custom_call_target="tpu_custom_call", output_to_operand_aliasing={{0}: (2, {}), {1}: (3, {})} | custom-call | flops 1258291200 | bytes 1048576 | tf_op jit(solution)/shard_map/early/pallas_call | solution.py:286
  96.8 1.8 %collective-permute-done.8 = f32[8,4,128]{2,1,0:T(4,128)S(1)} collective-permute-done((f32[8,4,128]{2,1,0:T(4,128)S(1)}, f32[8,4,128]{2,1,0:T(4,128)S(1)}, u32[]{:S(2)}, u32[]{:S(2)}) %collective-permute-start.8) | collective-permute-done | bytes 16416 | tf_op jit(solution)/shard_map/ppermute | solution.py:305
  98.6 1.9 %collective-permute-start.11 = (f32[24,4,128]{2,1,0:T(4,128)S(1)}, f32[24,4,128]{2,1,0:T(4,128)S(1)}, u32[]{:S(2)}, u32[]{:S(2)}) collective-permute-start(f32[24,4,128]{2,1,0:T(4,128)S(1)} %constant_dynamic-update-slice_fusion.3.middle), channel_id=1, source_target_pairs={{0,1},{1,0},{2,3},{3,2},{4,5},{5,4},{6,7},{7,6},{8,9},{9,8},{10,11... | collective-permute-start | bytes 147464 | tf_op jit(solution)/shard_map/ppermute | solution.py:305
  100.6 5.1 %collective-permute-start.10 = (f32[24,4,128]{2,1,0:T(4,128)S(1)}, f32[24,4,128]{2,1,0:T(4,128)S(1)}, u32[]{:S(2)}, u32[]{:S(2)}) collective-permute-start(f32[24,4,128]{2,1,0:T(4,128)S(1)} %constant_dynamic-update-slice_fusion.3.middle), channel_id=1, source_target_pairs={{1,2},{2,1},{3,4},{4,3},{5,6},{6,5},{7,8},{8,7},{9,10},{10,9},{11,... | collective-permute-start | bytes 147464 | tf_op jit(solution)/shard_map/ppermute | solution.py:305
  105.7 9.1 %late.4 = (f32[64,4,128]{2,1,0:T(4,128)S(1)}, f32[64,4,128]{2,1,0:T(4,128)S(1)}, bf16[136,128,128]{2,1,0:T(8,128)(2,1)S(1)}, bf16[136,16,128]{2,1,0:T(8,128)(2,1)S(1)}) custom-call(s32[8,64]{1,0:T(8,128)S(1)} %copy-done.6, s32[1]{0:T(128)S(6)} %copy.67.count, ...), custom_call_target="tpu_custom_call", output_to_operand_aliasing={{0}: (2, {}), {1}: (3, {}), {2}: (5, {}), {3}: (6, {})} | custom-call | flops 1258291200 | bytes 1048576 | tf_op jit(solution)/shard_map/late/pallas_call | solution.py:286
  114.8 3.1 %ghost.5 = (bf16[136,128,128]{2,1,0:T(8,128)(2,1)S(1)}, bf16[136,16,128]{2,1,0:T(8,128)(2,1)S(1)}, f32[8,4,128]{2,1,0:T(4,128)S(1)}) custom-call(s32[8,64]{1,0:T(8,128)S(1)} %copy-done.6, s32[8]{0:T(128)S(1)} %copy-done.9, s32[2]{0:T(128)S(1)} %and_select_fusion.parity, ...), custom_call_target="tpu_custom_call", output_to_operand_aliasing={{0}: (9, {}), {1}: (10, {})} | custom-call | flops 314572800 | bytes 1048576 | tf_op jit(solution)/shard_map/ghost/pallas_call | solution.py:286
  117.9 1.9 %collective-permute-start.13 = (f32[8,4,128]{2,1,0:T(4,128)S(1)}, f32[8,4,128]{2,1,0:T(4,128)S(1)}, u32[]{:S(2)}, u32[]{:S(2)}) collective-permute-start(f32[8,4,128]{2,1,0:T(4,128)S(1)} %get-tuple-element.65), channel_id=1, source_target_pairs={{0,32},{32,0},{64,96},{96,64},{128,160},{160,128},{192,224},{224,1... | collective-permute-start | bytes 49160 | tf_op jit(solution)/shard_map/ppermute | solution.py:305
  119.8 3.0 %collective-permute-start.12 = (f32[8,4,128]{2,1,0:T(4,128)S(1)}, f32[8,4,128]{2,1,0:T(4,128)S(1)}, u32[]{:S(2)}, u32[]{:S(2)}) collective-permute-start(f32[8,4,128]{2,1,0:T(4,128)S(1)} %get-tuple-element.65), channel_id=1, source_target_pairs={{32,64},{64,32},{96,128},{128,96},{160,192},{192,160},{224,256},{2... | collective-permute-start | bytes 49160 | tf_op jit(solution)/shard_map/ppermute | solution.py:305
  122.8 7.6 %early.5 = (f32[64,4,128]{2,1,0:T(4,128)S(1)}, f32[64,4,128]{2,1,0:T(4,128)S(1)}) custom-call(s32[8,64]{1,0:T(8,128)S(1)} %copy-done.6, s32[1]{0:T(128)S(6)} %copy.67.count, f32[64,4,128]{2,1,0:T(4,128)S(1)} %get-tuple-element.54.own, f32[64,4,128]{2,1,0:T(4,128)S(1)} %get-tuple-element.55.speeds, ...), custom_call_target="tpu_custom_call", output_to_operand_aliasing={{0}: (2, {}), {1}: (3, {})} | custom-call | flops 1258291200 | bytes 1048576 | tf_op jit(solution)/shard_map/early/pallas_call | solution.py:286
  130.4 2.0 %collective-permute-done.12 = f32[8,4,128]{2,1,0:T(4,128)S(1)} collective-permute-done((f32[8,4,128]{2,1,0:T(4,128)S(1)}, f32[8,4,128]{2,1,0:T(4,128)S(1)}, u32[]{:S(2)}, u32[]{:S(2)}) %collective-permute-start.12) | collective-permute-done | bytes 16416 | tf_op jit(solution)/shard_map/ppermute | solution.py:305
  132.4 1.9 %collective-permute-start.15 = (f32[24,4,128]{2,1,0:T(4,128)S(1)}, f32[24,4,128]{2,1,0:T(4,128)S(1)}, u32[]{:S(2)}, u32[]{:S(2)}) collective-permute-start(f32[24,4,128]{2,1,0:T(4,128)S(1)} %constant_dynamic-update-slice_fusion.6.middle), channel_id=1, source_target_pairs={{0,1},{1,0},{2,3},{3,2},{4,5},{5,4},{6,7},{7,6},{8,9},{9,8},{10,11... | collective-permute-start | bytes 147464 | tf_op jit(solution)/shard_map/ppermute | solution.py:305
  134.3 4.9 %collective-permute-start.14 = (f32[24,4,128]{2,1,0:T(4,128)S(1)}, f32[24,4,128]{2,1,0:T(4,128)S(1)}, u32[]{:S(2)}, u32[]{:S(2)}) collective-permute-start(f32[24,4,128]{2,1,0:T(4,128)S(1)} %constant_dynamic-update-slice_fusion.6.middle), channel_id=1, source_target_pairs={{1,2},{2,1},{3,4},{4,3},{5,6},{6,5},{7,8},{8,7},{9,10},{10,9},{11,... | collective-permute-start | bytes 147464 | tf_op jit(solution)/shard_map/ppermute | solution.py:305
  139.2 8.9 %late.5 = (f32[64,4,128]{2,1,0:T(4,128)S(1)}, f32[64,4,128]{2,1,0:T(4,128)S(1)}, bf16[136,128,128]{2,1,0:T(8,128)(2,1)S(1)}, bf16[136,16,128]{2,1,0:T(8,128)(2,1)S(1)}) custom-call(s32[8,64]{1,0:T(8,128)S(1)} %copy-done.6, s32[1]{0:T(128)S(6)} %copy.67.count, ...), custom_call_target="tpu_custom_call", output_to_operand_aliasing={{0}: (2, {}), {1}: (3, {}), {2}: (5, {}), {3}: (6, {})} | custom-call | flops 1258291200 | bytes 1048576 | tf_op jit(solution)/shard_map/late/pallas_call | solution.py:286
  148.1 16.0 %last.1 = (f32[3,8192]{1,0:T(4,128)}, f32[3,8192]{1,0:T(4,128)}, bf16[136,128,128]{2,1,0:T(8,128)(2,1)S(1)}, bf16[136,16,128]{2,1,0:T(8,128)(2,1)S(1)}) custom-call(s32[8,64]{1,0:T(8,128)S(1)} %copy-done.7, s32[2]{0:T(128)S(1)} %and_select_fusion.parity, s32[1]{0:T(128)S(6)} %copy.67.count, ...), custom_call_target="tpu_custom_call", output_to_operand_aliasing={{2}: (9, {}), {3}: (10, {})} | custom-call | flops 2516582400 | bytes 1048576 | tf_op jit(solution)/shard_map/last/pallas_call | solution.py:286
  (43 shorter events, 6.1 us)
Async XLA Ops:
  0.6 0.9 copy-start
  1.5 0.8 copy-start.4
  2.3 0.7 copy-start.8
  3.5 17.7 %collective-permute-start.1 = (f32[8,4,128]{2,1,0:T(4,128)S(1)}, f32[8,4,128]{2,1,0:T(4,128)S(1)}, u32[]{:S(2)}, u32[]{:S(2)}) collective-permute-start(f32[8,4,128]{2,1,0:T(4,128)S(1)} %choose.1), channel_id=1, source_target_pairs={{0,32},{32,0},{64,96},{96,64},{128,160},{160,128},{192,224},{224,1... | collective-permute-start | bytes 49160 | tf_op jit(solution)/shard_map/ppermute | solution.py:305
  6.9 16.0 %collective-permute-start = (f32[8,4,128]{2,1,0:T(4,128)S(1)}, f32[8,4,128]{2,1,0:T(4,128)S(1)}, u32[]{:S(2)}, u32[]{:S(2)}) collective-permute-start(f32[8,4,128]{2,1,0:T(4,128)S(1)} %choose.1), channel_id=1, source_target_pairs={{32,64},{64,32},{96,128},{128,96},{160,192},{192,160},{224,256},{2... | collective-permute-start | bytes 49160 | tf_op jit(solution)/shard_map/ppermute | solution.py:305
  22.9 14.1 %collective-permute-start.3 = (f32[24,4,128]{2,1,0:T(4,128)S(1)}, f32[24,4,128]{2,1,0:T(4,128)S(1)}, u32[]{:S(2)}, u32[]{:S(2)}) collective-permute-start(f32[24,4,128]{2,1,0:T(4,128)S(1)} %pad_maximum_fusion.middle), channel_id=1, source_target_pairs={{0,1},{1,0},{2,3},{3,2},{4,5},{5,4},{6,7},{7,6},{8,9},{9,8},{10,11... | collective-permute-start | bytes 147464 | tf_op jit(solution)/shard_map/ppermute | solution.py:305
  24.8 12.1 %collective-permute-start.2 = (f32[24,4,128]{2,1,0:T(4,128)S(1)}, f32[24,4,128]{2,1,0:T(4,128)S(1)}, u32[]{:S(2)}, u32[]{:S(2)}) collective-permute-start(f32[24,4,128]{2,1,0:T(4,128)S(1)} %pad_maximum_fusion.middle), channel_id=1, source_target_pairs={{1,2},{2,1},{3,4},{4,3},{5,6},{6,5},{7,8},{8,7},{9,10},{10,9},{11,... | collective-permute-start | bytes 147464 | tf_op jit(solution)/shard_map/ppermute | solution.py:305
  32.2 0.9 copy-start.1
  33.1 0.9 copy-start.2
  34.0 0.9 copy-start.3
  34.9 0.8 copy-start.5
  37.0 0.7 copy-start.6
  37.7 0.7 copy-start.9
  41.4 16.3 %collective-permute-start.5 = (f32[8,4,128]{2,1,0:T(4,128)S(1)}, f32[8,4,128]{2,1,0:T(4,128)S(1)}, u32[]{:S(2)}, u32[]{:S(2)}) collective-permute-start(f32[8,4,128]{2,1,0:T(4,128)S(1)} %get-tuple-element.47), channel_id=1, source_target_pairs={{0,32},{32,0},{64,96},{96,64},{128,160},{160,128},{192,224},{224,1... | collective-permute-start | bytes 49160 | tf_op jit(solution)/shard_map/ppermute | solution.py:305
  43.4 14.3 %collective-permute-start.4 = (f32[8,4,128]{2,1,0:T(4,128)S(1)}, f32[8,4,128]{2,1,0:T(4,128)S(1)}, u32[]{:S(2)}, u32[]{:S(2)}) collective-permute-start(f32[8,4,128]{2,1,0:T(4,128)S(1)} %get-tuple-element.47), channel_id=1, source_target_pairs={{32,64},{64,32},{96,128},{128,96},{160,192},{192,160},{224,256},{2... | collective-permute-start | bytes 49160 | tf_op jit(solution)/shard_map/ppermute | solution.py:305
  57.7 23.3 %collective-permute-start.7 = (f32[24,4,128]{2,1,0:T(4,128)S(1)}, f32[24,4,128]{2,1,0:T(4,128)S(1)}, u32[]{:S(2)}, u32[]{:S(2)}) collective-permute-start(f32[24,4,128]{2,1,0:T(4,128)S(1)} %constant_dynamic-update-slice_fusion.middle), channel_id=1, source_target_pairs={{0,1},{1,0},{2,3},{3,2},{4,5},{5,4},{6,7},{7,6},{8,9},{9,8},{10,11... | collective-permute-start | bytes 147464 | tf_op jit(solution)/shard_map/ppermute | solution.py:305
  59.7 21.3 %collective-permute-start.6 = (f32[24,4,128]{2,1,0:T(4,128)S(1)}, f32[24,4,128]{2,1,0:T(4,128)S(1)}, u32[]{:S(2)}, u32[]{:S(2)}) collective-permute-start(f32[24,4,128]{2,1,0:T(4,128)S(1)} %constant_dynamic-update-slice_fusion.middle), channel_id=1, source_target_pairs={{1,2},{2,1},{3,4},{4,3},{5,6},{6,5},{7,8},{8,7},{9,10},{10,9},{11,... | collective-permute-start | bytes 147464 | tf_op jit(solution)/shard_map/ppermute | solution.py:305
  84.1 14.5 %collective-permute-start.9 = (f32[8,4,128]{2,1,0:T(4,128)S(1)}, f32[8,4,128]{2,1,0:T(4,128)S(1)}, u32[]{:S(2)}, u32[]{:S(2)}) collective-permute-start(f32[8,4,128]{2,1,0:T(4,128)S(1)} %get-tuple-element.56), channel_id=1, source_target_pairs={{0,32},{32,0},{64,96},{96,64},{128,160},{160,128},{192,224},{224,1... | collective-permute-start | bytes 49160 | tf_op jit(solution)/shard_map/ppermute | solution.py:305
  86.1 12.5 %collective-permute-start.8 = (f32[8,4,128]{2,1,0:T(4,128)S(1)}, f32[8,4,128]{2,1,0:T(4,128)S(1)}, u32[]{:S(2)}, u32[]{:S(2)}) collective-permute-start(f32[8,4,128]{2,1,0:T(4,128)S(1)} %get-tuple-element.56), channel_id=1, source_target_pairs={{32,64},{64,32},{96,128},{128,96},{160,192},{192,160},{224,256},{2... | collective-permute-start | bytes 49160 | tf_op jit(solution)/shard_map/ppermute | solution.py:305
  98.6 16.1 %collective-permute-start.11 = (f32[24,4,128]{2,1,0:T(4,128)S(1)}, f32[24,4,128]{2,1,0:T(4,128)S(1)}, u32[]{:S(2)}, u32[]{:S(2)}) collective-permute-start(f32[24,4,128]{2,1,0:T(4,128)S(1)} %constant_dynamic-update-slice_fusion.3.middle), channel_id=1, source_target_pairs={{0,1},{1,0},{2,3},{3,2},{4,5},{5,4},{6,7},{7,6},{8,9},{9,8},{10,11... | collective-permute-start | bytes 147464 | tf_op jit(solution)/shard_map/ppermute | solution.py:305
  100.6 14.2 %collective-permute-start.10 = (f32[24,4,128]{2,1,0:T(4,128)S(1)}, f32[24,4,128]{2,1,0:T(4,128)S(1)}, u32[]{:S(2)}, u32[]{:S(2)}) collective-permute-start(f32[24,4,128]{2,1,0:T(4,128)S(1)} %constant_dynamic-update-slice_fusion.3.middle), channel_id=1, source_target_pairs={{1,2},{2,1},{3,4},{4,3},{5,6},{6,5},{7,8},{8,7},{9,10},{10,9},{11,... | collective-permute-start | bytes 147464 | tf_op jit(solution)/shard_map/ppermute | solution.py:305
  117.9 14.5 %collective-permute-start.13 = (f32[8,4,128]{2,1,0:T(4,128)S(1)}, f32[8,4,128]{2,1,0:T(4,128)S(1)}, u32[]{:S(2)}, u32[]{:S(2)}) collective-permute-start(f32[8,4,128]{2,1,0:T(4,128)S(1)} %get-tuple-element.65), channel_id=1, source_target_pairs={{0,32},{32,0},{64,96},{96,64},{128,160},{160,128},{192,224},{224,1... | collective-permute-start | bytes 49160 | tf_op jit(solution)/shard_map/ppermute | solution.py:305
  119.8 12.5 %collective-permute-start.12 = (f32[8,4,128]{2,1,0:T(4,128)S(1)}, f32[8,4,128]{2,1,0:T(4,128)S(1)}, u32[]{:S(2)}, u32[]{:S(2)}) collective-permute-start(f32[8,4,128]{2,1,0:T(4,128)S(1)} %get-tuple-element.65), channel_id=1, source_target_pairs={{32,64},{64,32},{96,128},{128,96},{160,192},{192,160},{224,256},{2... | collective-permute-start | bytes 49160 | tf_op jit(solution)/shard_map/ppermute | solution.py:305
  130.4 17.7 %copy-start.7 = (s32[8,64]{1,0:T(8,128)S(1)}, s32[8,64]{1,0:T(8,128)}, u32[]{:S(2)}) copy-start(s32[8,64]{1,0:T(8,128)} %lists.19) | copy-start | bytes 6148
  132.4 15.7 %collective-permute-start.15 = (f32[24,4,128]{2,1,0:T(4,128)S(1)}, f32[24,4,128]{2,1,0:T(4,128)S(1)}, u32[]{:S(2)}, u32[]{:S(2)}) collective-permute-start(f32[24,4,128]{2,1,0:T(4,128)S(1)} %constant_dynamic-update-slice_fusion.6.middle), channel_id=1, source_target_pairs={{0,1},{1,0},{2,3},{3,2},{4,5},{5,4},{6,7},{7,6},{8,9},{9,8},{10,11... | collective-permute-start | bytes 147464 | tf_op jit(solution)/shard_map/ppermute | solution.py:305
  134.3 13.8 %collective-permute-start.14 = (f32[24,4,128]{2,1,0:T(4,128)S(1)}, f32[24,4,128]{2,1,0:T(4,128)S(1)}, u32[]{:S(2)}, u32[]{:S(2)}) collective-permute-start(f32[24,4,128]{2,1,0:T(4,128)S(1)} %constant_dynamic-update-slice_fusion.6.middle), channel_id=1, source_target_pairs={{1,2},{2,1},{3,4},{4,3},{5,6},{6,5},{7,8},{8,7},{9,10},{10,9},{11,... | collective-permute-start | bytes 147464 | tf_op jit(solution)/shard_map/ppermute | solution.py:305

commit v3 on v2

--- a/solution.py
+++ b/solution.py
@@ -201,19 +201,19 @@
 
 
 def enter_ghosts(parity, sides, sources, moments):
-    for q, side in enumerate(sides):
-        b = jnp.where(parity[1] == 1, 2 - q, q)
+    for q, side in sides.items():
+        b = jnp.where(parity[1] == 1, q, 2 - q)
         for p in range(3):
-            a = jnp.where(parity[0] == 1, 2 - p, p)
+            a = jnp.where(parity[0] == 1, p, 2 - p)
             for g in range(GHOSTS):
                 enter(sources, moments, LEAVES + (a * 3 + b) * GHOSTS + g, side[p * GHOSTS + g])
 
 
 def ghost_kernel(
-    lists, ids, parity, own, speeds, kicks, far, middle, near, old_sources, old_moments,
+    lists, ids, parity, own, speeds, kicks, near, far, old_sources, old_moments,
     sources, moments, chosen,
 ):
-    enter_ghosts(parity, (far, middle, near), sources, moments)
+    enter_ghosts(parity, {0: near, 2: far}, sources, moments)
 
     results = group_moved(
         lists, sources, moments, own, speeds, kicks, [ids[g] for g in range(GHOSTS)]
@@ -235,8 +235,12 @@
     )
 
 
+def middle_kernel(parity, middle, old_sources, old_moments, sources, moments):
+    enter_ghosts(parity, {1: middle}, sources, moments)
+
+
 def late_kernel(
-    lists, count, own, speeds, kicks, old_sources, old_moments,
+    lists, parity, count, own, speeds, kicks, middle, old_sources, old_moments,
     new_own, new_speeds, sources, moments,
 ):
     groups = groups_of(count)
@@ -245,13 +249,14 @@
         lax.div(groups, 2), groups,
     )
     enter_all(sources, moments, new_own, lambda leaf: leaf, LEAVES)
+    enter_ghosts(parity, {1: middle}, sources, moments)
 
 
 def last_kernel(
-    lists, parity, count, own, speeds, kicks, far, middle, near, old_sources, old_moments,
+    lists, parity, count, own, speeds, kicks, near, far, old_sources, old_moments,
     places, paces, sources, moments,
 ):
-    enter_ghosts(parity, (far, middle, near), sources, moments)
+    enter_ghosts(parity, {0: near, 2: far}, sources, moments)
 
     def group(index, carry):
         leaves = [index * GROUP + u for u in range(GROUP)]
@@ -323,27 +328,35 @@
                 early_kernel, "early", (lists, count), (own, speeds, kicks, sources, moments),
                 (record_shape, record_shape), {0: 0, 1: 1}, LEAVES // 2,
             )
-        middle = jnp.concatenate([far, chosen, near], axis=0)
+        middle = jnp.concatenate([near, chosen, far], axis=0)
+        if not subcycle:
+            middle, own = lax.optimization_barrier((middle, own))
         far = swapped(middle, "gy", 1)
         near = swapped(middle, "gy", 0)
         if subcycle:
             own, speeds, sources, moments = call(
-                late_kernel, "late", (lists, count), (own, speeds, kicks, sources, moments),
+                late_kernel, "late", (lists, parity, count),
+                (own, speeds, kicks, middle, sources, moments),
                 (record_shape, record_shape, sources_shape, moments_shape),
-                {0: 0, 1: 1, 3: 2, 4: 3}, LEAVES // 2,
+                {0: 0, 1: 1, 4: 2, 5: 3}, LEAVES // 2,
+            )
+        else:
+            sources, moments = call(
+                middle_kernel, "middle", (parity,), (middle, sources, moments),
+                (sources_shape, moments_shape), {1: 0, 2: 1}, 1,
             )
         if subcycle < SUBCYCLES - 1:
             sources, moments, chosen = call(
                 ghost_kernel, "ghost", (lists, ids, parity),
-                (own, speeds, kicks, far, middle, near, sources, moments),
-                (sources_shape, moments_shape, chosen_shape), {6: 0, 7: 1}, GHOSTS,
+                (own, speeds, kicks, near, far, sources, moments),
+                (sources_shape, moments_shape, chosen_shape), {5: 0, 6: 1}, GHOSTS,
             )
         else:
             places, paces, _, _ = call(
                 last_kernel, "last", (lists, parity, count),
-                (own, speeds, kicks, far, middle, near, sources, moments),
+                (own, speeds, kicks, near, far, sources, moments),
                 (whole_shape, whole_shape, sources_shape, moments_shape),
-                {6: 2, 7: 3}, LEAVES,
+                {5: 2, 6: 3}, LEAVES,
             )
     return places, paces
 

time: 165 us -> 148 us (0.90)
  the two profiles are of different devices: /device:TPU:8 before, /device:TPU:0 now
where the time goes in v3:
time: 148 us; the launch traced here: 147 us
  Pallas kernels  77.6 us (52%)
  starting transfers between devices  60.2 us (41%)
  local copies, waits for them, and re-layouts  5.85 us (4%)
  waiting for transfers between devices  1.71 us (1%)
  between operations  1.69 us (1%)
    pallas_call x13, Pallas kernels, call(): pl.pallas_call(kernel, out_shape=outs, in_specs=[SMEM] * len(scalars) + [...  77.6 us
    ppermute x16, starting transfers between devices, swapped(): return lax.ppermute(block, axis, route)  60.2 us
    unnamed x24, local copies, waits for them, and re-layouts  5.83 us
  transfers between devices with their start and end apart: 16, of which 2 were waited for; matrix products, arithmetic and copies ran while one was open for 0% of the time, Pallas kernels for 36%

profile of v3, /device:TPU:0, one launch (start us, length us, event | category | flops | bytes accessed | tf_op | source)
XLA Modules:
  0.0 147.1 jit_solution(11120535524848852807)
XLA Ops:
  0.7 0.9 copy-done
  3.5 5.9 %collective-permute-start.1 = (f32[8,4,128]{2,1,0:T(4,128)S(1)}, f32[8,4,128]{2,1,0:T(4,128)S(1)}, u32[]{:S(2)}, u32[]{:S(2)}) collective-permute-start(f32[8,4,128]{2,1,0:T(4,128)S(1)} %choose.1), channel_id=1, source_target_pairs={{32,64},{64,32},{96,128},{128,96},{160,192},{192,160},{224,256},{2... | collective-permute-start | bytes 49160 | tf_op jit(solution)/shard_map/ppermute | solution.py:310
  9.4 1.9 %collective-permute-start = (f32[8,4,128]{2,1,0:T(4,128)S(1)}, f32[8,4,128]{2,1,0:T(4,128)S(1)}, u32[]{:S(2)}, u32[]{:S(2)}) collective-permute-start(f32[8,4,128]{2,1,0:T(4,128)S(1)} %choose.1), channel_id=1, source_target_pairs={{0,32},{32,0},{64,96},{96,64},{128,160},{160,128},{192,224},{224,1... | collective-permute-start | bytes 49160 | tf_op jit(solution)/shard_map/ppermute | solution.py:310
  11.4 0.9 copy-done.1
  12.3 0.9 copy-done.2
  13.2 0.9 copy-done.3
  14.9 1.3 open.1
  16.2 12.1 %collective-permute-start.3 = (f32[24,4,128]{2,1,0:T(4,128)S(1)}, f32[24,4,128]{2,1,0:T(4,128)S(1)}, u32[]{:S(2)}, u32[]{:S(2)}) collective-permute-start(f32[24,4,128]{2,1,0:T(4,128)S(1)} %pad_maximum_fusion.middle), channel_id=1, source_target_pairs={{1,2},{2,1},{3,4},{4,3},{5,6},{6,5},{7,8},{8,7},{9,10},{10,9},{11,... | collective-permute-start | bytes 147464 | tf_op jit(solution)/shard_map/ppermute | solution.py:310
  28.4 1.9 %collective-permute-start.2 = (f32[24,4,128]{2,1,0:T(4,128)S(1)}, f32[24,4,128]{2,1,0:T(4,128)S(1)}, u32[]{:S(2)}, u32[]{:S(2)}) collective-permute-start(f32[24,4,128]{2,1,0:T(4,128)S(1)} %pad_maximum_fusion.middle), channel_id=1, source_target_pairs={{0,1},{1,0},{2,3},{3,2},{4,5},{5,4},{6,7},{7,6},{8,9},{9,8},{10,11... | collective-permute-start | bytes 147464 | tf_op jit(solution)/shard_map/ppermute | solution.py:310
  31.9 2.9 %ghost.3 = (bf16[136,128,128]{2,1,0:T(8,128)(2,1)S(1)}, bf16[136,16,128]{2,1,0:T(8,128)(2,1)S(1)}, f32[8,4,128]{2,1,0:T(4,128)S(1)}) custom-call(s32[8,64]{1,0:T(8,128)S(1)} %copy-done.6, s32[8]{0:T(128)S(1)} %copy-done.8, s32[2]{0:T(128)S(1)} %and_select_fusion.parity, ...), custom_call_target="tpu_custom_call", output_to_operand_aliasing={{0}: (8, {}), {1}: (9, {})} | custom-call | flops 314572800 | bytes 1048576 | tf_op jit(solution)/shard_map/ghost/pallas_call | solution.py:291
  34.8 5.3 %collective-permute-start.5 = (f32[8,4,128]{2,1,0:T(4,128)S(1)}, f32[8,4,128]{2,1,0:T(4,128)S(1)}, u32[]{:S(2)}, u32[]{:S(2)}) collective-permute-start(f32[8,4,128]{2,1,0:T(4,128)S(1)} %get-tuple-element.53), channel_id=1, source_target_pairs={{32,64},{64,32},{96,128},{128,96},{160,192},{192,160},{224,256},{2... | collective-permute-start | bytes 49160 | tf_op jit(solution)/shard_map/ppermute | solution.py:310
  40.1 1.9 %collective-permute-start.4 = (f32[8,4,128]{2,1,0:T(4,128)S(1)}, f32[8,4,128]{2,1,0:T(4,128)S(1)}, u32[]{:S(2)}, u32[]{:S(2)}) collective-permute-start(f32[8,4,128]{2,1,0:T(4,128)S(1)} %get-tuple-element.53), channel_id=1, source_target_pairs={{0,32},{32,0},{64,96},{96,64},{128,160},{160,128},{192,224},{224,1... | collective-permute-start | bytes 49160 | tf_op jit(solution)/shard_map/ppermute | solution.py:310
  42.0 7.6 %early.3 = (f32[64,4,128]{2,1,0:T(4,128)S(1)}, f32[64,4,128]{2,1,0:T(4,128)S(1)}) custom-call(s32[8,64]{1,0:T(8,128)S(1)} %copy-done.6, s32[1]{0:T(128)S(6)} %copy.71.count, f32[64,4,128]{2,1,0:T(4,128)S(1)} %get-tuple-element.41.own, f32[64,4,128]{2,1,0:T(4,128)S(1)} %get-tuple-element.42.speeds, ...), custom_call_target="tpu_custom_call", output_to_operand_aliasing={{0}: (2, {}), {1}: (3, {})} | custom-call | flops 1258291200 | bytes 1048576 | tf_op jit(solution)/shard_map/early/pallas_call | solution.py:291
  49.7 6.8 %collective-permute-start.7 = (f32[24,4,128]{2,1,0:T(4,128)S(1)}, f32[24,4,128]{2,1,0:T(4,128)S(1)}, u32[]{:S(2)}, u32[]{:S(2)}) collective-permute-start(f32[24,4,128]{2,1,0:T(4,128)S(1)} %constant_dynamic-update-slice_fusion.middle), channel_id=1, source_target_pairs={{1,2},{2,1},{3,4},{4,3},{5,6},{6,5},{7,8},{8,7},{9,10},{10,9},{11,... | collective-permute-start | bytes 147464 | tf_op jit(solution)/shard_map/ppermute | solution.py:310
  56.5 1.9 %collective-permute-start.6 = (f32[24,4,128]{2,1,0:T(4,128)S(1)}, f32[24,4,128]{2,1,0:T(4,128)S(1)}, u32[]{:S(2)}, u32[]{:S(2)}) collective-permute-start(f32[24,4,128]{2,1,0:T(4,128)S(1)} %constant_dynamic-update-slice_fusion.middle), channel_id=1, source_target_pairs={{0,1},{1,0},{2,3},{3,2},{4,5},{5,4},{6,7},{7,6},{8,9},{9,8},{10,11... | collective-permute-start | bytes 147464 | tf_op jit(solution)/shard_map/ppermute | solution.py:310
  58.4 9.2 %late.3 = (f32[64,4,128]{2,1,0:T(4,128)S(1)}, f32[64,4,128]{2,1,0:T(4,128)S(1)}, bf16[136,128,128]{2,1,0:T(8,128)(2,1)S(1)}, bf16[136,16,128]{2,1,0:T(8,128)(2,1)S(1)}) custom-call(s32[8,64]{1,0:T(8,128)S(1)} %copy-done.6, s32[2]{0:T(128)S(1)} %and_select_fusion.parity, ...), custom_call_target="tpu_custom_call", output_to_operand_aliasing={{0}: (3, {}), {1}: (4, {}), {2}: (7, {}), {3}: (8, {})} | custom-call | flops 1258291200 | bytes 1048576 | tf_op jit(solution)/shard_map/late/pallas_call | solution.py:291
  67.6 2.9 %ghost.4 = (bf16[136,128,128]{2,1,0:T(8,128)(2,1)S(1)}, bf16[136,16,128]{2,1,0:T(8,128)(2,1)S(1)}, f32[8,4,128]{2,1,0:T(4,128)S(1)}) custom-call(s32[8,64]{1,0:T(8,128)S(1)} %copy-done.6, s32[8]{0:T(128)S(1)} %copy-done.8, s32[2]{0:T(128)S(1)} %and_select_fusion.parity, ...), custom_call_target="tpu_custom_call", output_to_operand_aliasing={{0}: (8, {}), {1}: (9, {})} | custom-call | flops 314572800 | bytes 1048576 | tf_op jit(solution)/shard_map/ghost/pallas_call | solution.py:291
  70.5 1.9 %collective-permute-start.9 = (f32[8,4,128]{2,1,0:T(4,128)S(1)}, f32[8,4,128]{2,1,0:T(4,128)S(1)}, u32[]{:S(2)}, u32[]{:S(2)}) collective-permute-start(f32[8,4,128]{2,1,0:T(4,128)S(1)} %get-tuple-element.62), channel_id=1, source_target_pairs={{32,64},{64,32},{96,128},{128,96},{160,192},{192,160},{224,256},{2... | collective-permute-start | bytes 49160 | tf_op jit(solution)/shard_map/ppermute | solution.py:310
  72.4 1.9 %collective-permute-start.8 = (f32[8,4,128]{2,1,0:T(4,128)S(1)}, f32[8,4,128]{2,1,0:T(4,128)S(1)}, u32[]{:S(2)}, u32[]{:S(2)}) collective-permute-start(f32[8,4,128]{2,1,0:T(4,128)S(1)} %get-tuple-element.62), channel_id=1, source_target_pairs={{0,32},{32,0},{64,96},{96,64},{128,160},{160,128},{192,224},{224,1... | collective-permute-start | bytes 49160 | tf_op jit(solution)/shard_map/ppermute | solution.py:310
  74.3 7.6 %early.4 = (f32[64,4,128]{2,1,0:T(4,128)S(1)}, f32[64,4,128]{2,1,0:T(4,128)S(1)}) custom-call(s32[8,64]{1,0:T(8,128)S(1)} %copy-done.6, s32[1]{0:T(128)S(6)} %copy.71.count, f32[64,4,128]{2,1,0:T(4,128)S(1)} %get-tuple-element.54.own, f32[64,4,128]{2,1,0:T(4,128)S(1)} %get-tuple-element.55.speeds, ...), custom_call_target="tpu_custom_call", output_to_operand_aliasing={{0}: (2, {}), {1}: (3, {})} | custom-call | flops 1258291200 | bytes 1048576 | tf_op jit(solution)/shard_map/early/pallas_call | solution.py:291
  81.9 1.1 collective-permute-done.9
  83.0 1.9 %collective-permute-start.11 = (f32[24,4,128]{2,1,0:T(4,128)S(1)}, f32[24,4,128]{2,1,0:T(4,128)S(1)}, u32[]{:S(2)}, u32[]{:S(2)}) collective-permute-start(f32[24,4,128]{2,1,0:T(4,128)S(1)} %constant_dynamic-update-slice_fusion.3.middle), channel_id=1, source_target_pairs={{1,2},{2,1},{3,4},{4,3},{5,6},{6,5},{7,8},{8,7},{9,10},{10,9},{11,... | collective-permute-start | bytes 147464 | tf_op jit(solution)/shard_map/ppermute | solution.py:310
  84.9 1.9 %collective-permute-start.10 = (f32[24,4,128]{2,1,0:T(4,128)S(1)}, f32[24,4,128]{2,1,0:T(4,128)S(1)}, u32[]{:S(2)}, u32[]{:S(2)}) collective-permute-start(f32[24,4,128]{2,1,0:T(4,128)S(1)} %constant_dynamic-update-slice_fusion.3.middle), channel_id=1, source_target_pairs={{0,1},{1,0},{2,3},{3,2},{4,5},{5,4},{6,7},{7,6},{8,9},{9,8},{10,11... | collective-permute-start | bytes 147464 | tf_op jit(solution)/shard_map/ppermute | solution.py:310
  86.9 9.4 %late.4 = (f32[64,4,128]{2,1,0:T(4,128)S(1)}, f32[64,4,128]{2,1,0:T(4,128)S(1)}, bf16[136,128,128]{2,1,0:T(8,128)(2,1)S(1)}, bf16[136,16,128]{2,1,0:T(8,128)(2,1)S(1)}) custom-call(s32[8,64]{1,0:T(8,128)S(1)} %copy-done.6, s32[2]{0:T(128)S(1)} %and_select_fusion.parity, ...), custom_call_target="tpu_custom_call", output_to_operand_aliasing={{0}: (3, {}), {1}: (4, {}), {2}: (7, {}), {3}: (8, {})} | custom-call | flops 1258291200 | bytes 1048576 | tf_op jit(solution)/shard_map/late/pallas_call | solution.py:291
  96.8 2.9 %ghost.5 = (bf16[136,128,128]{2,1,0:T(8,128)(2,1)S(1)}, bf16[136,16,128]{2,1,0:T(8,128)(2,1)S(1)}, f32[8,4,128]{2,1,0:T(4,128)S(1)}) custom-call(s32[8,64]{1,0:T(8,128)S(1)} %copy-done.6, s32[8]{0:T(128)S(1)} %copy-done.8, s32[2]{0:T(128)S(1)} %and_select_fusion.parity, ...), custom_call_target="tpu_custom_call", output_to_operand_aliasing={{0}: (8, {}), {1}: (9, {})} | custom-call | flops 314572800 | bytes 1048576 | tf_op jit(solution)/shard_map/ghost/pallas_call | solution.py:291
  99.7 5.9 %collective-permute-start.13 = (f32[8,4,128]{2,1,0:T(4,128)S(1)}, f32[8,4,128]{2,1,0:T(4,128)S(1)}, u32[]{:S(2)}, u32[]{:S(2)}) collective-permute-start(f32[8,4,128]{2,1,0:T(4,128)S(1)} %get-tuple-element.71), channel_id=1, source_target_pairs={{32,64},{64,32},{96,128},{128,96},{160,192},{192,160},{224,256},{2... | collective-permute-start | bytes 49160 | tf_op jit(solution)/shard_map/ppermute | solution.py:310
  105.6 1.9 %collective-permute-start.12 = (f32[8,4,128]{2,1,0:T(4,128)S(1)}, f32[8,4,128]{2,1,0:T(4,128)S(1)}, u32[]{:S(2)}, u32[]{:S(2)}) collective-permute-start(f32[8,4,128]{2,1,0:T(4,128)S(1)} %get-tuple-element.71), channel_id=1, source_target_pairs={{0,32},{32,0},{64,96},{96,64},{128,160},{160,128},{192,224},{224,1... | collective-permute-start | bytes 49160 | tf_op jit(solution)/shard_map/ppermute | solution.py:310
  107.5 7.6 %early.5 = (f32[64,4,128]{2,1,0:T(4,128)S(1)}, f32[64,4,128]{2,1,0:T(4,128)S(1)}) custom-call(s32[8,64]{1,0:T(8,128)S(1)} %copy-done.6, s32[1]{0:T(128)S(6)} %copy.71.count, f32[64,4,128]{2,1,0:T(4,128)S(1)} %get-tuple-element.63.own, f32[64,4,128]{2,1,0:T(4,128)S(1)} %get-tuple-element.64.speeds, ...), custom_call_target="tpu_custom_call", output_to_operand_aliasing={{0}: (2, {}), {1}: (3, {})} | custom-call | flops 1258291200 | bytes 1048576 | tf_op jit(solution)/shard_map/early/pallas_call | solution.py:291
  115.2 5.0 %collective-permute-start.15 = (f32[24,4,128]{2,1,0:T(4,128)S(1)}, f32[24,4,128]{2,1,0:T(4,128)S(1)}, u32[]{:S(2)}, u32[]{:S(2)}) collective-permute-start(f32[24,4,128]{2,1,0:T(4,128)S(1)} %constant_dynamic-update-slice_fusion.6.middle), channel_id=1, source_target_pairs={{1,2},{2,1},{3,4},{4,3},{5,6},{6,5},{7,8},{8,7},{9,10},{10,9},{11,... | collective-permute-start | bytes 147464 | tf_op jit(solution)/shard_map/ppermute | solution.py:310
  120.2 1.9 %collective-permute-start.14 = (f32[24,4,128]{2,1,0:T(4,128)S(1)}, f32[24,4,128]{2,1,0:T(4,128)S(1)}, u32[]{:S(2)}, u32[]{:S(2)}) collective-permute-start(f32[24,4,128]{2,1,0:T(4,128)S(1)} %constant_dynamic-update-slice_fusion.6.middle), channel_id=1, source_target_pairs={{0,1},{1,0},{2,3},{3,2},{4,5},{5,4},{6,7},{7,6},{8,9},{9,8},{10,11... | collective-permute-start | bytes 147464 | tf_op jit(solution)/shard_map/ppermute | solution.py:310
  122.1 9.2 %late.5 = (f32[64,4,128]{2,1,0:T(4,128)S(1)}, f32[64,4,128]{2,1,0:T(4,128)S(1)}, bf16[136,128,128]{2,1,0:T(8,128)(2,1)S(1)}, bf16[136,16,128]{2,1,0:T(8,128)(2,1)S(1)}) custom-call(s32[8,64]{1,0:T(8,128)S(1)} %copy-done.6, s32[2]{0:T(128)S(1)} %and_select_fusion.parity, ...), custom_call_target="tpu_custom_call", output_to_operand_aliasing={{0}: (3, {}), {1}: (4, {}), {2}: (7, {}), {3}: (8, {})} | custom-call | flops 1258291200 | bytes 1048576 | tf_op jit(solution)/shard_map/late/pallas_call | solution.py:291
  131.3 15.8 %last.1 = (f32[3,8192]{1,0:T(4,128)}, f32[3,8192]{1,0:T(4,128)}, bf16[136,128,128]{2,1,0:T(8,128)(2,1)S(1)}, bf16[136,16,128]{2,1,0:T(8,128)(2,1)S(1)}) custom-call(s32[8,64]{1,0:T(8,128)S(1)} %copy-done.6, s32[2]{0:T(128)S(1)} %and_select_fusion.parity, s32[1]{0:T(128)S(6)} %copy.71.count, ...), custom_call_target="tpu_custom_call", output_to_operand_aliasing={{2}: (8, {}), {3}: (9, {})} | custom-call | flops 2516582400 | bytes 1048576 | tf_op jit(solution)/shard_map/last/pallas_call | solution.py:291
  (42 shorter events, 4.4 us)
Async XLA Ops:
  0.6 31.3 %copy-start.8 = (s32[8]{0:T(128)S(1)}, s32[8]{0:T(128)}, u32[]{:S(2)}) copy-start(s32[8]{0:T(128)} %ids.7) | copy-start | bytes 100
  0.6 0.9 copy-start
  1.6 0.8 copy-start.4
  2.3 0.7 copy-start.7
  3.0 28.9 %copy-start.6 = (s32[8,64]{1,0:T(8,128)S(1)}, s32[8,64]{1,0:T(8,128)}, u32[]{:S(2)}) copy-start(s32[8,64]{1,0:T(8,128)} %lists.19) | copy-start | bytes 6148
  3.5 12.7 %collective-permute-start.1 = (f32[8,4,128]{2,1,0:T(4,128)S(1)}, f32[8,4,128]{2,1,0:T(4,128)S(1)}, u32[]{:S(2)}, u32[]{:S(2)}) collective-permute-start(f32[8,4,128]{2,1,0:T(4,128)S(1)} %choose.1), channel_id=1, source_target_pairs={{32,64},{64,32},{96,128},{128,96},{160,192},{192,160},{224,256},{2... | collective-permute-start | bytes 49160 | tf_op jit(solution)/shard_map/ppermute | solution.py:310
  9.4 6.8 %collective-permute-start = (f32[8,4,128]{2,1,0:T(4,128)S(1)}, f32[8,4,128]{2,1,0:T(4,128)S(1)}, u32[]{:S(2)}, u32[]{:S(2)}) collective-permute-start(f32[8,4,128]{2,1,0:T(4,128)S(1)} %choose.1), channel_id=1, source_target_pairs={{0,32},{32,0},{64,96},{96,64},{128,160},{160,128},{192,224},{224,1... | collective-permute-start | bytes 49160 | tf_op jit(solution)/shard_map/ppermute | solution.py:310
  11.4 0.9 copy-start.1
  12.3 0.9 copy-start.2
  13.2 0.9 copy-start.3
  14.1 0.8 copy-start.5
  16.2 15.6 %collective-permute-start.3 = (f32[24,4,128]{2,1,0:T(4,128)S(1)}, f32[24,4,128]{2,1,0:T(4,128)S(1)}, u32[]{:S(2)}, u32[]{:S(2)}) collective-permute-start(f32[24,4,128]{2,1,0:T(4,128)S(1)} %pad_maximum_fusion.middle), channel_id=1, source_target_pairs={{1,2},{2,1},{3,4},{4,3},{5,6},{6,5},{7,8},{8,7},{9,10},{10,9},{11,... | collective-permute-start | bytes 147464 | tf_op jit(solution)/shard_map/ppermute | solution.py:310
  28.4 3.5 %collective-permute-start.2 = (f32[24,4,128]{2,1,0:T(4,128)S(1)}, f32[24,4,128]{2,1,0:T(4,128)S(1)}, u32[]{:S(2)}, u32[]{:S(2)}) collective-permute-start(f32[24,4,128]{2,1,0:T(4,128)S(1)} %pad_maximum_fusion.middle), channel_id=1, source_target_pairs={{0,1},{1,0},{2,3},{3,2},{4,5},{5,4},{6,7},{7,6},{8,9},{9,8},{10,11... | collective-permute-start | bytes 147464 | tf_op jit(solution)/shard_map/ppermute | solution.py:310
  34.8 14.9 %collective-permute-start.5 = (f32[8,4,128]{2,1,0:T(4,128)S(1)}, f32[8,4,128]{2,1,0:T(4,128)S(1)}, u32[]{:S(2)}, u32[]{:S(2)}) collective-permute-start(f32[8,4,128]{2,1,0:T(4,128)S(1)} %get-tuple-element.53), channel_id=1, source_target_pairs={{32,64},{64,32},{96,128},{128,96},{160,192},{192,160},{224,256},{2... | collective-permute-start | bytes 49160 | tf_op jit(solution)/shard_map/ppermute | solution.py:310
  40.1 9.5 %collective-permute-start.4 = (f32[8,4,128]{2,1,0:T(4,128)S(1)}, f32[8,4,128]{2,1,0:T(4,128)S(1)}, u32[]{:S(2)}, u32[]{:S(2)}) collective-permute-start(f32[8,4,128]{2,1,0:T(4,128)S(1)} %get-tuple-element.53), channel_id=1, source_target_pairs={{0,32},{32,0},{64,96},{96,64},{128,160},{160,128},{192,224},{224,1... | collective-permute-start | bytes 49160 | tf_op jit(solution)/shard_map/ppermute | solution.py:310
  49.7 17.9 %collective-permute-start.7 = (f32[24,4,128]{2,1,0:T(4,128)S(1)}, f32[24,4,128]{2,1,0:T(4,128)S(1)}, u32[]{:S(2)}, u32[]{:S(2)}) collective-permute-start(f32[24,4,128]{2,1,0:T(4,128)S(1)} %constant_dynamic-update-slice_fusion.middle), channel_id=1, source_target_pairs={{1,2},{2,1},{3,4},{4,3},{5,6},{6,5},{7,8},{8,7},{9,10},{10,9},{11,... | collective-permute-start | bytes 147464 | tf_op jit(solution)/shard_map/ppermute | solution.py:310
  56.5 11.1 %collective-permute-start.6 = (f32[24,4,128]{2,1,0:T(4,128)S(1)}, f32[24,4,128]{2,1,0:T(4,128)S(1)}, u32[]{:S(2)}, u32[]{:S(2)}) collective-permute-start(f32[24,4,128]{2,1,0:T(4,128)S(1)} %constant_dynamic-update-slice_fusion.middle), channel_id=1, source_target_pairs={{0,1},{1,0},{2,3},{3,2},{4,5},{5,4},{6,7},{7,6},{8,9},{9,8},{10,11... | collective-permute-start | bytes 147464 | tf_op jit(solution)/shard_map/ppermute | solution.py:310
  70.5 12.5 %collective-permute-start.9 = (f32[8,4,128]{2,1,0:T(4,128)S(1)}, f32[8,4,128]{2,1,0:T(4,128)S(1)}, u32[]{:S(2)}, u32[]{:S(2)}) collective-permute-start(f32[8,4,128]{2,1,0:T(4,128)S(1)} %get-tuple-element.62), channel_id=1, source_target_pairs={{32,64},{64,32},{96,128},{128,96},{160,192},{192,160},{224,256},{2... | collective-permute-start | bytes 49160 | tf_op jit(solution)/shard_map/ppermute | solution.py:310
  72.4 9.5 %collective-permute-start.8 = (f32[8,4,128]{2,1,0:T(4,128)S(1)}, f32[8,4,128]{2,1,0:T(4,128)S(1)}, u32[]{:S(2)}, u32[]{:S(2)}) collective-permute-start(f32[8,4,128]{2,1,0:T(4,128)S(1)} %get-tuple-element.62), channel_id=1, source_target_pairs={{0,32},{32,0},{64,96},{96,64},{128,160},{160,128},{192,224},{224,1... | collective-permute-start | bytes 49160 | tf_op jit(solution)/shard_map/ppermute | solution.py:310
  83.0 13.8 %collective-permute-start.11 = (f32[24,4,128]{2,1,0:T(4,128)S(1)}, f32[24,4,128]{2,1,0:T(4,128)S(1)}, u32[]{:S(2)}, u32[]{:S(2)}) collective-permute-start(f32[24,4,128]{2,1,0:T(4,128)S(1)} %constant_dynamic-update-slice_fusion.3.middle), channel_id=1, source_target_pairs={{1,2},{2,1},{3,4},{4,3},{5,6},{6,5},{7,8},{8,7},{9,10},{10,9},{11,... | collective-permute-start | bytes 147464 | tf_op jit(solution)/shard_map/ppermute | solution.py:310
  84.9 11.9 %collective-permute-start.10 = (f32[24,4,128]{2,1,0:T(4,128)S(1)}, f32[24,4,128]{2,1,0:T(4,128)S(1)}, u32[]{:S(2)}, u32[]{:S(2)}) collective-permute-start(f32[24,4,128]{2,1,0:T(4,128)S(1)} %constant_dynamic-update-slice_fusion.3.middle), channel_id=1, source_target_pairs={{0,1},{1,0},{2,3},{3,2},{4,5},{5,4},{6,7},{7,6},{8,9},{9,8},{10,11... | collective-permute-start | bytes 147464 | tf_op jit(solution)/shard_map/ppermute | solution.py:310
  99.7 15.4 %collective-permute-start.13 = (f32[8,4,128]{2,1,0:T(4,128)S(1)}, f32[8,4,128]{2,1,0:T(4,128)S(1)}, u32[]{:S(2)}, u32[]{:S(2)}) collective-permute-start(f32[8,4,128]{2,1,0:T(4,128)S(1)} %get-tuple-element.71), channel_id=1, source_target_pairs={{32,64},{64,32},{96,128},{128,96},{160,192},{192,160},{224,256},{2... | collective-permute-start | bytes 49160 | tf_op jit(solution)/shard_map/ppermute | solution.py:310
  105.6 9.5 %collective-permute-start.12 = (f32[8,4,128]{2,1,0:T(4,128)S(1)}, f32[8,4,128]{2,1,0:T(4,128)S(1)}, u32[]{:S(2)}, u32[]{:S(2)}) collective-permute-start(f32[8,4,128]{2,1,0:T(4,128)S(1)} %get-tuple-element.71), channel_id=1, source_target_pairs={{0,32},{32,0},{64,96},{96,64},{128,160},{160,128},{192,224},{224,1... | collective-permute-start | bytes 49160 | tf_op jit(solution)/shard_map/ppermute | solution.py:310
  115.2 16.1 %collective-permute-start.15 = (f32[24,4,128]{2,1,0:T(4,128)S(1)}, f32[24,4,128]{2,1,0:T(4,128)S(1)}, u32[]{:S(2)}, u32[]{:S(2)}) collective-permute-start(f32[24,4,128]{2,1,0:T(4,128)S(1)} %constant_dynamic-update-slice_fusion.6.middle), channel_id=1, source_target_pairs={{1,2},{2,1},{3,4},{4,3},{5,6},{6,5},{7,8},{8,7},{9,10},{10,9},{11,... | collective-permute-start | bytes 147464 | tf_op jit(solution)/shard_map/ppermute | solution.py:310
  120.2 11.1 %collective-permute-start.14 = (f32[24,4,128]{2,1,0:T(4,128)S(1)}, f32[24,4,128]{2,1,0:T(4,128)S(1)}, u32[]{:S(2)}, u32[]{:S(2)}) collective-permute-start(f32[24,4,128]{2,1,0:T(4,128)S(1)} %constant_dynamic-update-slice_fusion.6.middle), channel_id=1, source_target_pairs={{0,1},{1,0},{2,3},{3,2},{4,5},{5,4},{6,7},{7,6},{8,9},{9,8},{10,11... | collective-permute-start | bytes 147464 | tf_op jit(solution)/shard_map/ppermute | solution.py:310

commit v4 on v3

--- a/solution.py
+++ b/solution.py
@@ -13,7 +13,7 @@
 POOL = LEAVES + 9 * GHOSTS
 FEATURES = 32
 SUMS = 16
-GROUP = 8
+GROUP = 16
 UNROLL = 8
 
 soften_sq = 0.04
@@ -150,7 +150,7 @@
 def group_moved(lists, sources, moments, own, speeds, kicks, leaves):
     records = [own[leaf] for leaf in leaves]
     totals = []
-    for k in range(0, GROUP, 2):
+    for k in range(0, len(leaves), 2):
         totals += pair_sums(lists, sources, moments, leaves[k : k + 2], records[k : k + 2])
     return [
         moved(total, record, speeds[leaf], kicks[leaf])

time: 148 us -> 151 us (1.020)
  the two profiles are of different devices: /device:TPU:0 before, /device:TPU:2 now
where the time goes in v4:
time: 151 us; the launch traced here: 153 us
  Pallas kernels  73.2 us (48%)
  starting transfers between devices  69 us (46%)
  local copies, waits for them, and re-layouts  5.85 us (4%)
  waiting for transfers between devices  2.73 us (2%)
  between operations  1.69 us (1%)
    pallas_call x13, Pallas kernels, call(): pl.pallas_call(kernel, out_shape=outs, in_specs=[SMEM] * len(scalars) + [...  73.2 us
    ppermute x16, starting transfers between devices, swapped(): return lax.ppermute(block, axis, route)  69 us
    unnamed x24, local copies, waits for them, and re-layouts  5.83 us
  transfers between devices with their start and end apart: 16, of which 2 were waited for; matrix products, arithmetic and copies ran while one was open for 0% of the time, Pallas kernels for 32%

profile of v4, /device:TPU:2, one launch (start us, length us, event | category | flops | bytes accessed | tf_op | source)
XLA Modules:
  0.0 152.6 jit_solution(6432187321741185036)
XLA Ops:
  0.7 0.9 copy-done
  3.5 3.4 %collective-permute-start.1 = (f32[8,4,128]{2,1,0:T(4,128)S(1)}, f32[8,4,128]{2,1,0:T(4,128)S(1)}, u32[]{:S(2)}, u32[]{:S(2)}) collective-permute-start(f32[8,4,128]{2,1,0:T(4,128)S(1)} %choose.1), channel_id=1, source_target_pairs={{32,64},{64,32},{96,128},{128,96},{160,192},{192,160},{224,256},{2... | collective-permute-start | bytes 49160 | tf_op jit(solution)/shard_map/ppermute | solution.py:310
  6.9 14.0 %collective-permute-start = (f32[8,4,128]{2,1,0:T(4,128)S(1)}, f32[8,4,128]{2,1,0:T(4,128)S(1)}, u32[]{:S(2)}, u32[]{:S(2)}) collective-permute-start(f32[8,4,128]{2,1,0:T(4,128)S(1)} %choose.1), channel_id=1, source_target_pairs={{0,32},{32,0},{64,96},{96,64},{128,160},{160,128},{192,224},{224,1... | collective-permute-start | bytes 49160 | tf_op jit(solution)/shard_map/ppermute | solution.py:310
  21.8 0.9 copy-done.2
  22.7 0.9 copy-done.3
  24.4 1.3 open.1
  25.8 11.8 %collective-permute-start.3 = (f32[24,4,128]{2,1,0:T(4,128)S(1)}, f32[24,4,128]{2,1,0:T(4,128)S(1)}, u32[]{:S(2)}, u32[]{:S(2)}) collective-permute-start(f32[24,4,128]{2,1,0:T(4,128)S(1)} %pad_maximum_fusion.middle), channel_id=1, source_target_pairs={{1,2},{2,1},{3,4},{4,3},{5,6},{6,5},{7,8},{8,7},{9,10},{10,9},{11,... | collective-permute-start | bytes 147464 | tf_op jit(solution)/shard_map/ppermute | solution.py:310
  37.6 1.9 %collective-permute-start.2 = (f32[24,4,128]{2,1,0:T(4,128)S(1)}, f32[24,4,128]{2,1,0:T(4,128)S(1)}, u32[]{:S(2)}, u32[]{:S(2)}) collective-permute-start(f32[24,4,128]{2,1,0:T(4,128)S(1)} %pad_maximum_fusion.middle), channel_id=1, source_target_pairs={{0,1},{1,0},{2,3},{3,2},{4,5},{5,4},{6,7},{7,6},{8,9},{9,8},{10,11... | collective-permute-start | bytes 147464 | tf_op jit(solution)/shard_map/ppermute | solution.py:310
  41.2 2.9 %ghost.3 = (bf16[136,128,128]{2,1,0:T(8,128)(2,1)S(1)}, bf16[136,16,128]{2,1,0:T(8,128)(2,1)S(1)}, f32[8,4,128]{2,1,0:T(4,128)S(1)}) custom-call(s32[8,64]{1,0:T(8,128)S(1)} %copy-done.6, s32[8]{0:T(128)S(1)} %copy-done.8, s32[2]{0:T(128)S(1)} %and_select_fusion.parity, ...), custom_call_target="tpu_custom_call", output_to_operand_aliasing={{0}: (8, {}), {1}: (9, {})} | custom-call | flops 314572800 | bytes 1048576 | tf_op jit(solution)/shard_map/ghost/pallas_call | solution.py:291
  44.0 1.9 %collective-permute-start.5 = (f32[8,4,128]{2,1,0:T(4,128)S(1)}, f32[8,4,128]{2,1,0:T(4,128)S(1)}, u32[]{:S(2)}, u32[]{:S(2)}) collective-permute-start(f32[8,4,128]{2,1,0:T(4,128)S(1)} %get-tuple-element.53), channel_id=1, source_target_pairs={{32,64},{64,32},{96,128},{128,96},{160,192},{192,160},{224,256},{2... | collective-permute-start | bytes 49160 | tf_op jit(solution)/shard_map/ppermute | solution.py:310
  46.0 5.6 %collective-permute-start.4 = (f32[8,4,128]{2,1,0:T(4,128)S(1)}, f32[8,4,128]{2,1,0:T(4,128)S(1)}, u32[]{:S(2)}, u32[]{:S(2)}) collective-permute-start(f32[8,4,128]{2,1,0:T(4,128)S(1)} %get-tuple-element.53), channel_id=1, source_target_pairs={{0,32},{32,0},{64,96},{96,64},{128,160},{160,128},{192,224},{224,1... | collective-permute-start | bytes 49160 | tf_op jit(solution)/shard_map/ppermute | solution.py:310
  51.6 7.0 %early.3 = (f32[64,4,128]{2,1,0:T(4,128)S(1)}, f32[64,4,128]{2,1,0:T(4,128)S(1)}) custom-call(s32[8,64]{1,0:T(8,128)S(1)} %copy-done.6, s32[1]{0:T(128)S(6)} %copy.71.count, f32[64,4,128]{2,1,0:T(4,128)S(1)} %get-tuple-element.41.own, f32[64,4,128]{2,1,0:T(4,128)S(1)} %get-tuple-element.42.speeds, ...), custom_call_target="tpu_custom_call", output_to_operand_aliasing={{0}: (2, {}), {1}: (3, {})} | custom-call | flops 1258291200 | bytes 1048576 | tf_op jit(solution)/shard_map/early/pallas_call | solution.py:291
  58.6 3.4 %collective-permute-start.7 = (f32[24,4,128]{2,1,0:T(4,128)S(1)}, f32[24,4,128]{2,1,0:T(4,128)S(1)}, u32[]{:S(2)}, u32[]{:S(2)}) collective-permute-start(f32[24,4,128]{2,1,0:T(4,128)S(1)} %constant_dynamic-update-slice_fusion.middle), channel_id=1, source_target_pairs={{1,2},{2,1},{3,4},{4,3},{5,6},{6,5},{7,8},{8,7},{9,10},{10,9},{11,... | collective-permute-start | bytes 147464 | tf_op jit(solution)/shard_map/ppermute | solution.py:310
  62.0 1.9 %collective-permute-start.6 = (f32[24,4,128]{2,1,0:T(4,128)S(1)}, f32[24,4,128]{2,1,0:T(4,128)S(1)}, u32[]{:S(2)}, u32[]{:S(2)}) collective-permute-start(f32[24,4,128]{2,1,0:T(4,128)S(1)} %constant_dynamic-update-slice_fusion.middle), channel_id=1, source_target_pairs={{0,1},{1,0},{2,3},{3,2},{4,5},{5,4},{6,7},{7,6},{8,9},{9,8},{10,11... | collective-permute-start | bytes 147464 | tf_op jit(solution)/shard_map/ppermute | solution.py:310
  63.9 8.8 %late.3 = (f32[64,4,128]{2,1,0:T(4,128)S(1)}, f32[64,4,128]{2,1,0:T(4,128)S(1)}, bf16[136,128,128]{2,1,0:T(8,128)(2,1)S(1)}, bf16[136,16,128]{2,1,0:T(8,128)(2,1)S(1)}) custom-call(s32[8,64]{1,0:T(8,128)S(1)} %copy-done.6, s32[2]{0:T(128)S(1)} %and_select_fusion.parity, ...), custom_call_target="tpu_custom_call", output_to_operand_aliasing={{0}: (3, {}), {1}: (4, {}), {2}: (7, {}), {3}: (8, {})} | custom-call | flops 1258291200 | bytes 1048576 | tf_op jit(solution)/shard_map/late/pallas_call | solution.py:291
  72.8 2.9 %ghost.4 = (bf16[136,128,128]{2,1,0:T(8,128)(2,1)S(1)}, bf16[136,16,128]{2,1,0:T(8,128)(2,1)S(1)}, f32[8,4,128]{2,1,0:T(4,128)S(1)}) custom-call(s32[8,64]{1,0:T(8,128)S(1)} %copy-done.6, s32[8]{0:T(128)S(1)} %copy-done.8, s32[2]{0:T(128)S(1)} %and_select_fusion.parity, ...), custom_call_target="tpu_custom_call", output_to_operand_aliasing={{0}: (8, {}), {1}: (9, {})} | custom-call | flops 314572800 | bytes 1048576 | tf_op jit(solution)/shard_map/ghost/pallas_call | solution.py:291
  75.6 1.9 %collective-permute-start.9 = (f32[8,4,128]{2,1,0:T(4,128)S(1)}, f32[8,4,128]{2,1,0:T(4,128)S(1)}, u32[]{:S(2)}, u32[]{:S(2)}) collective-permute-start(f32[8,4,128]{2,1,0:T(4,128)S(1)} %get-tuple-element.62), channel_id=1, source_target_pairs={{32,64},{64,32},{96,128},{128,96},{160,192},{192,160},{224,256},{2... | collective-permute-start | bytes 49160 | tf_op jit(solution)/shard_map/ppermute | solution.py:310
  77.6 7.1 %collective-permute-start.8 = (f32[8,4,128]{2,1,0:T(4,128)S(1)}, f32[8,4,128]{2,1,0:T(4,128)S(1)}, u32[]{:S(2)}, u32[]{:S(2)}) collective-permute-start(f32[8,4,128]{2,1,0:T(4,128)S(1)} %get-tuple-element.62), channel_id=1, source_target_pairs={{0,32},{32,0},{64,96},{96,64},{128,160},{160,128},{192,224},{224,1... | collective-permute-start | bytes 49160 | tf_op jit(solution)/shard_map/ppermute | solution.py:310
  84.6 7.0 %early.4 = (f32[64,4,128]{2,1,0:T(4,128)S(1)}, f32[64,4,128]{2,1,0:T(4,128)S(1)}) custom-call(s32[8,64]{1,0:T(8,128)S(1)} %copy-done.6, s32[1]{0:T(128)S(6)} %copy.71.count, f32[64,4,128]{2,1,0:T(4,128)S(1)} %get-tuple-element.54.own, f32[64,4,128]{2,1,0:T(4,128)S(1)} %get-tuple-element.55.speeds, ...), custom_call_target="tpu_custom_call", output_to_operand_aliasing={{0}: (2, {}), {1}: (3, {})} | custom-call | flops 1258291200 | bytes 1048576 | tf_op jit(solution)/shard_map/early/pallas_call | solution.py:291
  91.7 1.9 %collective-permute-start.11 = (f32[24,4,128]{2,1,0:T(4,128)S(1)}, f32[24,4,128]{2,1,0:T(4,128)S(1)}, u32[]{:S(2)}, u32[]{:S(2)}) collective-permute-start(f32[24,4,128]{2,1,0:T(4,128)S(1)} %constant_dynamic-update-slice_fusion.3.middle), channel_id=1, source_target_pairs={{1,2},{2,1},{3,4},{4,3},{5,6},{6,5},{7,8},{8,7},{9,10},{10,9},{11,... | collective-permute-start | bytes 147464 | tf_op jit(solution)/shard_map/ppermute | solution.py:310
  93.6 1.9 %collective-permute-start.10 = (f32[24,4,128]{2,1,0:T(4,128)S(1)}, f32[24,4,128]{2,1,0:T(4,128)S(1)}, u32[]{:S(2)}, u32[]{:S(2)}) collective-permute-start(f32[24,4,128]{2,1,0:T(4,128)S(1)} %constant_dynamic-update-slice_fusion.3.middle), channel_id=1, source_target_pairs={{0,1},{1,0},{2,3},{3,2},{4,5},{5,4},{6,7},{7,6},{8,9},{9,8},{10,11... | collective-permute-start | bytes 147464 | tf_op jit(solution)/shard_map/ppermute | solution.py:310
  95.6 8.6 %late.4 = (f32[64,4,128]{2,1,0:T(4,128)S(1)}, f32[64,4,128]{2,1,0:T(4,128)S(1)}, bf16[136,128,128]{2,1,0:T(8,128)(2,1)S(1)}, bf16[136,16,128]{2,1,0:T(8,128)(2,1)S(1)}) custom-call(s32[8,64]{1,0:T(8,128)S(1)} %copy-done.6, s32[2]{0:T(128)S(1)} %and_select_fusion.parity, ...), custom_call_target="tpu_custom_call", output_to_operand_aliasing={{0}: (3, {}), {1}: (4, {}), {2}: (7, {}), {3}: (8, {})} | custom-call | flops 1258291200 | bytes 1048576 | tf_op jit(solution)/shard_map/late/pallas_call | solution.py:291
  104.2 1.3 collective-permute-done.11.far
  105.5 2.9 %ghost.5 = (bf16[136,128,128]{2,1,0:T(8,128)(2,1)S(1)}, bf16[136,16,128]{2,1,0:T(8,128)(2,1)S(1)}, f32[8,4,128]{2,1,0:T(4,128)S(1)}) custom-call(s32[8,64]{1,0:T(8,128)S(1)} %copy-done.6, s32[8]{0:T(128)S(1)} %copy-done.8, s32[2]{0:T(128)S(1)} %and_select_fusion.parity, ...), custom_call_target="tpu_custom_call", output_to_operand_aliasing={{0}: (8, {}), {1}: (9, {})} | custom-call | flops 314572800 | bytes 1048576 | tf_op jit(solution)/shard_map/ghost/pallas_call | solution.py:291
  108.4 1.9 %collective-permute-start.13 = (f32[8,4,128]{2,1,0:T(4,128)S(1)}, f32[8,4,128]{2,1,0:T(4,128)S(1)}, u32[]{:S(2)}, u32[]{:S(2)}) collective-permute-start(f32[8,4,128]{2,1,0:T(4,128)S(1)} %get-tuple-element.71), channel_id=1, source_target_pairs={{32,64},{64,32},{96,128},{128,96},{160,192},{192,160},{224,256},{2... | collective-permute-start | bytes 49160 | tf_op jit(solution)/shard_map/ppermute | solution.py:310
  110.3 6.5 %collective-permute-start.12 = (f32[8,4,128]{2,1,0:T(4,128)S(1)}, f32[8,4,128]{2,1,0:T(4,128)S(1)}, u32[]{:S(2)}, u32[]{:S(2)}) collective-permute-start(f32[8,4,128]{2,1,0:T(4,128)S(1)} %get-tuple-element.71), channel_id=1, source_target_pairs={{0,32},{32,0},{64,96},{96,64},{128,160},{160,128},{192,224},{224,1... | collective-permute-start | bytes 49160 | tf_op jit(solution)/shard_map/ppermute | solution.py:310
  116.8 7.2 %early.5 = (f32[64,4,128]{2,1,0:T(4,128)S(1)}, f32[64,4,128]{2,1,0:T(4,128)S(1)}) custom-call(s32[8,64]{1,0:T(8,128)S(1)} %copy-done.6, s32[1]{0:T(128)S(6)} %copy.71.count, f32[64,4,128]{2,1,0:T(4,128)S(1)} %get-tuple-element.63.own, f32[64,4,128]{2,1,0:T(4,128)S(1)} %get-tuple-element.64.speeds, ...), custom_call_target="tpu_custom_call", output_to_operand_aliasing={{0}: (2, {}), {1}: (3, {})} | custom-call | flops 1258291200 | bytes 1048576 | tf_op jit(solution)/shard_map/early/pallas_call | solution.py:291
  124.1 1.9 %collective-permute-start.15 = (f32[24,4,128]{2,1,0:T(4,128)S(1)}, f32[24,4,128]{2,1,0:T(4,128)S(1)}, u32[]{:S(2)}, u32[]{:S(2)}) collective-permute-start(f32[24,4,128]{2,1,0:T(4,128)S(1)} %constant_dynamic-update-slice_fusion.6.middle), channel_id=1, source_target_pairs={{1,2},{2,1},{3,4},{4,3},{5,6},{6,5},{7,8},{8,7},{9,10},{10,9},{11,... | collective-permute-start | bytes 147464 | tf_op jit(solution)/shard_map/ppermute | solution.py:310
  126.0 1.9 %collective-permute-start.14 = (f32[24,4,128]{2,1,0:T(4,128)S(1)}, f32[24,4,128]{2,1,0:T(4,128)S(1)}, u32[]{:S(2)}, u32[]{:S(2)}) collective-permute-start(f32[24,4,128]{2,1,0:T(4,128)S(1)} %constant_dynamic-update-slice_fusion.6.middle), channel_id=1, source_target_pairs={{0,1},{1,0},{2,3},{3,2},{4,5},{5,4},{6,7},{7,6},{8,9},{9,8},{10,11... | collective-permute-start | bytes 147464 | tf_op jit(solution)/shard_map/ppermute | solution.py:310
  128.0 8.6 %late.5 = (f32[64,4,128]{2,1,0:T(4,128)S(1)}, f32[64,4,128]{2,1,0:T(4,128)S(1)}, bf16[136,128,128]{2,1,0:T(8,128)(2,1)S(1)}, bf16[136,16,128]{2,1,0:T(8,128)(2,1)S(1)}) custom-call(s32[8,64]{1,0:T(8,128)S(1)} %copy-done.6, s32[2]{0:T(128)S(1)} %and_select_fusion.parity, ...), custom_call_target="tpu_custom_call", output_to_operand_aliasing={{0}: (3, {}), {1}: (4, {}), {2}: (7, {}), {3}: (8, {})} | custom-call | flops 1258291200 | bytes 1048576 | tf_op jit(solution)/shard_map/late/pallas_call | solution.py:291
  136.6 1.3 collective-permute-done.15.far
  137.9 14.6 %last.1 = (f32[3,8192]{1,0:T(4,128)}, f32[3,8192]{1,0:T(4,128)}, bf16[136,128,128]{2,1,0:T(8,128)(2,1)S(1)}, bf16[136,16,128]{2,1,0:T(8,128)(2,1)S(1)}) custom-call(s32[8,64]{1,0:T(8,128)S(1)} %copy-done.6, s32[2]{0:T(128)S(1)} %and_select_fusion.parity, s32[1]{0:T(128)S(6)} %copy.71.count, ...), custom_call_target="tpu_custom_call", output_to_operand_aliasing={{2}: (8, {}), {3}: (9, {})} | custom-call | flops 2516582400 | bytes 1048576 | tf_op jit(solution)/shard_map/last/pallas_call | solution.py:291
  (42 shorter events, 4.7 us)
Async XLA Ops:
  0.6 40.5 %copy-start.8 = (s32[8]{0:T(128)S(1)}, s32[8]{0:T(128)}, u32[]{:S(2)}) copy-start(s32[8]{0:T(128)} %ids.7) | copy-start | bytes 100
  0.6 0.9 copy-start
  1.6 0.8 copy-start.4
  2.3 0.7 copy-start.7
  3.0 38.2 %copy-start.6 = (s32[8,64]{1,0:T(8,128)S(1)}, s32[8,64]{1,0:T(8,128)}, u32[]{:S(2)}) copy-start(s32[8,64]{1,0:T(8,128)} %lists.19) | copy-start | bytes 6148
  3.5 22.2 %collective-permute-start.1 = (f32[8,4,128]{2,1,0:T(4,128)S(1)}, f32[8,4,128]{2,1,0:T(4,128)S(1)}, u32[]{:S(2)}, u32[]{:S(2)}) collective-permute-start(f32[8,4,128]{2,1,0:T(4,128)S(1)} %choose.1), channel_id=1, source_target_pairs={{32,64},{64,32},{96,128},{128,96},{160,192},{192,160},{224,256},{2... | collective-permute-start | bytes 49160 | tf_op jit(solution)/shard_map/ppermute | solution.py:310
  6.9 18.8 %collective-permute-start = (f32[8,4,128]{2,1,0:T(4,128)S(1)}, f32[8,4,128]{2,1,0:T(4,128)S(1)}, u32[]{:S(2)}, u32[]{:S(2)}) collective-permute-start(f32[8,4,128]{2,1,0:T(4,128)S(1)} %choose.1), channel_id=1, source_target_pairs={{0,32},{32,0},{64,96},{96,64},{128,160},{160,128},{192,224},{224,1... | collective-permute-start | bytes 49160 | tf_op jit(solution)/shard_map/ppermute | solution.py:310
  20.9 0.9 copy-start.1
  21.8 0.9 copy-start.2
  22.7 0.9 copy-start.3
  23.6 0.8 copy-start.5
  25.8 15.4 %collective-permute-start.3 = (f32[24,4,128]{2,1,0:T(4,128)S(1)}, f32[24,4,128]{2,1,0:T(4,128)S(1)}, u32[]{:S(2)}, u32[]{:S(2)}) collective-permute-start(f32[24,4,128]{2,1,0:T(4,128)S(1)} %pad_maximum_fusion.middle), channel_id=1, source_target_pairs={{1,2},{2,1},{3,4},{4,3},{5,6},{6,5},{7,8},{8,7},{9,10},{10,9},{11,... | collective-permute-start | bytes 147464 | tf_op jit(solution)/shard_map/ppermute | solution.py:310
  37.6 3.5 %collective-permute-start.2 = (f32[24,4,128]{2,1,0:T(4,128)S(1)}, f32[24,4,128]{2,1,0:T(4,128)S(1)}, u32[]{:S(2)}, u32[]{:S(2)}) collective-permute-start(f32[24,4,128]{2,1,0:T(4,128)S(1)} %pad_maximum_fusion.middle), channel_id=1, source_target_pairs={{0,1},{1,0},{2,3},{3,2},{4,5},{5,4},{6,7},{7,6},{8,9},{9,8},{10,11... | collective-permute-start | bytes 147464 | tf_op jit(solution)/shard_map/ppermute | solution.py:310
  44.0 14.6 %collective-permute-start.5 = (f32[8,4,128]{2,1,0:T(4,128)S(1)}, f32[8,4,128]{2,1,0:T(4,128)S(1)}, u32[]{:S(2)}, u32[]{:S(2)}) collective-permute-start(f32[8,4,128]{2,1,0:T(4,128)S(1)} %get-tuple-element.53), channel_id=1, source_target_pairs={{32,64},{64,32},{96,128},{128,96},{160,192},{192,160},{224,256},{2... | collective-permute-start | bytes 49160 | tf_op jit(solution)/shard_map/ppermute | solution.py:310
  46.0 12.6 %collective-permute-start.4 = (f32[8,4,128]{2,1,0:T(4,128)S(1)}, f32[8,4,128]{2,1,0:T(4,128)S(1)}, u32[]{:S(2)}, u32[]{:S(2)}) collective-permute-start(f32[8,4,128]{2,1,0:T(4,128)S(1)} %get-tuple-element.53), channel_id=1, source_target_pairs={{0,32},{32,0},{64,96},{96,64},{128,160},{160,128},{192,224},{224,1... | collective-permute-start | bytes 49160 | tf_op jit(solution)/shard_map/ppermute | solution.py:310
  58.6 14.1 %collective-permute-start.7 = (f32[24,4,128]{2,1,0:T(4,128)S(1)}, f32[24,4,128]{2,1,0:T(4,128)S(1)}, u32[]{:S(2)}, u32[]{:S(2)}) collective-permute-start(f32[24,4,128]{2,1,0:T(4,128)S(1)} %constant_dynamic-update-slice_fusion.middle), channel_id=1, source_target_pairs={{1,2},{2,1},{3,4},{4,3},{5,6},{6,5},{7,8},{8,7},{9,10},{10,9},{11,... | collective-permute-start | bytes 147464 | tf_op jit(solution)/shard_map/ppermute | solution.py:310
  62.0 10.7 %collective-permute-start.6 = (f32[24,4,128]{2,1,0:T(4,128)S(1)}, f32[24,4,128]{2,1,0:T(4,128)S(1)}, u32[]{:S(2)}, u32[]{:S(2)}) collective-permute-start(f32[24,4,128]{2,1,0:T(4,128)S(1)} %constant_dynamic-update-slice_fusion.middle), channel_id=1, source_target_pairs={{0,1},{1,0},{2,3},{3,2},{4,5},{5,4},{6,7},{7,6},{8,9},{9,8},{10,11... | collective-permute-start | bytes 147464 | tf_op jit(solution)/shard_map/ppermute | solution.py:310
  75.6 16.1 %collective-permute-start.9 = (f32[8,4,128]{2,1,0:T(4,128)S(1)}, f32[8,4,128]{2,1,0:T(4,128)S(1)}, u32[]{:S(2)}, u32[]{:S(2)}) collective-permute-start(f32[8,4,128]{2,1,0:T(4,128)S(1)} %get-tuple-element.62), channel_id=1, source_target_pairs={{32,64},{64,32},{96,128},{128,96},{160,192},{192,160},{224,256},{2... | collective-permute-start | bytes 49160 | tf_op jit(solution)/shard_map/ppermute | solution.py:310
  77.6 14.1 %collective-permute-start.8 = (f32[8,4,128]{2,1,0:T(4,128)S(1)}, f32[8,4,128]{2,1,0:T(4,128)S(1)}, u32[]{:S(2)}, u32[]{:S(2)}) collective-permute-start(f32[8,4,128]{2,1,0:T(4,128)S(1)} %get-tuple-element.62), channel_id=1, source_target_pairs={{0,32},{32,0},{64,96},{96,64},{128,160},{160,128},{192,224},{224,1... | collective-permute-start | bytes 49160 | tf_op jit(solution)/shard_map/ppermute | solution.py:310
  91.7 13.8 %collective-permute-start.11 = (f32[24,4,128]{2,1,0:T(4,128)S(1)}, f32[24,4,128]{2,1,0:T(4,128)S(1)}, u32[]{:S(2)}, u32[]{:S(2)}) collective-permute-start(f32[24,4,128]{2,1,0:T(4,128)S(1)} %constant_dynamic-update-slice_fusion.3.middle), channel_id=1, source_target_pairs={{1,2},{2,1},{3,4},{4,3},{5,6},{6,5},{7,8},{8,7},{9,10},{10,9},{11,... | collective-permute-start | bytes 147464 | tf_op jit(solution)/shard_map/ppermute | solution.py:310
  93.6 11.9 %collective-permute-start.10 = (f32[24,4,128]{2,1,0:T(4,128)S(1)}, f32[24,4,128]{2,1,0:T(4,128)S(1)}, u32[]{:S(2)}, u32[]{:S(2)}) collective-permute-start(f32[24,4,128]{2,1,0:T(4,128)S(1)} %constant_dynamic-update-slice_fusion.3.middle), channel_id=1, source_target_pairs={{0,1},{1,0},{2,3},{3,2},{4,5},{5,4},{6,7},{7,6},{8,9},{9,8},{10,11... | collective-permute-start | bytes 147464 | tf_op jit(solution)/shard_map/ppermute | solution.py:310
  108.4 15.7 %collective-permute-start.13 = (f32[8,4,128]{2,1,0:T(4,128)S(1)}, f32[8,4,128]{2,1,0:T(4,128)S(1)}, u32[]{:S(2)}, u32[]{:S(2)}) collective-permute-start(f32[8,4,128]{2,1,0:T(4,128)S(1)} %get-tuple-element.71), channel_id=1, source_target_pairs={{32,64},{64,32},{96,128},{128,96},{160,192},{192,160},{224,256},{2... | collective-permute-start | bytes 49160 | tf_op jit(solution)/shard_map/ppermute | solution.py:310
  110.3 13.7 %collective-permute-start.12 = (f32[8,4,128]{2,1,0:T(4,128)S(1)}, f32[8,4,128]{2,1,0:T(4,128)S(1)}, u32[]{:S(2)}, u32[]{:S(2)}) collective-permute-start(f32[8,4,128]{2,1,0:T(4,128)S(1)} %get-tuple-element.71), channel_id=1, source_target_pairs={{0,32},{32,0},{64,96},{96,64},{128,160},{160,128},{192,224},{224,1... | collective-permute-start | bytes 49160 | tf_op jit(solution)/shard_map/ppermute | solution.py:310
  124.1 13.8 %collective-permute-start.15 = (f32[24,4,128]{2,1,0:T(4,128)S(1)}, f32[24,4,128]{2,1,0:T(4,128)S(1)}, u32[]{:S(2)}, u32[]{:S(2)}) collective-permute-start(f32[24,4,128]{2,1,0:T(4,128)S(1)} %constant_dynamic-update-slice_fusion.6.middle), channel_id=1, source_target_pairs={{1,2},{2,1},{3,4},{4,3},{5,6},{6,5},{7,8},{8,7},{9,10},{10,9},{11,... | collective-permute-start | bytes 147464 | tf_op jit(solution)/shard_map/ppermute | solution.py:310
  126.0 11.9 %collective-permute-start.14 = (f32[24,4,128]{2,1,0:T(4,128)S(1)}, f32[24,4,128]{2,1,0:T(4,128)S(1)}, u32[]{:S(2)}, u32[]{:S(2)}) collective-permute-start(f32[24,4,128]{2,1,0:T(4,128)S(1)} %constant_dynamic-update-slice_fusion.6.middle), channel_id=1, source_target_pairs={{0,1},{1,0},{2,3},{3,2},{4,5},{5,4},{6,7},{7,6},{8,9},{9,8},{10,11... | collective-permute-start | bytes 147464 | tf_op jit(solution)/shard_map/ppermute | solution.py:310

commit v5 on v4

--- a/solution.py
+++ b/solution.py
@@ -15,6 +15,7 @@
 SUMS = 16
 GROUP = 16
 UNROLL = 8
+PLAIN_BELOW = 2000.0
 
 soften_sq = 0.04
 cutoff_sq = 9.0
@@ -30,9 +31,13 @@
     return first, second, (rest - second).astype(bf16).astype(f32)
 
 
+def norm(record):
+    square = record * record
+    return square[0:1] + square[1:2] + square[2:3]
+
+
 def norm_parts(record, more=0.0):
-    square = record * record
-    return three_parts(square[0:1] + square[1:2] + square[2:3] + more)
+    return three_parts(norm(record) + more)
 
 
 def with_row(parts, row):
@@ -89,19 +94,24 @@
     blank = jnp.zeros((LEAF - FEATURES, LEAF), f32)
     sources[slot] = jnp.concatenate([features, blank], axis=0).T.astype(bf16)
     moments[slot] = moment_rows(record)
-
-
-def enter_all(sources, moments, rows, slot_of, many):
-    def some(index, carry):
+    return norm(record)
+
+
+def enter_own(sources, moments, rows):
+    def some(index, peak):
         for u in range(UNROLL):
             row = index * UNROLL + u
-            enter(sources, moments, slot_of(row), rows[row])
-        return carry
-
-    lax.fori_loop(0, many // UNROLL, some, 0)
-
-
-def pair_sums(lists, sources, moments, leaves, records):
+            peak = jnp.maximum(peak, enter(sources, moments, row, rows[row]))
+        return peak
+
+    return lax.fori_loop(0, LEAVES // UNROLL, some, jnp.zeros((1, LEAF), f32))
+
+
+def is_plain(peak):
+    return jnp.max(peak) < PLAIN_BELOW
+
+
+def pair_sums(lists, sources, moments, leaves, records, plain):
     blank = jnp.zeros((FEATURES, LEAF), bf16)
     rest = jnp.zeros((LEAF - FEATURES, 2 * LEAF), bf16)
     first, second = (target_features(r).astype(bf16) for r in records)
@@ -122,8 +132,10 @@
     )
     weights, rows = [], []
     for n, pair in enumerate(slots):
-        near = jnp.maximum(apart[n * LEAF : (n + 1) * LEAF], soften_sq)
-        taper = jnp.maximum(cutoff_sq + soften_sq - near, 0.0)
+        near = jnp.minimum(apart[n * LEAF : (n + 1) * LEAF], cutoff_sq + soften_sq)
+        if not plain:
+            near = jnp.maximum(near, soften_sq)
+        taper = (cutoff_sq + soften_sq) - near
         inverse = lax.rsqrt(near)
         product = taper * inverse
         weight = product * product * inverse
@@ -147,28 +159,43 @@
     return record + time_step * speed, speed
 
 
-def group_moved(lists, sources, moments, own, speeds, kicks, leaves):
+def group_moved(lists, sources, moments, own, speeds, kicks, leaves, plain):
     records = [own[leaf] for leaf in leaves]
     totals = []
     for k in range(0, len(leaves), 2):
-        totals += pair_sums(lists, sources, moments, leaves[k : k + 2], records[k : k + 2])
+        totals += pair_sums(lists, sources, moments, leaves[k : k + 2], records[k : k + 2], plain)
     return [
         moved(total, record, speeds[leaf], kicks[leaf])
         for total, record, leaf in zip(totals, records, leaves)
     ]
 
 
-def move_groups(lists, count, sources, moments, own, speeds, kicks, new_own, new_speeds, begin, end):
+def for_groups(plain, begin, end, size, move):
     def group(index, carry):
-        leaves = [index * GROUP + u for u in range(GROUP)]
-        results = group_moved(lists, sources, moments, own, speeds, kicks, leaves)
+        move([index * size + u for u in range(size)], True)
+        return carry
+
+    def pair(index, carry):
+        move([index * 2, index * 2 + 1], False)
+        return carry
+
+    begin, end = jnp.int32(begin), jnp.int32(end)
+    halfway = jnp.where(plain, end, begin)
+    lax.fori_loop(begin, halfway, group, 0)
+    lax.fori_loop(halfway * (size // 2), end * (size // 2), pair, 0)
+
+
+def move_groups(
+    lists, count, peak, sources, moments, own, speeds, kicks, new_own, new_speeds, begin, end
+):
+    def move(leaves, plain):
+        results = group_moved(lists, sources, moments, own, speeds, kicks, leaves, plain)
         for leaf, (record, speed) in zip(leaves, results):
             live = leaf < count[0]
             new_own[leaf] = jnp.where(live, record, own[leaf])
             new_speeds[leaf] = jnp.where(live, speed, speeds[leaf])
-        return carry
-
-    lax.fori_loop(begin, end, group, 0)
+
+    for_groups(is_plain(peak[...]), begin, end, GROUP, move)
 
 
 def lanes(leaf):
@@ -184,42 +211,50 @@
         chosen[g] = first_record(positions, masses, ids[g])
 
 
-def open_kernel(positions, velocities, masses, long_kick, own, speeds, kicks, sources, moments):
+def open_kernel(
+    positions, velocities, masses, long_kick, own, speeds, kicks, sources, moments, peak
+):
     blank = jnp.zeros((1, LEAF), f32)
 
-    def some(index, carry):
+    def some(index, highest):
         for u in range(UNROLL):
             leaf = index * UNROLL + u
             record = first_record(positions, masses, leaf)
             own[leaf] = record
             speeds[leaf] = jnp.concatenate([velocities[:, lanes(leaf)], blank], axis=0)
             kicks[leaf] = jnp.concatenate([long_kick[:, lanes(leaf)], blank], axis=0)
-            enter(sources, moments, leaf, record)
-        return carry
-
-    lax.fori_loop(0, LEAVES // UNROLL, some, 0)
-
-
-def enter_ghosts(parity, sides, sources, moments):
+            highest = jnp.maximum(highest, enter(sources, moments, leaf, record))
+        return highest
+
+    peak[...] = lax.fori_loop(0, LEAVES // UNROLL, some, blank)
+
+
+def enter_ghosts(parity, sides, sources, moments, highest):
     for q, side in sides.items():
         b = jnp.where(parity[1] == 1, q, 2 - q)
         for p in range(3):
             a = jnp.where(parity[0] == 1, p, 2 - p)
             for g in range(GHOSTS):
-                enter(sources, moments, LEAVES + (a * 3 + b) * GHOSTS + g, side[p * GHOSTS + g])
+                slot = LEAVES + (a * 3 + b) * GHOSTS + g
+                highest = jnp.maximum(
+                    highest, enter(sources, moments, slot, side[p * GHOSTS + g])
+                )
+    return highest
 
 
 def ghost_kernel(
-    lists, ids, parity, own, speeds, kicks, near, far, old_sources, old_moments,
-    sources, moments, chosen,
-):
-    enter_ghosts(parity, {0: near, 2: far}, sources, moments)
-
-    results = group_moved(
-        lists, sources, moments, own, speeds, kicks, [ids[g] for g in range(GHOSTS)]
-    )
-    for g, (record, _) in enumerate(results):
-        chosen[g] = record
+    lists, ids, parity, own, speeds, kicks, near, far, old_peak, old_sources, old_moments,
+    sources, moments, chosen, peak,
+):
+    peak[...] = enter_ghosts(parity, {0: near, 2: far}, sources, moments, old_peak[...])
+
+    def move(places, plain):
+        leaves = [ids[g] for g in places]
+        results = group_moved(lists, sources, moments, own, speeds, kicks, leaves, plain)
+        for g, (record, _) in zip(places, results):
+            chosen[g] = record
+
+    for_groups(is_plain(peak[...]), 0, 1, GHOSTS, move)
 
 
 def groups_of(count):
@@ -227,45 +262,43 @@
 
 
 def early_kernel(
-    lists, count, own, speeds, kicks, sources, moments, new_own, new_speeds
+    lists, count, own, speeds, kicks, peak, sources, moments, new_own, new_speeds
 ):
     move_groups(
-        lists, count, sources, moments, own, speeds, kicks, new_own, new_speeds,
+        lists, count, peak, sources, moments, own, speeds, kicks, new_own, new_speeds,
         0, lax.div(groups_of(count), 2),
     )
 
 
-def middle_kernel(parity, middle, old_sources, old_moments, sources, moments):
-    enter_ghosts(parity, {1: middle}, sources, moments)
+def middle_kernel(parity, middle, old_peak, old_sources, old_moments, sources, moments, peak):
+    peak[...] = enter_ghosts(parity, {1: middle}, sources, moments, old_peak[...])
 
 
 def late_kernel(
-    lists, parity, count, own, speeds, kicks, middle, old_sources, old_moments,
-    new_own, new_speeds, sources, moments,
+    lists, parity, count, own, speeds, kicks, middle, old_peak, old_sources, old_moments,
+    new_own, new_speeds, sources, moments, peak,
 ):
     groups = groups_of(count)
     move_groups(
-        lists, count, sources, moments, own, speeds, kicks, new_own, new_speeds,
+        lists, count, old_peak, sources, moments, own, speeds, kicks, new_own, new_speeds,
         lax.div(groups, 2), groups,
     )
-    enter_all(sources, moments, new_own, lambda leaf: leaf, LEAVES)
-    enter_ghosts(parity, {1: middle}, sources, moments)
+    highest = enter_own(sources, moments, new_own)
+    peak[...] = enter_ghosts(parity, {1: middle}, sources, moments, highest)
 
 
 def last_kernel(
-    lists, parity, count, own, speeds, kicks, near, far, old_sources, old_moments,
+    lists, parity, count, own, speeds, kicks, near, far, old_peak, old_sources, old_moments,
     places, paces, sources, moments,
 ):
-    enter_ghosts(parity, {0: near, 2: far}, sources, moments)
-
-    def group(index, carry):
-        leaves = [index * GROUP + u for u in range(GROUP)]
-        results = group_moved(lists, sources, moments, own, speeds, kicks, leaves)
+    highest = enter_ghosts(parity, {0: near, 2: far}, sources, moments, old_peak[...])
+
+    def move(leaves, plain):
+        results = group_moved(lists, sources, moments, own, speeds, kicks, leaves, plain)
         for leaf, (record, speed) in zip(leaves, results):
             live = leaf < count[0]
             places[:, lanes(leaf)] = jnp.where(live, record, own[leaf])[:3]
             paces[:, lanes(leaf)] = jnp.where(live, speed, speeds[leaf])[:3]
-        return carry
 
     def keep(leaf, carry):
         places[:, lanes(leaf)] = own[leaf][:3]
@@ -273,7 +306,7 @@
         return carry
 
     groups = groups_of(count)
-    lax.fori_loop(0, groups, group, 0)
+    for_groups(is_plain(highest), 0, groups, GROUP, move)
     lax.fori_loop(groups * GROUP, LEAVES, keep, 0)
 
 
@@ -281,6 +314,7 @@
 SMEM = pl.BlockSpec(memory_space=pltpu.SMEM)
 record_shape = jax.ShapeDtypeStruct((LEAVES, 4, LEAF), f32)
 whole_shape = jax.ShapeDtypeStruct((3, LEAVES * LEAF), f32)
+peak_shape = jax.ShapeDtypeStruct((1, LEAF), f32)
 chosen_shape = jax.ShapeDtypeStruct((GHOSTS, 4, LEAF), f32)
 sources_shape = jax.ShapeDtypeStruct((POOL, LEAF, LEAF), bf16)
 moments_shape = jax.ShapeDtypeStruct((POOL, SUMS, LEAF), bf16)
@@ -316,16 +350,17 @@
 
     masses = masses[None]
     chosen = call(choose_kernel, "choose", (ids,), (positions, masses), chosen_shape)
-    own, speeds, kicks, sources, moments = call(
+    own, speeds, kicks, sources, moments, peak = call(
         open_kernel, "open", (), (positions, velocities, masses, long_kick),
-        (record_shape,) * 3 + (sources_shape, moments_shape),
+        (record_shape,) * 3 + (sources_shape, moments_shape, peak_shape),
     )
     for subcycle in range(SUBCYCLES):
         far = swapped(chosen, "gx", 1)
         near = swapped(chosen, "gx", 0)
         if subcycle:
             own, speeds = call(
-                early_kernel, "early", (lists, count), (own, speeds, kicks, sources, moments),
+                early_kernel, "early", (lists, count),
+                (own, speeds, kicks, peak, sources, moments),
                 (record_shape, record_shape), {0: 0, 1: 1}, LEAVES // 2,
             )
         middle = jnp.concatenate([near, chosen, far], axis=0)
@@ -334,29 +369,29 @@
         far = swapped(middle, "gy", 1)
         near = swapped(middle, "gy", 0)
         if subcycle:
-            own, speeds, sources, moments = call(
+            own, speeds, sources, moments, peak = call(
                 late_kernel, "late", (lists, parity, count),
-                (own, speeds, kicks, middle, sources, moments),
-                (record_shape, record_shape, sources_shape, moments_shape),
-                {0: 0, 1: 1, 4: 2, 5: 3}, LEAVES // 2,
+                (own, speeds, kicks, middle, peak, sources, moments),
+                (record_shape, record_shape, sources_shape, moments_shape, peak_shape),
+                {0: 0, 1: 1, 5: 2, 6: 3}, LEAVES // 2,
             )
         else:
-            sources, moments = call(
-                middle_kernel, "middle", (parity,), (middle, sources, moments),
-                (sources_shape, moments_shape), {1: 0, 2: 1}, 1,
+            sources, moments, peak = call(
+                middle_kernel, "middle", (parity,), (middle, peak, sources, moments),
+                (sources_shape, moments_shape, peak_shape), {2: 0, 3: 1}, 1,
             )
         if subcycle < SUBCYCLES - 1:
-            sources, moments, chosen = call(
+            sources, moments, chosen, peak = call(
                 ghost_kernel, "ghost", (lists, ids, parity),
-                (own, speeds, kicks, near, far, sources, moments),
-                (sources_shape, moments_shape, chosen_shape), {5: 0, 6: 1}, GHOSTS,
+                (own, speeds, kicks, near, far, peak, sources, moments),
+                (sources_shape, moments_shape, chosen_shape, peak_shape), {6: 0, 7: 1}, GHOSTS,
             )
         else:
             places, paces, _, _ = call(
                 last_kernel, "last", (lists, parity, count),
-                (own, speeds, kicks, near, far, sources, moments),
+                (own, speeds, kicks, near, far, peak, sources, moments),
                 (whole_shape, whole_shape, sources_shape, moments_shape),
-                {5: 2, 6: 3}, LEAVES,
+                {6: 2, 7: 3}, LEAVES,
             )
     return places, paces
 

time: 151 us -> 151 us (level); the launches traced: 153 us -> 150 us
  Pallas kernels: 73.2 us -> 58.6 us
  starting transfers between devices: 69 us -> 82.7 us
  waiting for transfers between devices: 2.73 us -> 0.56 us
    pallas_call x13, Pallas kernels: 73.2 us -> 58.6 us  [call(): pl.pallas_call(kernel, out_shape=outs, in_specs=[SMEM] * len(scalars) + [...]
    ppermute x16, starting transfers between devices: 69 us -> 82.7 us  [swapped(): return lax.ppermute(block, axis, route)]
    ppermute x16, waiting for transfers between devices: 2.73 us -> 0.56 us  [swapped(): return lax.ppermute(block, axis, route)]
  transfers between devices with their start and end apart: 16 -> 16, of which waited for: 2 -> 1; matrix products, arithmetic and copies ran while one was open for 0% -> 0% of each run, Pallas kernels for 32% -> 26%
where the time goes in v5:
time: 151 us; the launch traced here: 150 us
  starting transfers between devices  82.7 us (55%)
  Pallas kernels  58.6 us (39%)
  local copies, waits for them, and re-layouts  5.85 us (4%)
  between operations  1.72 us (1%)
    ppermute x16, starting transfers between devices, swapped(): return lax.ppermute(block, axis, route)  82.7 us
    pallas_call x13, Pallas kernels, call(): pl.pallas_call(kernel, out_shape=outs, in_specs=[SMEM] * len(scalars) + [...  58.6 us
    unnamed x24, local copies, waits for them, and re-layouts  5.83 us
  transfers between devices with their start and end apart: 16, of which 1 were waited for; matrix products, arithmetic and copies ran while one was open for 0% of the time, Pallas kernels for 26%

profile of v5, /device:TPU:2, one launch (start us, length us, event | category | flops | bytes accessed | tf_op | source)
XLA Modules:
  0.0 149.5 jit_solution(9316036617189322025)
XLA Ops:
  0.7 0.9 copy-done
  3.5 3.4 %collective-permute-start.1 = (f32[8,4,128]{2,1,0:T(4,128)S(1)}, f32[8,4,128]{2,1,0:T(4,128)S(1)}, u32[]{:S(2)}, u32[]{:S(2)}) collective-permute-start(f32[8,4,128]{2,1,0:T(4,128)S(1)} %choose.1), channel_id=1, source_target_pairs={{32,64},{64,32},{96,128},{128,96},{160,192},{192,160},{224,256},{2... | collective-permute-start | bytes 49160 | tf_op jit(solution)/shard_map/ppermute | solution.py:344
  6.9 14.0 %collective-permute-start = (f32[8,4,128]{2,1,0:T(4,128)S(1)}, f32[8,4,128]{2,1,0:T(4,128)S(1)}, u32[]{:S(2)}, u32[]{:S(2)}) collective-permute-start(f32[8,4,128]{2,1,0:T(4,128)S(1)} %choose.1), channel_id=1, source_target_pairs={{0,32},{32,0},{64,96},{96,64},{128,160},{160,128},{192,224},{224,1... | collective-permute-start | bytes 49160 | tf_op jit(solution)/shard_map/ppermute | solution.py:344
  20.9 0.9 copy-done.1
  21.8 0.9 copy-done.2
  22.7 0.9 copy-done.3
  24.4 1.3 open.1
  25.8 11.8 %collective-permute-start.3 = (f32[24,4,128]{2,1,0:T(4,128)S(1)}, f32[24,4,128]{2,1,0:T(4,128)S(1)}, u32[]{:S(2)}, u32[]{:S(2)}) collective-permute-start(f32[24,4,128]{2,1,0:T(4,128)S(1)} %pad_maximum_fusion.middle), channel_id=1, source_target_pairs={{1,2},{2,1},{3,4},{4,3},{5,6},{6,5},{7,8},{8,7},{9,10},{10,9},{11,... | collective-permute-start | bytes 147464 | tf_op jit(solution)/shard_map/ppermute | solution.py:344
  37.6 1.9 %collective-permute-start.2 = (f32[24,4,128]{2,1,0:T(4,128)S(1)}, f32[24,4,128]{2,1,0:T(4,128)S(1)}, u32[]{:S(2)}, u32[]{:S(2)}) collective-permute-start(f32[24,4,128]{2,1,0:T(4,128)S(1)} %pad_maximum_fusion.middle), channel_id=1, source_target_pairs={{0,1},{1,0},{2,3},{3,2},{4,5},{5,4},{6,7},{7,6},{8,9},{9,8},{10,11... | collective-permute-start | bytes 147464 | tf_op jit(solution)/shard_map/ppermute | solution.py:344
  40.3 0.9 middle.1
  41.2 2.9 %ghost.3 = (bf16[136,128,128]{2,1,0:T(8,128)(2,1)S(1)}, bf16[136,16,128]{2,1,0:T(8,128)(2,1)S(1)}, f32[8,4,128]{2,1,0:T(4,128)S(1)}, f32[1,128]{1,0:T(1,128)S(1)}) custom-call(s32[8,64]{1,0:T(8,128)S(1)} %copy-done.6, s32[8]{0:T(128)S(1)} %copy-done.8, s32[2]{0:T(128)S(1)} %and_select_fusion.parity, ...), custom_call_target="tpu_custom_call", output_to_operand_aliasing={{0}: (9, {}), {1}: (10, {})} | custom-call | flops 314572800 | bytes 1048576 | tf_op jit(solution)/shard_map/ghost/pallas_call | solution.py:325
  44.0 1.9 %collective-permute-start.5 = (f32[8,4,128]{2,1,0:T(4,128)S(1)}, f32[8,4,128]{2,1,0:T(4,128)S(1)}, u32[]{:S(2)}, u32[]{:S(2)}) collective-permute-start(f32[8,4,128]{2,1,0:T(4,128)S(1)} %get-tuple-element.64), channel_id=1, source_target_pairs={{32,64},{64,32},{96,128},{128,96},{160,192},{192,160},{224,256},{2... | collective-permute-start | bytes 49160 | tf_op jit(solution)/shard_map/ppermute | solution.py:344
  46.0 5.6 %collective-permute-start.4 = (f32[8,4,128]{2,1,0:T(4,128)S(1)}, f32[8,4,128]{2,1,0:T(4,128)S(1)}, u32[]{:S(2)}, u32[]{:S(2)}) collective-permute-start(f32[8,4,128]{2,1,0:T(4,128)S(1)} %get-tuple-element.64), channel_id=1, source_target_pairs={{0,32},{32,0},{64,96},{96,64},{128,160},{160,128},{192,224},{224,1... | collective-permute-start | bytes 49160 | tf_op jit(solution)/shard_map/ppermute | solution.py:344
  51.6 3.7 %early.3 = (f32[64,4,128]{2,1,0:T(4,128)S(1)}, f32[64,4,128]{2,1,0:T(4,128)S(1)}) custom-call(s32[8,64]{1,0:T(8,128)S(1)} %copy-done.6, s32[1]{0:T(128)S(6)} %copy.71.count, f32[64,4,128]{2,1,0:T(4,128)S(1)} %get-tuple-element.49.own, f32[64,4,128]{2,1,0:T(4,128)S(1)} %get-tuple-element.50.speeds, ...), custom_call_target="tpu_custom_call", output_to_operand_aliasing={{0}: (2, {}), {1}: (3, {})} | custom-call | flops 1258291200 | bytes 1048576 | tf_op jit(solution)/shard_map/early/pallas_call | solution.py:325
  55.3 6.6 %collective-permute-start.7 = (f32[24,4,128]{2,1,0:T(4,128)S(1)}, f32[24,4,128]{2,1,0:T(4,128)S(1)}, u32[]{:S(2)}, u32[]{:S(2)}) collective-permute-start(f32[24,4,128]{2,1,0:T(4,128)S(1)} %constant_dynamic-update-slice_fusion.middle), channel_id=1, source_target_pairs={{1,2},{2,1},{3,4},{4,3},{5,6},{6,5},{7,8},{8,7},{9,10},{10,9},{11,... | collective-permute-start | bytes 147464 | tf_op jit(solution)/shard_map/ppermute | solution.py:344
  62.0 1.9 %collective-permute-start.6 = (f32[24,4,128]{2,1,0:T(4,128)S(1)}, f32[24,4,128]{2,1,0:T(4,128)S(1)}, u32[]{:S(2)}, u32[]{:S(2)}) collective-permute-start(f32[24,4,128]{2,1,0:T(4,128)S(1)} %constant_dynamic-update-slice_fusion.middle), channel_id=1, source_target_pairs={{0,1},{1,0},{2,3},{3,2},{4,5},{5,4},{6,7},{7,6},{8,9},{9,8},{10,11... | collective-permute-start | bytes 147464 | tf_op jit(solution)/shard_map/ppermute | solution.py:344
  63.9 8.3 %late.3 = (f32[64,4,128]{2,1,0:T(4,128)S(1)}, f32[64,4,128]{2,1,0:T(4,128)S(1)}, bf16[136,128,128]{2,1,0:T(8,128)(2,1)S(1)}, bf16[136,16,128]{2,1,0:T(8,128)(2,1)S(1)}, f32[1,128]{1,0:T(1,128)S(1)}) custom-call(s32[8,64]{1,0:T(8,128)S(1)} %copy-done.6, ...), custom_call_target="tpu_custom_call", output_to_operand_aliasing={{0}: (3, {}), {1}: (4, {}), {2}: (8, {}), {3}: (9, {})} | custom-call | flops 1258291200 | bytes 1048576 | tf_op jit(solution)/shard_map/late/pallas_call | solution.py:325
  72.3 3.0 %ghost.4 = (bf16[136,128,128]{2,1,0:T(8,128)(2,1)S(1)}, bf16[136,16,128]{2,1,0:T(8,128)(2,1)S(1)}, f32[8,4,128]{2,1,0:T(4,128)S(1)}, f32[1,128]{1,0:T(1,128)S(1)}) custom-call(s32[8,64]{1,0:T(8,128)S(1)} %copy-done.6, s32[8]{0:T(128)S(1)} %copy-done.8, s32[2]{0:T(128)S(1)} %and_select_fusion.parity, ...), custom_call_target="tpu_custom_call", output_to_operand_aliasing={{0}: (9, {}), {1}: (10, {})} | custom-call | flops 314572800 | bytes 1048576 | tf_op jit(solution)/shard_map/ghost/pallas_call | solution.py:325
  75.3 1.9 %collective-permute-start.9 = (f32[8,4,128]{2,1,0:T(4,128)S(1)}, f32[8,4,128]{2,1,0:T(4,128)S(1)}, u32[]{:S(2)}, u32[]{:S(2)}) collective-permute-start(f32[8,4,128]{2,1,0:T(4,128)S(1)} %get-tuple-element.75), channel_id=1, source_target_pairs={{32,64},{64,32},{96,128},{128,96},{160,192},{192,160},{224,256},{2... | collective-permute-start | bytes 49160 | tf_op jit(solution)/shard_map/ppermute | solution.py:344
  77.2 9.1 %collective-permute-start.8 = (f32[8,4,128]{2,1,0:T(4,128)S(1)}, f32[8,4,128]{2,1,0:T(4,128)S(1)}, u32[]{:S(2)}, u32[]{:S(2)}) collective-permute-start(f32[8,4,128]{2,1,0:T(4,128)S(1)} %get-tuple-element.75), channel_id=1, source_target_pairs={{0,32},{32,0},{64,96},{96,64},{128,160},{160,128},{192,224},{224,1... | collective-permute-start | bytes 49160 | tf_op jit(solution)/shard_map/ppermute | solution.py:344
  86.4 3.7 %early.4 = (f32[64,4,128]{2,1,0:T(4,128)S(1)}, f32[64,4,128]{2,1,0:T(4,128)S(1)}) custom-call(s32[8,64]{1,0:T(8,128)S(1)} %copy-done.6, s32[1]{0:T(128)S(6)} %copy.71.count, f32[64,4,128]{2,1,0:T(4,128)S(1)} %get-tuple-element.65.own, f32[64,4,128]{2,1,0:T(4,128)S(1)} %get-tuple-element.66.speeds, ...), custom_call_target="tpu_custom_call", output_to_operand_aliasing={{0}: (2, {}), {1}: (3, {})} | custom-call | flops 1258291200 | bytes 1048576 | tf_op jit(solution)/shard_map/early/pallas_call | solution.py:325
  90.2 3.1 %collective-permute-start.11 = (f32[24,4,128]{2,1,0:T(4,128)S(1)}, f32[24,4,128]{2,1,0:T(4,128)S(1)}, u32[]{:S(2)}, u32[]{:S(2)}) collective-permute-start(f32[24,4,128]{2,1,0:T(4,128)S(1)} %constant_dynamic-update-slice_fusion.3.middle), channel_id=1, source_target_pairs={{1,2},{2,1},{3,4},{4,3},{5,6},{6,5},{7,8},{8,7},{9,10},{10,9},{11,... | collective-permute-start | bytes 147464 | tf_op jit(solution)/shard_map/ppermute | solution.py:344
  93.2 1.9 %collective-permute-start.10 = (f32[24,4,128]{2,1,0:T(4,128)S(1)}, f32[24,4,128]{2,1,0:T(4,128)S(1)}, u32[]{:S(2)}, u32[]{:S(2)}) collective-permute-start(f32[24,4,128]{2,1,0:T(4,128)S(1)} %constant_dynamic-update-slice_fusion.3.middle), channel_id=1, source_target_pairs={{0,1},{1,0},{2,3},{3,2},{4,5},{5,4},{6,7},{7,6},{8,9},{9,8},{10,11... | collective-permute-start | bytes 147464 | tf_op jit(solution)/shard_map/ppermute | solution.py:344
  95.2 8.3 %late.4 = (f32[64,4,128]{2,1,0:T(4,128)S(1)}, f32[64,4,128]{2,1,0:T(4,128)S(1)}, bf16[136,128,128]{2,1,0:T(8,128)(2,1)S(1)}, bf16[136,16,128]{2,1,0:T(8,128)(2,1)S(1)}, f32[1,128]{1,0:T(1,128)S(1)}) custom-call(s32[8,64]{1,0:T(8,128)S(1)} %copy-done.6, ...), custom_call_target="tpu_custom_call", output_to_operand_aliasing={{0}: (3, {}), {1}: (4, {}), {2}: (8, {}), {3}: (9, {})} | custom-call | flops 1258291200 | bytes 1048576 | tf_op jit(solution)/shard_map/late/pallas_call | solution.py:325
  104.0 2.8 %ghost.5 = (bf16[136,128,128]{2,1,0:T(8,128)(2,1)S(1)}, bf16[136,16,128]{2,1,0:T(8,128)(2,1)S(1)}, f32[8,4,128]{2,1,0:T(4,128)S(1)}, f32[1,128]{1,0:T(1,128)S(1)}) custom-call(s32[8,64]{1,0:T(8,128)S(1)} %copy-done.6, s32[8]{0:T(128)S(1)} %copy-done.8, s32[2]{0:T(128)S(1)} %and_select_fusion.parity, ...), custom_call_target="tpu_custom_call", output_to_operand_aliasing={{0}: (9, {}), {1}: (10, {})} | custom-call | flops 314572800 | bytes 1048576 | tf_op jit(solution)/shard_map/ghost/pallas_call | solution.py:325
  106.9 1.9 %collective-permute-start.13 = (f32[8,4,128]{2,1,0:T(4,128)S(1)}, f32[8,4,128]{2,1,0:T(4,128)S(1)}, u32[]{:S(2)}, u32[]{:S(2)}) collective-permute-start(f32[8,4,128]{2,1,0:T(4,128)S(1)} %get-tuple-element.86), channel_id=1, source_target_pairs={{32,64},{64,32},{96,128},{128,96},{160,192},{192,160},{224,256},{2... | collective-permute-start | bytes 49160 | tf_op jit(solution)/shard_map/ppermute | solution.py:344
  108.8 10.8 %collective-permute-start.12 = (f32[8,4,128]{2,1,0:T(4,128)S(1)}, f32[8,4,128]{2,1,0:T(4,128)S(1)}, u32[]{:S(2)}, u32[]{:S(2)}) collective-permute-start(f32[8,4,128]{2,1,0:T(4,128)S(1)} %get-tuple-element.86), channel_id=1, source_target_pairs={{0,32},{32,0},{64,96},{96,64},{128,160},{160,128},{192,224},{224,1... | collective-permute-start | bytes 49160 | tf_op jit(solution)/shard_map/ppermute | solution.py:344
  119.6 3.7 %early.5 = (f32[64,4,128]{2,1,0:T(4,128)S(1)}, f32[64,4,128]{2,1,0:T(4,128)S(1)}) custom-call(s32[8,64]{1,0:T(8,128)S(1)} %copy-done.6, s32[1]{0:T(128)S(6)} %copy.71.count, f32[64,4,128]{2,1,0:T(4,128)S(1)} %get-tuple-element.76.own, f32[64,4,128]{2,1,0:T(4,128)S(1)} %get-tuple-element.77.speeds, ...), custom_call_target="tpu_custom_call", output_to_operand_aliasing={{0}: (2, {}), {1}: (3, {})} | custom-call | flops 1258291200 | bytes 1048576 | tf_op jit(solution)/shard_map/early/pallas_call | solution.py:325
  123.4 4.8 %collective-permute-start.15 = (f32[24,4,128]{2,1,0:T(4,128)S(1)}, f32[24,4,128]{2,1,0:T(4,128)S(1)}, u32[]{:S(2)}, u32[]{:S(2)}) collective-permute-start(f32[24,4,128]{2,1,0:T(4,128)S(1)} %constant_dynamic-update-slice_fusion.6.middle), channel_id=1, source_target_pairs={{1,2},{2,1},{3,4},{4,3},{5,6},{6,5},{7,8},{8,7},{9,10},{10,9},{11,... | collective-permute-start | bytes 147464 | tf_op jit(solution)/shard_map/ppermute | solution.py:344
  128.2 1.9 %collective-permute-start.14 = (f32[24,4,128]{2,1,0:T(4,128)S(1)}, f32[24,4,128]{2,1,0:T(4,128)S(1)}, u32[]{:S(2)}, u32[]{:S(2)}) collective-permute-start(f32[24,4,128]{2,1,0:T(4,128)S(1)} %constant_dynamic-update-slice_fusion.6.middle), channel_id=1, source_target_pairs={{0,1},{1,0},{2,3},{3,2},{4,5},{5,4},{6,7},{7,6},{8,9},{9,8},{10,11... | collective-permute-start | bytes 147464 | tf_op jit(solution)/shard_map/ppermute | solution.py:344
  130.2 8.3 %late.5 = (f32[64,4,128]{2,1,0:T(4,128)S(1)}, f32[64,4,128]{2,1,0:T(4,128)S(1)}, bf16[136,128,128]{2,1,0:T(8,128)(2,1)S(1)}, bf16[136,16,128]{2,1,0:T(8,128)(2,1)S(1)}, f32[1,128]{1,0:T(1,128)S(1)}) custom-call(s32[8,64]{1,0:T(8,128)S(1)} %copy-done.6, ...), custom_call_target="tpu_custom_call", output_to_operand_aliasing={{0}: (3, {}), {1}: (4, {}), {2}: (8, {}), {3}: (9, {})} | custom-call | flops 1258291200 | bytes 1048576 | tf_op jit(solution)/shard_map/late/pallas_call | solution.py:325
  138.5 11.0 %last.1 = (f32[3,8192]{1,0:T(4,128)}, f32[3,8192]{1,0:T(4,128)}, bf16[136,128,128]{2,1,0:T(8,128)(2,1)S(1)}, bf16[136,16,128]{2,1,0:T(8,128)(2,1)S(1)}) custom-call(s32[8,64]{1,0:T(8,128)S(1)} %copy-done.6, s32[2]{0:T(128)S(1)} %and_select_fusion.parity, s32[1]{0:T(128)S(6)} %copy.71.count, ...), custom_call_target="tpu_custom_call", output_to_operand_aliasing={{2}: (9, {}), {3}: (10, {})} | custom-call | flops 2516582400 | bytes 1048576 | tf_op jit(solution)/shard_map/last/pallas_call | solution.py:325
  (42 shorter events, 3.5 us)
Async XLA Ops:
  0.6 40.5 %copy-start.8 = (s32[8]{0:T(128)S(1)}, s32[8]{0:T(128)}, u32[]{:S(2)}) copy-start(s32[8]{0:T(128)} %ids.7) | copy-start | bytes 100
  0.6 0.9 copy-start
  1.6 0.8 copy-start.4
  2.3 0.7 copy-start.7
  3.0 38.2 %copy-start.6 = (s32[8,64]{1,0:T(8,128)S(1)}, s32[8,64]{1,0:T(8,128)}, u32[]{:S(2)}) copy-start(s32[8,64]{1,0:T(8,128)} %lists.19) | copy-start | bytes 6148
  3.5 22.2 %collective-permute-start.1 = (f32[8,4,128]{2,1,0:T(4,128)S(1)}, f32[8,4,128]{2,1,0:T(4,128)S(1)}, u32[]{:S(2)}, u32[]{:S(2)}) collective-permute-start(f32[8,4,128]{2,1,0:T(4,128)S(1)} %choose.1), channel_id=1, source_target_pairs={{32,64},{64,32},{96,128},{128,96},{160,192},{192,160},{224,256},{2... | collective-permute-start | bytes 49160 | tf_op jit(solution)/shard_map/ppermute | solution.py:344
  6.9 18.8 %collective-permute-start = (f32[8,4,128]{2,1,0:T(4,128)S(1)}, f32[8,4,128]{2,1,0:T(4,128)S(1)}, u32[]{:S(2)}, u32[]{:S(2)}) collective-permute-start(f32[8,4,128]{2,1,0:T(4,128)S(1)} %choose.1), channel_id=1, source_target_pairs={{0,32},{32,0},{64,96},{96,64},{128,160},{160,128},{192,224},{224,1... | collective-permute-start | bytes 49160 | tf_op jit(solution)/shard_map/ppermute | solution.py:344
  20.9 0.9 copy-start.1
  21.8 0.9 copy-start.2
  22.7 0.9 copy-start.3
  23.6 0.8 copy-start.5
  25.8 15.4 %collective-permute-start.3 = (f32[24,4,128]{2,1,0:T(4,128)S(1)}, f32[24,4,128]{2,1,0:T(4,128)S(1)}, u32[]{:S(2)}, u32[]{:S(2)}) collective-permute-start(f32[24,4,128]{2,1,0:T(4,128)S(1)} %pad_maximum_fusion.middle), channel_id=1, source_target_pairs={{1,2},{2,1},{3,4},{4,3},{5,6},{6,5},{7,8},{8,7},{9,10},{10,9},{11,... | collective-permute-start | bytes 147464 | tf_op jit(solution)/shard_map/ppermute | solution.py:344
  37.6 3.5 %collective-permute-start.2 = (f32[24,4,128]{2,1,0:T(4,128)S(1)}, f32[24,4,128]{2,1,0:T(4,128)S(1)}, u32[]{:S(2)}, u32[]{:S(2)}) collective-permute-start(f32[24,4,128]{2,1,0:T(4,128)S(1)} %pad_maximum_fusion.middle), channel_id=1, source_target_pairs={{0,1},{1,0},{2,3},{3,2},{4,5},{5,4},{6,7},{7,6},{8,9},{9,8},{10,11... | collective-permute-start | bytes 147464 | tf_op jit(solution)/shard_map/ppermute | solution.py:344
  44.0 11.3 %collective-permute-start.5 = (f32[8,4,128]{2,1,0:T(4,128)S(1)}, f32[8,4,128]{2,1,0:T(4,128)S(1)}, u32[]{:S(2)}, u32[]{:S(2)}) collective-permute-start(f32[8,4,128]{2,1,0:T(4,128)S(1)} %get-tuple-element.64), channel_id=1, source_target_pairs={{32,64},{64,32},{96,128},{128,96},{160,192},{192,160},{224,256},{2... | collective-permute-start | bytes 49160 | tf_op jit(solution)/shard_map/ppermute | solution.py:344
  46.0 9.3 %collective-permute-start.4 = (f32[8,4,128]{2,1,0:T(4,128)S(1)}, f32[8,4,128]{2,1,0:T(4,128)S(1)}, u32[]{:S(2)}, u32[]{:S(2)}) collective-permute-start(f32[8,4,128]{2,1,0:T(4,128)S(1)} %get-tuple-element.64), channel_id=1, source_target_pairs={{0,32},{32,0},{64,96},{96,64},{128,160},{160,128},{192,224},{224,1... | collective-permute-start | bytes 49160 | tf_op jit(solution)/shard_map/ppermute | solution.py:344
  55.3 16.9 %collective-permute-start.7 = (f32[24,4,128]{2,1,0:T(4,128)S(1)}, f32[24,4,128]{2,1,0:T(4,128)S(1)}, u32[]{:S(2)}, u32[]{:S(2)}) collective-permute-start(f32[24,4,128]{2,1,0:T(4,128)S(1)} %constant_dynamic-update-slice_fusion.middle), channel_id=1, source_target_pairs={{1,2},{2,1},{3,4},{4,3},{5,6},{6,5},{7,8},{8,7},{9,10},{10,9},{11,... | collective-permute-start | bytes 147464 | tf_op jit(solution)/shard_map/ppermute | solution.py:344
  62.0 10.3 %collective-permute-start.6 = (f32[24,4,128]{2,1,0:T(4,128)S(1)}, f32[24,4,128]{2,1,0:T(4,128)S(1)}, u32[]{:S(2)}, u32[]{:S(2)}) collective-permute-start(f32[24,4,128]{2,1,0:T(4,128)S(1)} %constant_dynamic-update-slice_fusion.middle), channel_id=1, source_target_pairs={{0,1},{1,0},{2,3},{3,2},{4,5},{5,4},{6,7},{7,6},{8,9},{9,8},{10,11... | collective-permute-start | bytes 147464 | tf_op jit(solution)/shard_map/ppermute | solution.py:344
  75.3 14.8 %collective-permute-start.9 = (f32[8,4,128]{2,1,0:T(4,128)S(1)}, f32[8,4,128]{2,1,0:T(4,128)S(1)}, u32[]{:S(2)}, u32[]{:S(2)}) collective-permute-start(f32[8,4,128]{2,1,0:T(4,128)S(1)} %get-tuple-element.75), channel_id=1, source_target_pairs={{32,64},{64,32},{96,128},{128,96},{160,192},{192,160},{224,256},{2... | collective-permute-start | bytes 49160 | tf_op jit(solution)/shard_map/ppermute | solution.py:344
  77.2 12.9 %collective-permute-start.8 = (f32[8,4,128]{2,1,0:T(4,128)S(1)}, f32[8,4,128]{2,1,0:T(4,128)S(1)}, u32[]{:S(2)}, u32[]{:S(2)}) collective-permute-start(f32[8,4,128]{2,1,0:T(4,128)S(1)} %get-tuple-element.75), channel_id=1, source_target_pairs={{0,32},{32,0},{64,96},{96,64},{128,160},{160,128},{192,224},{224,1... | collective-permute-start | bytes 49160 | tf_op jit(solution)/shard_map/ppermute | solution.py:344
  90.2 13.8 %collective-permute-start.11 = (f32[24,4,128]{2,1,0:T(4,128)S(1)}, f32[24,4,128]{2,1,0:T(4,128)S(1)}, u32[]{:S(2)}, u32[]{:S(2)}) collective-permute-start(f32[24,4,128]{2,1,0:T(4,128)S(1)} %constant_dynamic-update-slice_fusion.3.middle), channel_id=1, source_target_pairs={{1,2},{2,1},{3,4},{4,3},{5,6},{6,5},{7,8},{8,7},{9,10},{10,9},{11,... | collective-permute-start | bytes 147464 | tf_op jit(solution)/shard_map/ppermute | solution.py:344
  93.2 10.8 %collective-permute-start.10 = (f32[24,4,128]{2,1,0:T(4,128)S(1)}, f32[24,4,128]{2,1,0:T(4,128)S(1)}, u32[]{:S(2)}, u32[]{:S(2)}) collective-permute-start(f32[24,4,128]{2,1,0:T(4,128)S(1)} %constant_dynamic-update-slice_fusion.3.middle), channel_id=1, source_target_pairs={{0,1},{1,0},{2,3},{3,2},{4,5},{5,4},{6,7},{7,6},{8,9},{9,8},{10,11... | collective-permute-start | bytes 147464 | tf_op jit(solution)/shard_map/ppermute | solution.py:344
  106.9 16.5 %collective-permute-start.13 = (f32[8,4,128]{2,1,0:T(4,128)S(1)}, f32[8,4,128]{2,1,0:T(4,128)S(1)}, u32[]{:S(2)}, u32[]{:S(2)}) collective-permute-start(f32[8,4,128]{2,1,0:T(4,128)S(1)} %get-tuple-element.86), channel_id=1, source_target_pairs={{32,64},{64,32},{96,128},{128,96},{160,192},{192,160},{224,256},{2... | collective-permute-start | bytes 49160 | tf_op jit(solution)/shard_map/ppermute | solution.py:344
  108.8 14.5 %collective-permute-start.12 = (f32[8,4,128]{2,1,0:T(4,128)S(1)}, f32[8,4,128]{2,1,0:T(4,128)S(1)}, u32[]{:S(2)}, u32[]{:S(2)}) collective-permute-start(f32[8,4,128]{2,1,0:T(4,128)S(1)} %get-tuple-element.86), channel_id=1, source_target_pairs={{0,32},{32,0},{64,96},{96,64},{128,160},{160,128},{192,224},{224,1... | collective-permute-start | bytes 49160 | tf_op jit(solution)/shard_map/ppermute | solution.py:344
  123.4 15.1 %collective-permute-start.15 = (f32[24,4,128]{2,1,0:T(4,128)S(1)}, f32[24,4,128]{2,1,0:T(4,128)S(1)}, u32[]{:S(2)}, u32[]{:S(2)}) collective-permute-start(f32[24,4,128]{2,1,0:T(4,128)S(1)} %constant_dynamic-update-slice_fusion.6.middle), channel_id=1, source_target_pairs={{1,2},{2,1},{3,4},{4,3},{5,6},{6,5},{7,8},{8,7},{9,10},{10,9},{11,... | collective-permute-start | bytes 147464 | tf_op jit(solution)/shard_map/ppermute | solution.py:344
  128.2 10.3 %collective-permute-start.14 = (f32[24,4,128]{2,1,0:T(4,128)S(1)}, f32[24,4,128]{2,1,0:T(4,128)S(1)}, u32[]{:S(2)}, u32[]{:S(2)}) collective-permute-start(f32[24,4,128]{2,1,0:T(4,128)S(1)} %constant_dynamic-update-slice_fusion.6.middle), channel_id=1, source_target_pairs={{0,1},{1,0},{2,3},{3,2},{4,5},{5,4},{6,7},{7,6},{8,9},{9,8},{10,11... | collective-permute-start | bytes 147464 | tf_op jit(solution)/shard_map/ppermute | solution.py:344
